TPU v7x, 32 devices: a whole 2x2x4 slice. The times are simulated.
32 devices in a mesh: fsdp: 8 (over z, core), frame: 4 (over y, x).
Axes of the slice: x: 2, y: 2, z: 4, core: 2. Of those that a mesh axis runs over, the one named last changes fastest.
Arguments:
- frames: bfloat16 [8, 1536, 3072], P('fsdp', 'frame'), may hold values from -6 to 6
- modulation: float32 [8, 2, 3072], P('fsdp'), may hold values from -3 to 3
- w_qkv: bfloat16 [3072, 768], P('fsdp'), may hold values from -0.109375 to 0.109375
- qk_gain: float32 [2, 128], replicated, may hold values from 0.1 to 1.9
- w_out: bfloat16 [256, 3072], P(None, 'fsdp'), may hold values from -0.375 to 0.375
Outputs:
- mixed: bfloat16 [8, 1536, 3072], P('fsdp', 'frame')
All inputs are finite; a program needn't handle non-finite values.
Results may differ from a plain program's by a relative error of at most 0.0053.
Values may be sent and summed in bfloat16 or wider, within the bound.
No kernel may reach another device: no remote copies, remote signals or barrier semaphores. Data moves between devices by JAX's collectives and lax.ppermute only.
A program may use at most 64 MiB of HBM per device.

v0:
```python
import math

import jax
import jax.numpy as jnp
from jax import lax
from jax.sharding import PartitionSpec as P

HEAD_DIM = 128
HEADS = 2
TILE = 128
REACH = 2
BORDER = 256
WINDOW = 640


def with_halo(cells, sides, width):
    for axis, dim in sides:
        count = lax.axis_size(axis)
        ends = count - 1
        head = lax.slice_in_dim(cells, 0, width, axis=dim)
        tail = lax.slice_in_dim(cells, cells.shape[dim] - width, cells.shape[dim], axis=dim)
        cells = jnp.concatenate(
            [
                lax.ppermute(tail, axis, [(i, (i + 1) % count) for i in range(ends)]),
                cells,
                lax.ppermute(head, axis, [((i + 1) % count, i) for i in range(ends)]),
            ],
            axis=dim,
        )
    return cells


def norm_rows(frames_rows, modulation_rows):
    values_full = frames_rows.astype(jnp.float32)
    average = jnp.mean(values_full, axis=-1, keepdims=True)
    centered = values_full - average
    spread = jnp.mean(centered * centered, axis=-1, keepdims=True)
    normed = centered * lax.rsqrt(spread + 1e-06)
    return (normed * (1.0 + modulation_rows[0]) + modulation_rows[1]).astype(jnp.bfloat16)


def head_norm(projected, gain_row):
    count = projected.shape[0]
    shaped = projected.reshape(count, HEADS, HEAD_DIM)
    squares = jnp.mean(shaped * shaped, axis=-1, keepdims=True)
    scaled = shaped * lax.rsqrt(squares + 1e-06) * gain_row
    return scaled.reshape(count, HEADS * HEAD_DIM).astype(jnp.bfloat16)


def send_borders(key_part, value_part):
    stacked = jnp.concatenate([key_part, value_part], axis=1)
    return with_halo(stacked, (("frame", 0),), BORDER)


def make_folder(normed):

    def fold_rows(carry, block_rows, first_row):
        return jnp.dot(normed, block_rows, preferred_element_type=jnp.float32)

    return fold_rows


def on_device(frames, modulation, w_qkv, qk_gain, w_out):
    normed = norm_rows(frames[0], modulation[0])
    rows_here = normed.shape[0]
    width = HEADS * HEAD_DIM
    scale_factor = 1.0 / math.sqrt(HEAD_DIM)
    proj_width = w_qkv.shape[1]
    zeros_init = jnp.zeros((rows_here, proj_width), jnp.float32)
    folder = make_folder(normed)
    operand, folder, start_carry = (w_qkv, folder, zeros_init)
    projected = folder(
        start_carry, lax.all_gather(operand, "fsdp", axis=0, tiled=True), jnp.int32(0)
    )
    queries = head_norm(projected[:, :width], qk_gain[0])
    key_part = head_norm(projected[:, width : 2 * width], qk_gain[1])
    value_part = projected[:, 2 * width :].astype(jnp.bfloat16)
    padded = send_borders(key_part, value_part)
    tiles_here = rows_here // TILE
    video_tokens = rows_here * lax.axis_size("frame")
    tile_ids = jnp.arange(tiles_here, dtype=jnp.int32)
    first_tile = tile_ids - REACH
    pieces = []
    for offset in range(2 * REACH + 1):
        pieces.append(
            padded[offset * TILE : offset * TILE + rows_here].reshape(tiles_here, TILE, 2 * width)
        )
    windows = jnp.concatenate(pieces, axis=1)
    positions = (
        lax.axis_index("frame") * rows_here
        + first_tile[:, None] * TILE
        + jnp.arange(WINDOW, dtype=jnp.int32)[None, :]
    )
    inside = (positions >= 0) & (positions < video_tokens)
    key_win = windows[:, :, :width].reshape(tiles_here, WINDOW, HEADS, HEAD_DIM)
    value_win = windows[:, :, width:].reshape(tiles_here, WINDOW, HEADS, HEAD_DIM)
    query_tiles = queries.reshape(tiles_here, TILE, HEADS, HEAD_DIM)
    scores = (
        jnp.einsum("tqhd,tkhd->thqk", query_tiles, key_win, preferred_element_type=jnp.float32)
        * scale_factor
    )
    raised = jnp.where(inside[:, None, None, :], jnp.exp(scores), 0.0)
    probs = (raised / jnp.sum(raised, axis=-1, keepdims=True)).astype(jnp.bfloat16)
    attended = jnp.einsum("thqk,tkhd->tqhd", probs, value_win, preferred_element_type=jnp.float32)
    attended = attended.astype(jnp.bfloat16).reshape(rows_here, width)
    mixed = jnp.dot(
        attended,
        lax.all_gather(w_out, "fsdp", axis=1, tiled=True),
        preferred_element_type=jnp.float32,
    ).astype(jnp.bfloat16)
    return mixed[None]


def solution(mesh):
    return jax.shard_map(
        on_device,
        mesh=mesh,
        in_specs=(
            P("fsdp", "frame", None),
            P("fsdp", None, None),
            P("fsdp", None),
            P(),
            P(None, "fsdp"),
        ),
        out_specs=P("fsdp", "frame", None),
        check_vma=False,
    )
```

profile of v0, /device:TPU:0, one launch (start us, length us, event | category | flops | bytes accessed | tf_op | source)
XLA Modules:
  0.0 101.6 jit_solution(15423785712750466453)
XLA Ops:
  6.5 0.7 all-gather.3.cloned.1.call-update
  7.3 0.7 all-gather.5.cloned.1.call-update
  8.0 1.4 %slice_add_fusion = (f32[1,1,3072]{2,1,0:T(1,128)S(1)}, f32[1,1,3072]{2,1,0:T(1,128)}) fusion(f32[1,2,3072]{2,1,0:T(2,128)} %param.6), kind=kLoop, calls=%fused_computation.46 | loop fusion | flops 3072 | bytes 49152 | tf_op jit(solution)/shard_map/add | solution.py:39
  9.5 2.1 %convert_reduce_fusion = f32[384]{0:T(512)S(1)} fusion(bf16[1,384,3072]{2,1,0:T(8,128)(2,1)} %param.5), kind=kLoop, calls=%fused_computation | loop fusion | flops 2358912 | bytes 2360832 | tf_op jit(solution)/shard_map/reduce_sum | solution.py:35
  11.5 0.8 fusion.3
  12.3 0.6 add_rsqrt_fusion.2
  12.9 0.6 multiply_add_fusion
  13.5 0.6 broadcast_bitcast_fusion
  14.1 49.4 %all-gather.3.cloned.1.call-done = bf16[3072,768]{1,0:T(8,128)(2,1)} async-done(((bf16[384,768]{1,0:T(8,128)(2,1)}), bf16[3072,768]{1,0:T(8,128)(2,1)}) %all-gather.3.cloned.1.call-update) | async-done | bytes 4718608 | tf_op jit(solution)/shard_map/all_gather | solution.py:73
  63.4 4.6 %fusion.8 = f32[384,768]{1,0:T(8,128)S(1)} fusion(bf16[3072,768]{1,0:T(8,128)(2,1)} %all-gather.3.cloned.1.call-done, bf16[1,384,3072]{2,1,0:T(8,128)(2,1)S(1)} %copy-done, f32[3072]{0:T(1024)} %bitcast.72, f32[3072]{0:T(1024)S(1)} %bitcast.71, f32[384]{0:T(512)} %add_rsqrt_fusion.2, f32[384]{0:T(512)S(1)} %broadcast_multiply_fusion), kind=kOutput, calls=%fused_computation.11 | convolution fusion | flops 1819017216 | bytes 8285184 | tf_op jit(solution)/shard_map/dot_general | solution.py:58
  68.4 0.5 reduce_sum.47
  69.1 0.5 reduce_sum.48
  69.7 0.5 mul.107
  70.1 0.5 mul.119
  70.8 3.4 %collective-permute-start = (bf16[256,512]{1,0:T(8,128)(2,1)S(1)}, bf16[256,512]{1,0:T(8,128)(2,1)S(1)}, u32[]{:S(2)}, u32[]{:S(2)}) collective-permute-start(bf16[256,512]{1,0:T(8,128)(2,1)S(1)} %get-tuple-element.18), channel_id=1, source_target_pairs={{0,1},{1,2},{2,3},{4,5},{5,6},{6,7},{8,9},{9,10},{10,11},{12,13},{... | collective-permute-start | bytes 786440 | tf_op jit(solution)/shard_map/ppermute | solution.py:24
  74.2 1.3 %collective-permute-start.1 = (bf16[256,512]{1,0:T(8,128)(2,1)S(1)}, bf16[256,512]{1,0:T(8,128)(2,1)S(1)}, u32[]{:S(2)}, u32[]{:S(2)}) collective-permute-start(bf16[256,512]{1,0:T(8,128)(2,1)S(1)} %get-tuple-element.17), channel_id=1, source_target_pairs={{1,0},{2,1},{3,2},{5,4},{6,5},{7,6},{9,8},{10,9},{11,10},{13,12},{... | collective-permute-start | bytes 786440 | tf_op jit(solution)/shard_map/ppermute | solution.py:26
  75.7 0.2 copy.30
  76.0 4.2 %collective-permute-done = bf16[256,512]{1,0:T(8,128)(2,1)S(1)} collective-permute-done((bf16[256,512]{1,0:T(8,128)(2,1)S(1)}, bf16[256,512]{1,0:T(8,128)(2,1)S(1)}, u32[]{:S(2)}, u32[]{:S(2)}) %collective-permute-start) | collective-permute-done | bytes 262176 | tf_op jit(solution)/shard_map/ppermute | solution.py:24
  80.2 7.5 %collective-permute-done.1 = bf16[256,512]{1,0:T(8,128)(2,1)S(1)} collective-permute-done((bf16[256,512]{1,0:T(8,128)(2,1)S(1)}, bf16[256,512]{1,0:T(8,128)(2,1)S(1)}, u32[]{:S(2)}, u32[]{:S(2)}) %collective-permute-start.1) | collective-permute-done | bytes 262176 | tf_op jit(solution)/shard_map/ppermute | solution.py:26
  88.1 0.2 copy.29
  88.7 0.2 copy.32
  89.6 0.7 fusion.14
  90.3 0.7 fusion.15
  91.1 3.6 %fusion.7 = bf16[1,384,3072]{2,1,0:T(8,128)(2,1)} fusion(bf16[256,3072]{1,0:T(8,128)(2,1)} %all-gather.5.cloned.1.call-done, bf16[48,8,2,128]{3,2,1,0:T(2,128)(2,1)S(1)} %bitcast.69), kind=kOutput, calls=%fused_computation.10 | convolution fusion | flops 605159424 | bytes 4128768 | tf_op jit(solution)/shard_map/dot_general | solution.py:106
  (38 shorter events, 2.5 us)
Async XLA Ops:
  6.5 5.0 %copy-start = (bf16[1,384,3072]{2,1,0:T(8,128)(2,1)S(1)}, bf16[1,384,3072]{2,1,0:T(8,128)(2,1)}, u32[]{:S(2)}) copy-start(bf16[1,384,3072]{2,1,0:T(8,128)(2,1)} %param.5) | copy-start | bytes 7077892
  6.5 56.9 %all-gather.3.cloned.1.call-start = ((), (), s32[]{:S(2)}) async-start(), calls=%async_computation | async-start | bytes 5308416 | tf_op jit(solution)/shard_map/all_gather | solution.py:73
  7.3 83.9 %all-gather.5.cloned.1.call-start = ((), (), s32[]{:S(2)}) async-start(), calls=%async_computation.1 | async-start | bytes 1769472 | tf_op jit(solution)/shard_map/all_gather | solution.py:108
  9.4 3.4 %copy-start.3 = (f32[2,128]{1,0:T(2,128)S(1)}, f32[2,128]{1,0:T(2,128)}, u32[]{:S(2)}) copy-start(f32[2,128]{1,0:T(2,128)} %param.8) | copy-start | bytes 3076
  68.4 2.2 %copy-start.1 = (f32[256]{0:T(256)S(1)}, f32[256]{0:T(256)}, u32[]{:S(2)}) copy-start(f32[256]{0:T(256)} %get-tuple-element.25) | copy-start | bytes 3076
  68.4 2.2 %copy-start.2 = (f32[256]{0:T(256)S(1)}, f32[256]{0:T(256)}, u32[]{:S(2)}) copy-start(f32[256]{0:T(256)} %get-tuple-element.26) | copy-start | bytes 3076
  69.6 5.9 %copy-start.4 = (s32[3]{0:T(128)S(1)}, s32[3]{0:T(128)}, u32[]{:S(2)}) copy-start(s32[3]{0:T(128)} %multiply_add_fusion) | copy-start | bytes 40
  70.8 9.3 %collective-permute-start = (bf16[256,512]{1,0:T(8,128)(2,1)S(1)}, bf16[256,512]{1,0:T(8,128)(2,1)S(1)}, u32[]{:S(2)}, u32[]{:S(2)}) collective-permute-start(bf16[256,512]{1,0:T(8,128)(2,1)S(1)} %get-tuple-element.18), channel_id=1, source_target_pairs={{0,1},{1,2},{2,3},{4,5},{5,6},{6,7},{8,9},{9,10},{10,11},{12,13},{... | collective-permute-start | bytes 786440 | tf_op jit(solution)/shard_map/ppermute | solution.py:24
  74.2 13.5 %collective-permute-start.1 = (bf16[256,512]{1,0:T(8,128)(2,1)S(1)}, bf16[256,512]{1,0:T(8,128)(2,1)S(1)}, u32[]{:S(2)}, u32[]{:S(2)}) collective-permute-start(bf16[256,512]{1,0:T(8,128)(2,1)S(1)} %get-tuple-element.17), channel_id=1, source_target_pairs={{1,0},{2,1},{3,2},{5,4},{6,5},{7,6},{9,8},{10,9},{11,10},{13,12},{... | collective-permute-start | bytes 786440 | tf_op jit(solution)/shard_map/ppermute | solution.py:26
Sparse Core Ops, SparseCore 0:
  9.0 54.3 all-gather.2
  65.1 24.0 all-gather.4
where the time goes:
time: 102 us
  waiting for transfers between devices  62.6 us (61%)
  between operations  13.7 us (13%)
  matrix products  9.54 us (9%)
  other arithmetic  6.94 us (7%)
  starting transfers between devices  4.72 us (5%)
  local copies, waits for them, and re-layouts  4.14 us (4%)
    all_gather x1, waiting for transfers between devices, on_device(): lax.all_gather(operand, 'fsdp', axis=0, tiled=True)  49.4 us
    ppermute x1, waiting for transfers between devices, with_halo(): lax.ppermute(head, axis, [((i + 1) % count, i) for i in range(ends)])  7.54 us
    dot_general x1, matrix products, fold_rows(): return jnp.dot(normed, block_rows, preferred_element_type=jnp.float32)  4.61 us
    ppermute x1, waiting for transfers between devices, with_halo(): lax.ppermute(tail, axis, [(i, (i + 1) % count) for i in range(ends)])  4.22 us
    dot_general x1, matrix products, on_device(): jnp.dot(attended, lax.all_gather(w_out, 'fsdp', axis=1, tiled=True), pref...  3.6 us
    ppermute x1, starting transfers between devices, with_halo(): lax.ppermute(tail, axis, [(i, (i + 1) % count) for i in range(ends)])  3.39 us
    reduce_sum x1, other arithmetic, norm_rows(): average = jnp.mean(values_full, axis=-1, keepdims=True)  2.07 us
  transfers between devices with their start and end apart: 4, of which 3 were waited for; matrix products, arithmetic and copies ran while one was open for 17% of the time, Pallas kernels for 0%

commit v1 on v0

v1 whole, which is shorter than its diff:
```python
import functools
import math

import jax
import jax.numpy as jnp
from jax import lax
from jax.experimental import pallas as pl
from jax.experimental.pallas import tpu as pltpu
from jax.sharding import PartitionSpec as P

HEAD_DIM = 128
HEADS = 2
WIDTH = HEADS * HEAD_DIM
TILE = 128
REACH = 2
BORDER = REACH * TILE
VMEM_BYTES = 40 * 1024 * 1024

f32 = jnp.float32
bf16 = jnp.bfloat16
ANY = pl.BlockSpec(memory_space=pl.ANY)
VMEM = pl.BlockSpec(memory_space=pltpu.VMEM)


def params():
    return pltpu.CompilerParams(vmem_limit_bytes=VMEM_BYTES)


def dot(a, b):
    return jnp.dot(a, b, preferred_element_type=f32)


def dot_t(a, b):
    return lax.dot_general(a, b, (((1,), (1,)), ((), ())), preferred_element_type=f32)


def norm_kernel(frames_ref, modulation_ref, normed_ref):
    values = frames_ref[...].astype(f32)
    average = jnp.mean(values, axis=-1, keepdims=True)
    centered = values - average
    spread = jnp.mean(centered * centered, axis=-1, keepdims=True)
    normed = centered * lax.rsqrt(spread + 1e-06)
    normed_ref[...] = (normed * (1.0 + modulation_ref[0:1]) + modulation_ref[1:2]).astype(bf16)


def norm_rows(frames, modulation):
    rows, width = frames.shape
    block = TILE // 2
    return pl.pallas_call(
        norm_kernel,
        grid=(rows // block,),
        in_specs=[
            pl.BlockSpec((block, width), lambda i: (i, 0)),
            pl.BlockSpec((2, width), lambda i: (0, 0)),
        ],
        out_specs=pl.BlockSpec((block, width), lambda i: (i, 0)),
        out_shape=jax.ShapeDtypeStruct((rows, width), bf16),
        compiler_params=params(),
        cost_estimate=pl.CostEstimate(
            flops=10 * rows * width, bytes_accessed=4 * rows * width, transcendentals=rows
        ),
        name="layer_norm",
    )(frames, modulation)


def head_norm(projected, gain_row):
    parts = []
    for head in range(HEADS):
        x = projected[:, head * HEAD_DIM : (head + 1) * HEAD_DIM]
        squares = jnp.mean(x * x, axis=-1, keepdims=True)
        parts.append((x * lax.rsqrt(squares + 1e-06) * gain_row).astype(bf16))
    return parts


def project_kernel(plan, depth, normed_ref, gain_ref, *refs):
    count = len(plan.sources)
    sources = refs[:count]
    queries_ref, stacked_ref, weights, sems = refs[count:]
    copies = []
    groups = plan.groups()
    for first, pieces in groups:
        started = []
        for source, begin, rows, target in pieces:
            copy = pltpu.make_async_copy(
                sources[source].at[pl.ds(begin, rows)],
                weights.at[pl.ds(target, rows)],
                sems.at[sum(len(c) for c in copies) + len(started)],
            )
            copy.start()
            started.append(copy)
        copies.append(started)
    total = None
    for slot, (first, pieces) in enumerate(groups):
        for copy in copies[slot]:
            copy.wait()
        part = dot(
            normed_ref[:, pl.ds(first, depth)], weights[slot * depth : (slot + 1) * depth, :]
        )
        total = part if total is None else total + part
    for head, value in enumerate(head_norm(total[:, :WIDTH], gain_ref[0:1])):
        queries_ref[:, head * HEAD_DIM : (head + 1) * HEAD_DIM] = value
    for head, value in enumerate(head_norm(total[:, WIDTH : 2 * WIDTH], gain_ref[1:2])):
        stacked_ref[:, head * HEAD_DIM : (head + 1) * HEAD_DIM] = value
    stacked_ref[:, WIDTH:] = total[:, 2 * WIDTH :].astype(bf16)


def project(plan, normed, qk_gain):
    rows, width = normed.shape
    columns = plan.sources[0].shape[1]
    groups = len(plan.groups())
    pieces = sum(len(p) for _, p in plan.groups())
    return pl.pallas_call(
        functools.partial(project_kernel, plan, width // groups),
        in_specs=[VMEM, VMEM] + [ANY] * len(plan.sources),
        out_specs=[VMEM, VMEM],
        out_shape=[
            jax.ShapeDtypeStruct((rows, WIDTH), bf16),
            jax.ShapeDtypeStruct((rows, 2 * WIDTH), bf16),
        ],
        scratch_shapes=[
            pltpu.VMEM((width, columns), bf16),
            pltpu.SemaphoreType.DMA((pieces,)),
        ],
        compiler_params=params(),
        cost_estimate=pl.CostEstimate(
            flops=2 * rows * width * columns,
            bytes_accessed=2 * (rows * width + width * columns),
            transcendentals=rows,
        ),
        name="project",
    )(normed, qk_gain, *plan.sources)


def attend_kernel(
    out_plan, queries_ref, stacked_ref, before_ref, after_ref, *refs
):
    count = len(out_plan.sources)
    sources = refs[:count]
    mixed_ref, attended, blocks, sems = refs[count:]
    rows = queries_ref.shape[0]
    tiles = rows // TILE
    scale = 1.0 / math.sqrt(HEAD_DIM)
    place = lax.axis_index("frame")
    has_before = (place > 0).astype(f32)
    has_after = (place < lax.axis_size("frame") - 1).astype(f32)
    for head in range(HEADS):
        ks = slice(head * HEAD_DIM, (head + 1) * HEAD_DIM)
        vs = slice(WIDTH + head * HEAD_DIM, WIDTH + (head + 1) * HEAD_DIM)
        for tile in range(tiles):
            query = queries_ref[tile * TILE : (tile + 1) * TILE, ks]
            low, high = tile - REACH, tile + REACH + 1
            weighted = jnp.zeros((TILE, HEAD_DIM), f32)
            mass = jnp.zeros((TILE, 1), f32)
            spans = [(stacked_ref, max(low, 0), min(high, tiles), None)]
            if low < 0:
                spans.append((before_ref, low + REACH, REACH, has_before))
            if high > tiles:
                spans.append((after_ref, 0, high - tiles, has_after))
            for ref, begin, end, flag in spans:
                span = slice(begin * TILE, end * TILE)
                raised = jnp.exp(dot_t(query, ref[span, ks]) * scale)
                if flag is not None:
                    raised = raised * flag
                mass = mass + jnp.sum(raised, axis=-1, keepdims=True)
                weighted = weighted + dot(raised.astype(bf16), ref[span, vs])
            attended[tile * TILE : (tile + 1) * TILE, ks] = (weighted / mass).astype(bf16)
    width = blocks.shape[2]
    copies = []
    for source, begin, target in out_plan.blocks(width):
        number = len(copies)
        blocks[number] = dot(
            attended[...], sources[source][:, begin : begin + width]
        ).astype(bf16)
        copy = pltpu.make_async_copy(
            blocks.at[number],
            mixed_ref.at[0, :, pl.ds(pl.multiple_of(target, TILE), width)],
            sems.at[number],
        )
        copy.start()
        copies.append(copy)
    for copy in copies:
        copy.wait()


def attend(out_plan, queries, stacked, before, after, model, width):
    rows = queries.shape[0]
    return pl.pallas_call(
        functools.partial(attend_kernel, out_plan),
        in_specs=[VMEM] * (4 + len(out_plan.sources)),
        out_specs=ANY,
        out_shape=jax.ShapeDtypeStruct((1, rows, model), bf16),
        scratch_shapes=[
            pltpu.VMEM((rows, WIDTH), bf16),
            pltpu.VMEM((model // width, rows, width), bf16),
            pltpu.SemaphoreType.DMA((model // width,)),
        ],
        compiler_params=params(),
        cost_estimate=pl.CostEstimate(
            flops=2 * rows * WIDTH * (model + 2 * 5 * TILE),
            bytes_accessed=2 * (rows * model + WIDTH * model),
            transcendentals=rows * HEADS * 5 * TILE,
        ),
        name="attend_and_mix",
    )(queries, stacked, before, after, *out_plan.sources)


class WholeRows:
    def __init__(self, shard):
        self.sources = [lax.all_gather(shard, "fsdp", axis=0, tiled=True)]

    def groups(self):
        rows = self.sources[0].shape[0]
        return [(0, [(0, 0, rows, 0)])]


class WholeColumns:
    def __init__(self, shard):
        self.sources = [lax.all_gather(shard, "fsdp", axis=1, tiled=True)]

    def blocks(self, width):
        return [(0, i, i) for i in range(0, self.sources[0].shape[1], width)]


def swap(x, axis, bits):
    return lax.ppermute(x, axis, [(i, i ^ bits) for i in range(lax.axis_size(axis))])


def hop_order(chips):
    odd = [k for k in range(chips - 1, 0, -1) if k % 2]
    return odd + [k for k in range(2, chips, 2)]


class SplitRows:
    def __init__(self, shard):
        self.chips = lax.axis_size("fsdp") // 2
        self.shard_rows = shard.shape[0]
        half = self.shard_rows // 2
        quarter = half // 2
        place = lax.axis_index("frame")
        side = (place ^ (place >> 1)) & 1
        self.sources = [shard, swap(shard, "fsdp", 1)]
        self.hops = hop_order(self.chips)
        mine = lax.dynamic_slice_in_dim(shard, side * half, half, 0)
        come = {}
        for k in self.hops:
            come[k] = swap(mine, "fsdp", 2 * k) if k % 2 else swap(come[k + 1], "fsdp", 2)
        for k in self.hops:
            got = come[k]
            joined = jnp.concatenate(
                [got, swap(got[:quarter], "frame", 1), swap(got[quarter:], "frame", 2)], axis=0
            )
            self.sources += [joined, swap(joined, "fsdp", 1)]

    def groups(self):
        chip = lax.axis_index("fsdp") // 2
        core = lax.axis_index("fsdp") % 2
        place = lax.axis_index("frame")
        side = (place ^ (place >> 1)) & 1
        rows, half = self.shard_rows, self.shard_rows // 2

        def aligned(value):
            return pl.multiple_of(value, half)

        out = [
            (
                pl.multiple_of(chip * 2 * rows, 2 * rows),
                [(0, 0, rows, aligned(core * rows)), (1, 0, rows, aligned((1 - core) * rows))],
            )
        ]
        for slot, k in enumerate(self.hops, 1):
            pieces = []
            for source, half_core in ((2 * slot, core), (2 * slot + 1, 1 - core)):
                base = slot * 2 * rows + half_core * rows
                pieces.append((source, 0, half, aligned(base + side * half)))
                pieces.append((source, half, half, aligned(base + (1 - side) * half)))
            out.append((pl.multiple_of((chip ^ k) * 2 * rows, 2 * rows), pieces))
        return out


class SplitColumns:
    def __init__(self, shard):
        self.chips = lax.axis_size("fsdp") // 2
        self.sources = [shard, swap(shard, "fsdp", 1)]
        self.hops = hop_order(self.chips)
        come = {}
        for k in self.hops:
            come[k] = swap(shard, "fsdp", 2 * k) if k % 2 else swap(come[k + 1], "fsdp", 2)
            self.sources += [come[k], swap(come[k], "fsdp", 1)]

    def blocks(self, width):
        place = lax.axis_index("fsdp")
        out = []
        for slot, k in enumerate([0] + self.hops):
            for core in range(2):
                out.append((2 * slot + core, 0, (place ^ (2 * k + core)) * width))
        return out


def on_device(frames, modulation, w_qkv, qk_gain, w_out):
    devices, places = lax.axis_size("fsdp"), lax.axis_size("frame")
    chips = devices // 2
    split = (
        devices % 2 == 0
        and chips & (chips - 1) == 0
        and places % 4 == 0
        and w_qkv.shape[0] % TILE == 0
        and w_out.shape[1] % TILE == 0
    )
    model = frames.shape[2]
    rows_plan = (SplitRows if split else WholeRows)(w_qkv)
    normed = norm_rows(frames[0], modulation[0])
    queries, stacked = project(rows_plan, normed, qk_gain)
    ends = places - 1
    before = lax.ppermute(stacked[-BORDER:], "frame", [(i, i + 1) for i in range(ends)])
    after = lax.ppermute(stacked[:BORDER], "frame", [(i + 1, i) for i in range(ends)])
    columns_plan = (SplitColumns if split else WholeColumns)(w_out)
    width = w_out.shape[1] if split else 3 * TILE
    return attend(columns_plan, queries, stacked, before, after, model, width)


def solution(mesh):
    return jax.shard_map(
        on_device,
        mesh=mesh,
        in_specs=(
            P("fsdp", "frame", None),
            P("fsdp", None, None),
            P("fsdp", None),
            P(),
            P(None, "fsdp"),
        ),
        out_specs=P("fsdp", "frame", None),
        check_vma=False,
    )
```

time: 102 us -> 76.7 us (0.75)
  waiting for transfers between devices: 62.6 us -> 38.3 us
  starting transfers between devices: 4.72 us -> 27.6 us
  between operations: 13.7 us -> 0.22 us
  matrix products: 9.54 us -> 0 us
  Pallas kernels: 0 us -> 9.22 us
  other arithmetic: 6.94 us -> 0 us
  local copies, waits for them, and re-layouts: 4.14 us -> 1.22 us
    all_gather x2 -> x0, waiting for transfers between devices: 49.4 us -> none  [the longest x1 49.4 us: on_device(): lax.all_gather(operand, 'fsdp', axis=0, tiled=True)]
    ppermute x2 -> x22, waiting for transfers between devices: 11.8 us -> 38.3 us  [the longest x20 27.4 us: swap(): lax.ppermute(x, axis, [(i, i ^ bits) for i in range(lax.axis_size(axis))])]
    ppermute x2 -> x22, starting transfers between devices: 4.68 us -> 27.6 us  [the longest x20 24 us: swap(): lax.ppermute(x, axis, [(i, i ^ bits) for i in range(lax.axis_size(axis))])]
    dot_general x4 -> x0, matrix products: 9.54 us -> none  [the longest x1 4.61 us: fold_rows(): return jnp.dot(normed, block_rows, preferred_element_type=jnp.float32)]
    pallas_call x0 -> x3, Pallas kernels: none -> 9.22 us  [the longest x1 4.03 us: project(): pl.pallas_call(functools.partial(project_kernel, plan, width // groups),...]
    reduce_sum x4 -> x0, other arithmetic: 3.78 us -> none  [the longest x1 2.07 us: norm_rows(): average = jnp.mean(values_full, axis=-1, keepdims=True)]
    add x2 -> x0, other arithmetic: 2.02 us -> none  [the longest x1 1.44 us: norm_rows(): 1.0 + modulation_rows[0]]
    mul x6 -> x0, local copies, waits for them, and re-layouts: 1.93 us -> none  [the longest x4 1.52 us: head_norm(): scaled = shaped * lax.rsqrt(squares + 1e-06) * gain_row]
  transfers between devices with their start and end apart: 4 -> 22, of which waited for: 3 -> 12; matrix products, arithmetic and copies ran while one was open for 17% -> 0% of each run, Pallas kernels for 0% -> 8%
where the time goes in v1:
time: 76.7 us; the launch traced here: 76.5 us
  waiting for transfers between devices  38.3 us (50%)
  starting transfers between devices  27.6 us (36%)
  Pallas kernels  9.22 us (12%)
  local copies, waits for them, and re-layouts  1.22 us (2%)
    ppermute x20, waiting for transfers between devices, swap(): lax.ppermute(x, axis, [(i, i ^ bits) for i in range(lax.axis_size(axis))])  27.4 us
    ppermute x20, starting transfers between devices, swap(): lax.ppermute(x, axis, [(i, i ^ bits) for i in range(lax.axis_size(axis))])  24 us
    ppermute x1, waiting for transfers between devices, on_device(): lax.ppermute(stacked[:BORDER], 'frame', [(i + 1, i) for i in range(ends)])  8.76 us
    pallas_call x1, Pallas kernels, project(): pl.pallas_call(functools.partial(project_kernel, plan, width // groups),...  4.03 us
    pallas_call x1, Pallas kernels, attend(): pl.pallas_call(functools.partial(attend_kernel, out_plan), in_specs=[VMEM...  3.02 us
    ppermute x1, starting transfers between devices, on_device(): lax.ppermute(stacked[-BORDER:], 'frame', [(i, i + 1) for i in range(ends)])  2.22 us
    pallas_call x1, Pallas kernels, norm_rows(): pl.pallas_call(norm_kernel, grid=(rows // block,), in_specs=[pl.BlockSpec...  2.17 us
    ppermute x1, waiting for transfers between devices, on_device(): lax.ppermute(stacked[-BORDER:], 'frame', [(i, i + 1) for i in range(ends)])  2.11 us
  transfers between devices with their start and end apart: 22, of which 12 were waited for; matrix products, arithmetic and copies ran while one was open for 0% of the time, Pallas kernels for 8%

profile of v1, /device:TPU:0, one launch (start us, length us, event | category | flops | bytes accessed | tf_op | source)
XLA Modules:
  0.0 76.5 jit_solution(9930018998541543654)
XLA Ops:
  0.0 1.0 %constant_dynamic-slice_fusion = bf16[192,768]{1,0:T(8,128)(2,1)S(1)} fusion(bf16[384,768]{1,0:T(8,128)(2,1)} %refs_0_.2, s32[]{:T(128)S(6)} %select_n.3), kind=kLoop, calls=%fused_computation.9 | loop fusion | bytes 589828 | tf_op jit(solution)/shard_map/dynamic_slice | solution.py:243
  1.0 5.1 %collective-permute-start.1 = (bf16[192,768]{1,0:T(8,128)(2,1)S(1)}, bf16[192,768]{1,0:T(8,128)(2,1)S(1)}, u32[]{:S(2)}, u32[]{:S(2)}) collective-permute-start(bf16[192,768]{1,0:T(8,128)(2,1)S(1)} %constant_dynamic-slice_fusion), channel_id=1, source_target_pairs={{0,24},{4,28},{8,16},{12,20},{16,8},{20,12},{24,0},{28,4},{1,25},{... | collective-permute-start | bytes 884744 | tf_op jit(solution)/shard_map/ppermute | solution.py:225
  6.1 7.9 %collective-permute-done.1 = bf16[192,768]{1,0:T(8,128)(2,1)S(1)} collective-permute-done((bf16[192,768]{1,0:T(8,128)(2,1)S(1)}, bf16[192,768]{1,0:T(8,128)(2,1)S(1)}, u32[]{:S(2)}, u32[]{:S(2)}) %collective-permute-start.1) | collective-permute-done | bytes 294944 | tf_op jit(solution)/shard_map/ppermute | solution.py:225
  14.0 1.8 %collective-permute-start.2 = (bf16[96,768]{1,0:T(8,128)(2,1)S(1)}, bf16[96,768]{1,0:T(8,128)(2,1)S(1)}, u32[]{:S(2)}, u32[]{:S(2)}) collective-permute-start(bf16[96,768]{1,0:T(8,128)(2,1)S(1)} %get-tuple-element.16), channel_id=1, source_target_pairs={{0,1},{1,0},{2,3},{3,2},{4,5},{5,4},{6,7},{7,6},{8,9},{9,8},{10,11... | collective-permute-start | bytes 442376 | tf_op jit(solution)/shard_map/ppermute | solution.py:225
  15.8 1.5 %collective-permute-start.3 = (bf16[96,768]{1,0:T(8,128)(2,1)S(1)}, bf16[96,768]{1,0:T(8,128)(2,1)S(1)}, u32[]{:S(2)}, u32[]{:S(2)}) collective-permute-start(bf16[96,768]{1,0:T(8,128)(2,1)S(1)} %get-tuple-element.15), channel_id=1, source_target_pairs={{0,2},{1,3},{2,0},{3,1},{4,6},{5,7},{6,4},{7,5},{8,10},{9,11},{10,... | collective-permute-start | bytes 442376 | tf_op jit(solution)/shard_map/ppermute | solution.py:225
  17.3 2.2 %collective-permute-done.5 = bf16[192,768]{1,0:T(8,128)(2,1)S(1)} collective-permute-done((bf16[192,768]{1,0:T(8,128)(2,1)S(1)}, bf16[192,768]{1,0:T(8,128)(2,1)S(1)}, u32[]{:S(2)}, u32[]{:S(2)}) %collective-permute-start.5) | collective-permute-done | bytes 294944 | tf_op jit(solution)/shard_map/ppermute | solution.py:225
  19.6 1.6 %collective-permute-start.6 = (bf16[96,768]{1,0:T(8,128)(2,1)S(1)}, bf16[96,768]{1,0:T(8,128)(2,1)S(1)}, u32[]{:S(2)}, u32[]{:S(2)}) collective-permute-start(bf16[96,768]{1,0:T(8,128)(2,1)S(1)} %get-tuple-element.14), channel_id=1, source_target_pairs={{0,1},{1,0},{2,3},{3,2},{4,5},{5,4},{6,7},{7,6},{8,9},{9,8},{10,11... | collective-permute-start | bytes 442376 | tf_op jit(solution)/shard_map/ppermute | solution.py:225
  21.1 1.5 %collective-permute-start.7 = (bf16[96,768]{1,0:T(8,128)(2,1)S(1)}, bf16[96,768]{1,0:T(8,128)(2,1)S(1)}, u32[]{:S(2)}, u32[]{:S(2)}) collective-permute-start(bf16[96,768]{1,0:T(8,128)(2,1)S(1)} %get-tuple-element.13), channel_id=1, source_target_pairs={{0,2},{1,3},{2,0},{3,1},{4,6},{5,7},{6,4},{7,5},{8,10},{9,11},{10,... | collective-permute-start | bytes 442376 | tf_op jit(solution)/shard_map/ppermute | solution.py:225
  22.7 2.6 %collective-permute-start.9 = (bf16[192,768]{1,0:T(8,128)(2,1)S(1)}, bf16[192,768]{1,0:T(8,128)(2,1)S(1)}, u32[]{:S(2)}, u32[]{:S(2)}) collective-permute-start(bf16[192,768]{1,0:T(8,128)(2,1)S(1)} %collective-permute-done.1), channel_id=1, source_target_pairs={{0,8},{4,12},{8,0},{12,4},{16,24},{20,28},{24,16},{28,20},{1,9},{5... | collective-permute-start | bytes 884744 | tf_op jit(solution)/shard_map/ppermute | solution.py:225
  25.4 5.7 %collective-permute-done.9 = bf16[192,768]{1,0:T(8,128)(2,1)S(1)} collective-permute-done((bf16[192,768]{1,0:T(8,128)(2,1)S(1)}, bf16[192,768]{1,0:T(8,128)(2,1)S(1)}, u32[]{:S(2)}, u32[]{:S(2)}) %collective-permute-start.9) | collective-permute-done | bytes 294944 | tf_op jit(solution)/shard_map/ppermute | solution.py:225
  31.1 1.0 %collective-permute-start.10 = (bf16[96,768]{1,0:T(8,128)(2,1)S(1)}, bf16[96,768]{1,0:T(8,128)(2,1)S(1)}, u32[]{:S(2)}, u32[]{:S(2)}) collective-permute-start(bf16[96,768]{1,0:T(8,128)(2,1)S(1)} %get-tuple-element.12), channel_id=1, source_target_pairs={{0,1},{1,0},{2,3},{3,2},{4,5},{5,4},{6,7},{7,6},{8,9},{9,8},{10,11... | collective-permute-start | bytes 442376 | tf_op jit(solution)/shard_map/ppermute | solution.py:225
  32.2 1.6 %collective-permute-start.11 = (bf16[96,768]{1,0:T(8,128)(2,1)S(1)}, bf16[96,768]{1,0:T(8,128)(2,1)S(1)}, u32[]{:S(2)}, u32[]{:S(2)}) collective-permute-start(bf16[96,768]{1,0:T(8,128)(2,1)S(1)} %get-tuple-element.11), channel_id=1, source_target_pairs={{0,2},{1,3},{2,0},{3,1},{4,6},{5,7},{6,4},{7,5},{8,10},{9,11},{10,... | collective-permute-start | bytes 442376 | tf_op jit(solution)/shard_map/ppermute | solution.py:225
  33.8 2.5 %collective-permute-done.10 = bf16[96,768]{1,0:T(8,128)(2,1)S(1)} collective-permute-done((bf16[96,768]{1,0:T(8,128)(2,1)S(1)}, bf16[96,768]{1,0:T(8,128)(2,1)S(1)}, u32[]{:S(2)}, u32[]{:S(2)}) %collective-permute-start.10) | collective-permute-done | bytes 147488 | tf_op jit(solution)/shard_map/ppermute | solution.py:225
  36.4 2.1 %collective-permute-done.11 = bf16[96,768]{1,0:T(8,128)(2,1)S(1)} collective-permute-done((bf16[96,768]{1,0:T(8,128)(2,1)S(1)}, bf16[96,768]{1,0:T(8,128)(2,1)S(1)}, u32[]{:S(2)}, u32[]{:S(2)}) %collective-permute-start.11) | collective-permute-done | bytes 147488 | tf_op jit(solution)/shard_map/ppermute | solution.py:225
  38.6 2.2 %collective-permute-start.16 = (bf16[256,384]{1,0:T(8,128)(2,1)S(1)}, bf16[256,384]{1,0:T(8,128)(2,1)S(1)}, u32[]{:S(2)}, u32[]{:S(2)}) collective-permute-start(bf16[256,384]{1,0:T(8,128)(2,1)S(1)} %copy-done.2), channel_id=1, source_target_pairs={{0,24},{4,28},{8,16},{12,20},{16,8},{20,12},{24,0},{28,4},{1,25},{... | collective-permute-start | bytes 589832 | tf_op jit(solution)/shard_map/ppermute | solution.py:225
  40.8 2.2 %layer_norm.1.normed_ref = bf16[384,3072]{1,0:T(8,128)(2,1)S(1)} custom-call(bf16[384,3072]{1,0:T(8,128)(2,1)S(1)} %bitcast.2, f32[2,3072]{1,0:T(2,128)S(1)} %bitcast.3), custom_call_target="tpu_custom_call" | custom-call | flops 11796480 | bytes 4718592 | tf_op jit(solution)/shard_map/layer_norm/pallas_call | solution.py:49
  43.0 4.8 %collective-permute-done.16.refs_2_ = bf16[256,384]{1,0:T(8,128)(2,1)S(1)} collective-permute-done((bf16[256,384]{1,0:T(8,128)(2,1)S(1)}, bf16[256,384]{1,0:T(8,128)(2,1)S(1)}, u32[]{:S(2)}, u32[]{:S(2)}) %collective-permute-start.16) | collective-permute-done | bytes 196640 | tf_op jit(solution)/shard_map/ppermute | solution.py:225
  47.8 4.3 %collective-permute-start.18 = (bf16[256,384]{1,0:T(8,128)(2,1)S(1)}, bf16[256,384]{1,0:T(8,128)(2,1)S(1)}, u32[]{:S(2)}, u32[]{:S(2)}) collective-permute-start(bf16[256,384]{1,0:T(8,128)(2,1)S(1)} %copy-done.2), channel_id=1, source_target_pairs={{0,8},{4,12},{8,0},{12,4},{16,24},{20,28},{24,16},{28,20},{1,9},{5... | collective-permute-start | bytes 589832 | tf_op jit(solution)/shard_map/ppermute | solution.py:225
  52.3 4.0 %project.1 = (bf16[384,256]{1,0:T(8,128)(2,1)S(1)}, bf16[384,512]{1,0:T(8,128)(2,1)S(1)}) custom-call(bf16[384,3072]{1,0:T(8,128)(2,1)S(1)} %layer_norm.1.normed_ref, f32[2,128]{1,0:T(2,128)S(1)} %copy-done.4, bf16[384,768]{1,0:T(8,128)(2,1)S(1)} %copy-done.1, bf16[384,768]{1,0:T(8,128)(2,1)S(1)} %collective-permute-done.refs_1_, ...), custom_call_target="tpu_custom_call" | custom-call | flops 1811939328 | bytes 7077888 | tf_op jit(solution)/shard_map/project/pallas_call | solution.py:112
  56.4 2.2 %collective-permute-start.13 = (bf16[256,512]{1,0:T(8,128)(2,1)S(1)}, bf16[256,512]{1,0:T(8,128)(2,1)S(1)}, u32[]{:S(2)}, u32[]{:S(2)}) collective-permute-start(bf16[256,512]{1,0:T(8,128)(2,1)S(1)} %get-tuple-element.10), channel_id=1, source_target_pairs={{0,1},{1,2},{2,3},{4,5},{5,6},{6,7},{8,9},{9,10},{10,11},{12,13},{... | collective-permute-start | bytes 786440 | tf_op jit(solution)/shard_map/ppermute | solution.py:314
  58.6 1.3 %collective-permute-start.14 = (bf16[256,512]{1,0:T(8,128)(2,1)S(1)}, bf16[256,512]{1,0:T(8,128)(2,1)S(1)}, u32[]{:S(2)}, u32[]{:S(2)}) collective-permute-start(bf16[256,512]{1,0:T(8,128)(2,1)S(1)} %get-tuple-element.9), channel_id=1, source_target_pairs={{1,0},{2,1},{3,2},{5,4},{6,5},{7,6},{9,8},{10,9},{11,10},{13,12},{... | collective-permute-start | bytes 786440 | tf_op jit(solution)/shard_map/ppermute | solution.py:315
  62.6 2.1 %collective-permute-done.13.before_ref = bf16[256,512]{1,0:T(8,128)(2,1)S(1)} collective-permute-done((bf16[256,512]{1,0:T(8,128)(2,1)S(1)}, bf16[256,512]{1,0:T(8,128)(2,1)S(1)}, u32[]{:S(2)}, u32[]{:S(2)}) %collective-permute-start.13) | collective-permute-done | bytes 262176 | tf_op jit(solution)/shard_map/ppermute | solution.py:314
  64.7 8.8 %collective-permute-done.14.after_ref = bf16[256,512]{1,0:T(8,128)(2,1)S(1)} collective-permute-done((bf16[256,512]{1,0:T(8,128)(2,1)S(1)}, bf16[256,512]{1,0:T(8,128)(2,1)S(1)}, u32[]{:S(2)}, u32[]{:S(2)}) %collective-permute-start.14) | collective-permute-done | bytes 262176 | tf_op jit(solution)/shard_map/ppermute | solution.py:315
  73.5 3.0 %attend_and_mix.1 = bf16[1,384,3072]{2,1,0:T(8,128)(2,1)} custom-call(bf16[384,256]{1,0:T(8,128)(2,1)S(1)} %get-tuple-element.7.queries_ref, bf16[384,512]{1,0:T(8,128)(2,1)S(1)} %get-tuple-element.8.stacked_ref, bf16[256,512]{1,0:T(8,128)(2,1)S(1)} %collective-permute-done.13.before_ref, bf16[256,512]{1,0:T(8,128)(2,1)S(1)} %collective-permute-done.14.after_ref, ...), custom_call_target="tpu_custom_call" | custom-call | flops 855638016 | bytes 3932160 | tf_op jit(solution)/shard_map/attend_and_mix/pallas_call | solution.py:187
  (47 shorter events, 3.3 us)
Async XLA Ops:
  1.0 13.0 %collective-permute-start.1 = (bf16[192,768]{1,0:T(8,128)(2,1)S(1)}, bf16[192,768]{1,0:T(8,128)(2,1)S(1)}, u32[]{:S(2)}, u32[]{:S(2)}) collective-permute-start(bf16[192,768]{1,0:T(8,128)(2,1)S(1)} %constant_dynamic-slice_fusion), channel_id=1, source_target_pairs={{0,24},{4,28},{8,16},{12,20},{16,8},{20,12},{24,0},{28,4},{1,25},{... | collective-permute-start | bytes 884744 | tf_op jit(solution)/shard_map/ppermute | solution.py:225
  6.1 13.4 %collective-permute-start.5 = (bf16[192,768]{1,0:T(8,128)(2,1)S(1)}, bf16[192,768]{1,0:T(8,128)(2,1)S(1)}, u32[]{:S(2)}, u32[]{:S(2)}) collective-permute-start(bf16[192,768]{1,0:T(8,128)(2,1)S(1)} %constant_dynamic-slice_fusion), channel_id=1, source_target_pairs={{0,8},{4,12},{8,0},{12,4},{16,24},{20,28},{24,16},{28,20},{1,9},{5... | collective-permute-start | bytes 884744 | tf_op jit(solution)/shard_map/ppermute | solution.py:225
  6.1 46.0 %collective-permute-start = (bf16[384,768]{1,0:T(8,128)(2,1)}, bf16[384,768]{1,0:T(8,128)(2,1)S(1)}, u32[]{:S(2)}, u32[]{:S(2)}) collective-permute-start(bf16[384,768]{1,0:T(8,128)(2,1)} %refs_0_.2), channel_id=1, source_target_pairs={{0,4},{4,0},{8,12},{12,8},{16,20},{20,16},{24,28},{28,24},{1,5},{5... | collective-permute-start | bytes 1769480 | tf_op jit(solution)/shard_map/ppermute | solution.py:225
  14.0 8.6 %collective-permute-start.2 = (bf16[96,768]{1,0:T(8,128)(2,1)S(1)}, bf16[96,768]{1,0:T(8,128)(2,1)S(1)}, u32[]{:S(2)}, u32[]{:S(2)}) collective-permute-start(bf16[96,768]{1,0:T(8,128)(2,1)S(1)} %get-tuple-element.16), channel_id=1, source_target_pairs={{0,1},{1,0},{2,3},{3,2},{4,5},{5,4},{6,7},{7,6},{8,9},{9,8},{10,11... | collective-permute-start | bytes 442376 | tf_op jit(solution)/shard_map/ppermute | solution.py:225
  15.8 25.0 %copy-start = (bf16[1,384,3072]{2,1,0:T(8,128)(2,1)S(1)}, bf16[1,384,3072]{2,1,0:T(8,128)(2,1)}, u32[]{:S(2)}) copy-start(bf16[1,384,3072]{2,1,0:T(8,128)(2,1)} %param.5) | copy-start | bytes 7077892
  15.8 25.0 %copy-start.3 = (f32[1,2,3072]{2,1,0:T(2,128)S(1)}, f32[1,2,3072]{2,1,0:T(2,128)}, u32[]{:S(2)}) copy-start(f32[1,2,3072]{2,1,0:T(2,128)} %param.6) | copy-start | bytes 73732
  15.8 9.5 %collective-permute-start.3 = (bf16[96,768]{1,0:T(8,128)(2,1)S(1)}, bf16[96,768]{1,0:T(8,128)(2,1)S(1)}, u32[]{:S(2)}, u32[]{:S(2)}) collective-permute-start(bf16[96,768]{1,0:T(8,128)(2,1)S(1)} %get-tuple-element.15), channel_id=1, source_target_pairs={{0,2},{1,3},{2,0},{3,1},{4,6},{5,7},{6,4},{7,5},{8,10},{9,11},{10,... | collective-permute-start | bytes 442376 | tf_op jit(solution)/shard_map/ppermute | solution.py:225
  19.6 5.8 %collective-permute-start.6 = (bf16[96,768]{1,0:T(8,128)(2,1)S(1)}, bf16[96,768]{1,0:T(8,128)(2,1)S(1)}, u32[]{:S(2)}, u32[]{:S(2)}) collective-permute-start(bf16[96,768]{1,0:T(8,128)(2,1)S(1)} %get-tuple-element.14), channel_id=1, source_target_pairs={{0,1},{1,0},{2,3},{3,2},{4,5},{5,4},{6,7},{7,6},{8,9},{9,8},{10,11... | collective-permute-start | bytes 442376 | tf_op jit(solution)/shard_map/ppermute | solution.py:225
  21.1 11.0 %collective-permute-start.7 = (bf16[96,768]{1,0:T(8,128)(2,1)S(1)}, bf16[96,768]{1,0:T(8,128)(2,1)S(1)}, u32[]{:S(2)}, u32[]{:S(2)}) collective-permute-start(bf16[96,768]{1,0:T(8,128)(2,1)S(1)} %get-tuple-element.13), channel_id=1, source_target_pairs={{0,2},{1,3},{2,0},{3,1},{4,6},{5,7},{6,4},{7,5},{8,10},{9,11},{10,... | collective-permute-start | bytes 442376 | tf_op jit(solution)/shard_map/ppermute | solution.py:225
  22.7 8.4 %collective-permute-start.9 = (bf16[192,768]{1,0:T(8,128)(2,1)S(1)}, bf16[192,768]{1,0:T(8,128)(2,1)S(1)}, u32[]{:S(2)}, u32[]{:S(2)}) collective-permute-start(bf16[192,768]{1,0:T(8,128)(2,1)S(1)} %collective-permute-done.1), channel_id=1, source_target_pairs={{0,8},{4,12},{8,0},{12,4},{16,24},{20,28},{24,16},{28,20},{1,9},{5... | collective-permute-start | bytes 884744 | tf_op jit(solution)/shard_map/ppermute | solution.py:225
  25.3 26.8 %collective-permute-start.4 = (bf16[384,768]{1,0:T(8,128)(2,1)S(1)}, bf16[384,768]{1,0:T(8,128)(2,1)S(1)}, u32[]{:S(2)}, u32[]{:S(2)}) collective-permute-start(bf16[384,768]{1,0:T(8,128)(2,1)S(1)} %constant_dynamic-update-slice_fusion.refs_2_), channel_id=1, source_target_pairs={{0,4},{4,0},{8,12},{12,8},{16,20},{20,16},{24,28},{28,24},{1,5},{5... | collective-permute-start | bytes 1769480 | tf_op jit(solution)/shard_map/ppermute | solution.py:225
  31.1 5.2 %collective-permute-start.10 = (bf16[96,768]{1,0:T(8,128)(2,1)S(1)}, bf16[96,768]{1,0:T(8,128)(2,1)S(1)}, u32[]{:S(2)}, u32[]{:S(2)}) collective-permute-start(bf16[96,768]{1,0:T(8,128)(2,1)S(1)} %get-tuple-element.12), channel_id=1, source_target_pairs={{0,1},{1,0},{2,3},{3,2},{4,5},{5,4},{6,7},{7,6},{8,9},{9,8},{10,11... | collective-permute-start | bytes 442376 | tf_op jit(solution)/shard_map/ppermute | solution.py:225
  32.1 20.1 %collective-permute-start.8 = (bf16[384,768]{1,0:T(8,128)(2,1)S(1)}, bf16[384,768]{1,0:T(8,128)(2,1)S(1)}, u32[]{:S(2)}, u32[]{:S(2)}) collective-permute-start(bf16[384,768]{1,0:T(8,128)(2,1)S(1)} %constant_dynamic-update-slice_fusion.3.refs_4_), channel_id=1, source_target_pairs={{0,4},{4,0},{8,12},{12,8},{16,20},{20,16},{24,28},{28,24},{1,5},{5... | collective-permute-start | bytes 1769480 | tf_op jit(solution)/shard_map/ppermute | solution.py:225
  32.2 6.3 %collective-permute-start.11 = (bf16[96,768]{1,0:T(8,128)(2,1)S(1)}, bf16[96,768]{1,0:T(8,128)(2,1)S(1)}, u32[]{:S(2)}, u32[]{:S(2)}) collective-permute-start(bf16[96,768]{1,0:T(8,128)(2,1)S(1)} %get-tuple-element.11), channel_id=1, source_target_pairs={{0,2},{1,3},{2,0},{3,1},{4,6},{5,7},{6,4},{7,5},{8,10},{9,11},{10,... | collective-permute-start | bytes 442376 | tf_op jit(solution)/shard_map/ppermute | solution.py:225
  38.5 13.7 %collective-permute-start.12 = (bf16[384,768]{1,0:T(8,128)(2,1)S(1)}, bf16[384,768]{1,0:T(8,128)(2,1)S(1)}, u32[]{:S(2)}, u32[]{:S(2)}) collective-permute-start(bf16[384,768]{1,0:T(8,128)(2,1)S(1)} %constant_dynamic-update-slice_fusion.6.refs_6_), channel_id=1, source_target_pairs={{0,4},{4,0},{8,12},{12,8},{16,20},{20,16},{24,28},{28,24},{1,5},{5... | collective-permute-start | bytes 1769480 | tf_op jit(solution)/shard_map/ppermute | solution.py:225
  38.6 9.2 %collective-permute-start.16 = (bf16[256,384]{1,0:T(8,128)(2,1)S(1)}, bf16[256,384]{1,0:T(8,128)(2,1)S(1)}, u32[]{:S(2)}, u32[]{:S(2)}) collective-permute-start(bf16[256,384]{1,0:T(8,128)(2,1)S(1)} %copy-done.2), channel_id=1, source_target_pairs={{0,24},{4,28},{8,16},{12,20},{16,8},{20,12},{24,0},{28,4},{1,25},{... | collective-permute-start | bytes 589832 | tf_op jit(solution)/shard_map/ppermute | solution.py:225
  47.8 12.1 %collective-permute-start.18 = (bf16[256,384]{1,0:T(8,128)(2,1)S(1)}, bf16[256,384]{1,0:T(8,128)(2,1)S(1)}, u32[]{:S(2)}, u32[]{:S(2)}) collective-permute-start(bf16[256,384]{1,0:T(8,128)(2,1)S(1)} %copy-done.2), channel_id=1, source_target_pairs={{0,8},{4,12},{8,0},{12,4},{16,24},{20,28},{24,16},{28,20},{1,9},{5... | collective-permute-start | bytes 589832 | tf_op jit(solution)/shard_map/ppermute | solution.py:225
  52.1 8.0 %collective-permute-start.15 = (bf16[256,384]{1,0:T(8,128)(2,1)S(1)}, bf16[256,384]{1,0:T(8,128)(2,1)S(1)}, u32[]{:S(2)}, u32[]{:S(2)}) collective-permute-start(bf16[256,384]{1,0:T(8,128)(2,1)S(1)} %copy-done.2), channel_id=1, source_target_pairs={{0,4},{4,0},{8,12},{12,8},{16,20},{20,16},{24,28},{28,24},{1,5},{5... | collective-permute-start | bytes 589832 | tf_op jit(solution)/shard_map/ppermute | solution.py:225
  52.2 9.0 %collective-permute-start.20 = (bf16[256,384]{1,0:T(8,128)(2,1)S(1)}, bf16[256,384]{1,0:T(8,128)(2,1)S(1)}, u32[]{:S(2)}, u32[]{:S(2)}) collective-permute-start(bf16[256,384]{1,0:T(8,128)(2,1)S(1)} %collective-permute-done.16.refs_2_), channel_id=1, source_target_pairs={{0,8},{4,12},{8,0},{12,4},{16,24},{20,28},{24,16},{28,20},{1,9},{5... | collective-permute-start | bytes 589832 | tf_op jit(solution)/shard_map/ppermute | solution.py:225
  56.4 8.4 %collective-permute-start.13 = (bf16[256,512]{1,0:T(8,128)(2,1)S(1)}, bf16[256,512]{1,0:T(8,128)(2,1)S(1)}, u32[]{:S(2)}, u32[]{:S(2)}) collective-permute-start(bf16[256,512]{1,0:T(8,128)(2,1)S(1)} %get-tuple-element.10), channel_id=1, source_target_pairs={{0,1},{1,2},{2,3},{4,5},{5,6},{6,7},{8,9},{9,10},{10,11},{12,13},{... | collective-permute-start | bytes 786440 | tf_op jit(solution)/shard_map/ppermute | solution.py:314
  58.6 14.9 %collective-permute-start.14 = (bf16[256,512]{1,0:T(8,128)(2,1)S(1)}, bf16[256,512]{1,0:T(8,128)(2,1)S(1)}, u32[]{:S(2)}, u32[]{:S(2)}) collective-permute-start(bf16[256,512]{1,0:T(8,128)(2,1)S(1)} %get-tuple-element.9), channel_id=1, source_target_pairs={{1,0},{2,1},{3,2},{5,4},{6,5},{7,6},{9,8},{10,9},{11,10},{13,12},{... | collective-permute-start | bytes 786440 | tf_op jit(solution)/shard_map/ppermute | solution.py:315
  59.9 1.5 %collective-permute-start.17 = (bf16[256,384]{1,0:T(8,128)(2,1)S(1)}, bf16[256,384]{1,0:T(8,128)(2,1)S(1)}, u32[]{:S(2)}, u32[]{:S(2)}) collective-permute-start(bf16[256,384]{1,0:T(8,128)(2,1)S(1)} %collective-permute-done.16.refs_2_), channel_id=1, source_target_pairs={{0,4},{4,0},{8,12},{12,8},{16,20},{20,16},{24,28},{28,24},{1,5},{5... | collective-permute-start | bytes 589832 | tf_op jit(solution)/shard_map/ppermute | solution.py:225
  60.1 1.6 %collective-permute-start.19 = (bf16[256,384]{1,0:T(8,128)(2,1)S(1)}, bf16[256,384]{1,0:T(8,128)(2,1)S(1)}, u32[]{:S(2)}, u32[]{:S(2)}) collective-permute-start(bf16[256,384]{1,0:T(8,128)(2,1)S(1)} %collective-permute-done.18.refs_4_), channel_id=1, source_target_pairs={{0,4},{4,0},{8,12},{12,8},{16,20},{20,16},{24,28},{28,24},{1,5},{5... | collective-permute-start | bytes 589832 | tf_op jit(solution)/shard_map/ppermute | solution.py:225
  61.2 1.4 %collective-permute-start.21 = (bf16[256,384]{1,0:T(8,128)(2,1)S(1)}, bf16[256,384]{1,0:T(8,128)(2,1)S(1)}, u32[]{:S(2)}, u32[]{:S(2)}) collective-permute-start(bf16[256,384]{1,0:T(8,128)(2,1)S(1)} %collective-permute-done.20.refs_6_), channel_id=1, source_target_pairs={{0,4},{4,0},{8,12},{12,8},{16,20},{20,16},{24,28},{28,24},{1,5},{5... | collective-permute-start | bytes 589832 | tf_op jit(solution)/shard_map/ppermute | solution.py:225
  (3 other events, 45.6 us)

commit v2 on v1

v2 whole, which is shorter than its diff:
```python
import functools
import math

import jax
import jax.numpy as jnp
from jax import lax
from jax.experimental import pallas as pl
from jax.experimental.pallas import tpu as pltpu
from jax.sharding import PartitionSpec as P

HEAD_DIM = 128
HEADS = 2
WIDTH = HEADS * HEAD_DIM
TILE = 128
REACH = 2
BORDER = REACH * TILE
VMEM_BYTES = 40 * 1024 * 1024

f32 = jnp.float32
bf16 = jnp.bfloat16
ANY = pl.BlockSpec(memory_space=pl.ANY)
VMEM = pl.BlockSpec(memory_space=pltpu.VMEM)


def params():
    return pltpu.CompilerParams(vmem_limit_bytes=VMEM_BYTES)


def dot(a, b):
    return jnp.dot(a, b, preferred_element_type=f32)


def dot_t(a, b):
    return lax.dot_general(a, b, (((1,), (1,)), ((), ())), preferred_element_type=f32)


def norm_kernel(frames_ref, modulation_ref, normed_ref, values_ref, rows_ref, sems):
    blocks, rows = values_ref.shape[0], values_ref.shape[1]
    copies = [pltpu.make_async_copy(modulation_ref, rows_ref, sems.at[blocks])]
    for i in range(blocks):
        copies.append(
            pltpu.make_async_copy(
                frames_ref.at[pl.ds(i * rows, rows)], values_ref.at[i], sems.at[i]
            )
        )
    for copy in copies:
        copy.start()
    copies[0].wait()
    scale, shift = 1.0 + rows_ref[0:1], rows_ref[1:2]
    for i in range(blocks):
        copies[1 + i].wait()
        values = values_ref[i].astype(f32)
        average = jnp.mean(values, axis=-1, keepdims=True)
        centered = values - average
        spread = jnp.mean(centered * centered, axis=-1, keepdims=True)
        normed = centered * lax.rsqrt(spread + 1e-06)
        normed_ref[i * rows : (i + 1) * rows] = (normed * scale + shift).astype(bf16)


def norm_rows(frames, modulation):
    rows, width = frames.shape
    block = TILE // 2
    return pl.pallas_call(
        norm_kernel,
        in_specs=[ANY, ANY],
        out_specs=VMEM,
        out_shape=jax.ShapeDtypeStruct((rows, width), bf16),
        scratch_shapes=[
            pltpu.VMEM((rows // block, block, width), bf16),
            pltpu.VMEM((2, width), f32),
            pltpu.SemaphoreType.DMA((rows // block + 1,)),
        ],
        compiler_params=params(),
        cost_estimate=pl.CostEstimate(
            flops=10 * rows * width, bytes_accessed=4 * rows * width, transcendentals=rows
        ),
        name="layer_norm",
    )(frames, modulation)


def head_norm(x, gain_row):
    squares = jnp.mean(x * x, axis=-1, keepdims=True)
    return (x * lax.rsqrt(squares + 1e-06) * gain_row).astype(bf16)


def project_kernel(count, starts, kinds, columns, resumed, gain_ref, *refs):
    lefts, rights = refs[:count], refs[count : 2 * count]
    total_ref, out_ref = refs[2 * count] if resumed else None, refs[-1]
    first, number = columns
    total = total_ref[:, first : first + number] if resumed else None
    for i in range(count):
        depth = rights[i].shape[0]
        left = lefts[i][...] if starts is None else lefts[i][:, pl.ds(starts()[i], depth)]
        part = dot(left, rights[i][:, first : first + number])
        total = part if total is None else total + part
    if kinds is None:
        out_ref[...] = total
        return
    for block, kind in enumerate(kinds):
        for head in range(HEADS):
            begin = block * WIDTH + head * HEAD_DIM
            x = total[:, begin : begin + HEAD_DIM]
            out_ref[:, begin : begin + HEAD_DIM] = (
                x.astype(bf16) if kind is None else head_norm(x, gain_ref[kind : kind + 1])
            )


def project(pairs, qk_gain, columns, name, starts=None, kinds=None, total=None):
    lefts, rights = [list(side) for side in zip(*pairs)]
    rows = lefts[0].shape[0]
    depth = sum(right.shape[0] for right in rights)
    resumed = total is not None
    operands = [qk_gain, *lefts, *rights] + [total] * resumed
    return pl.pallas_call(
        functools.partial(project_kernel, len(pairs), starts, kinds, columns, resumed),
        in_specs=[VMEM] * len(operands),
        out_specs=VMEM,
        out_shape=jax.ShapeDtypeStruct((rows, columns[1]), f32 if kinds is None else bf16),
        compiler_params=params(),
        cost_estimate=pl.CostEstimate(
            flops=2 * rows * depth * columns[1],
            bytes_accessed=2 * depth * (rows + columns[1]),
            transcendentals=rows,
        ),
        name=name,
    )(*operands)


def arrange_kernel(starts, order, homes, normed_ref, *out_refs):
    rows = normed_ref.shape[0]
    places, cores = starts()
    depth = normed_ref.shape[1] // lax.axis_size("fsdp")
    quarter = depth // 4
    source = lax.broadcasted_iota(jnp.int32, (depth, depth), 0)
    target = lax.broadcasted_iota(jnp.int32, (depth, depth), 1)
    for here in range(2):
        wanted = target
        for i, number in enumerate(order(cores[here])):
            inside = (target >= i * quarter) & (target < (i + 1) * quarter)
            wanted = jnp.where(inside, target + (number - i) * quarter, wanted)
        chosen = (source == wanted).astype(f32).astype(bf16)
        for slot, place in enumerate(places[here]):
            strip = normed_ref[:, pl.ds(pl.multiple_of(place, TILE), depth)]
            moved = dot(strip, chosen).astype(bf16)
            for i, (out, at) in enumerate(homes[slot]):
                out_refs[2 * out + here][:, at * quarter : (at + 1) * quarter] = moved[
                    :, i * quarter : (i + 1) * quarter
                ]


def arrange(starts, order, homes, widths, normed):
    rows = normed.shape[0]
    shapes = [jax.ShapeDtypeStruct((rows, width), bf16) for width in widths for _ in range(2)]
    return pl.pallas_call(
        functools.partial(arrange_kernel, starts, order, homes),
        in_specs=[VMEM],
        out_specs=[VMEM] * len(shapes),
        out_shape=shapes,
        compiler_params=params(),
        cost_estimate=pl.CostEstimate(
            flops=8 * rows * normed.shape[1] * TILE, bytes_accessed=4 * rows * normed.shape[1],
            transcendentals=0,
        ),
        name="arrange",
    )(normed)


def load(sources, pieces, weights, sems):
    started = []
    for source, column in pieces:
        copy = pltpu.make_async_copy(
            sources[source],
            weights.at[:, pl.ds(column, sources[source].shape[1])],
            sems.at[len(started)],
        )
        copy.start()
        started.append(copy)
    return started


def attend_kernel(layout, count, queries_ref, stacked_ref, before_ref, after_ref, *refs):
    sources = refs[:count]
    mixed_ref, attended, weights, blocks, sems, out_sems = refs[count:]
    copies = load(sources, layout(), weights, sems)
    rows = queries_ref.shape[0]
    tiles = rows // TILE
    scale = 1.0 / math.sqrt(HEAD_DIM)
    place = lax.axis_index("frame")
    has_before = (place > 0).astype(f32)
    has_after = (place < lax.axis_size("frame") - 1).astype(f32)
    for head in range(HEADS):
        ks = slice(head * HEAD_DIM, (head + 1) * HEAD_DIM)
        vs = slice(WIDTH + head * HEAD_DIM, WIDTH + (head + 1) * HEAD_DIM)
        for tile in range(tiles):
            query = queries_ref[tile * TILE : (tile + 1) * TILE, ks]
            low, high = tile - REACH, tile + REACH + 1
            weighted = jnp.zeros((TILE, HEAD_DIM), f32)
            mass = jnp.zeros((TILE, 1), f32)
            spans = [(stacked_ref, max(low, 0), min(high, tiles), None)]
            if low < 0:
                spans.append((before_ref, low + REACH, REACH, has_before))
            if high > tiles:
                spans.append((after_ref, 0, high - tiles, has_after))
            for ref, begin, end, flag in spans:
                span = slice(begin * TILE, end * TILE)
                keys, values = ref[span, ks], ref[span, vs]
                raised = jnp.exp(dot_t(query, keys) * scale)
                if flag is not None:
                    raised = raised * flag
                mass = mass + jnp.sum(raised, axis=-1, keepdims=True)
                weighted = weighted + dot(raised.astype(bf16), values)
            attended[tile * TILE : (tile + 1) * TILE, ks] = (weighted / mass).astype(bf16)
    for copy in copies:
        copy.wait()
    number, width = blocks.shape[0], blocks.shape[2]
    copies = []
    for block in range(number):
        columns = slice(block * width, (block + 1) * width)
        blocks[block] = dot(attended[...], weights[:, columns]).astype(bf16)
        copy = pltpu.make_async_copy(
            blocks.at[block], mixed_ref.at[0, :, columns], out_sems.at[block]
        )
        copy.start()
        copies.append(copy)
    for copy in copies:
        copy.wait()


def attend(layout, sources, queries, stacked, before, after, model):
    rows = queries.shape[0]
    width = 4 * TILE if model % (4 * TILE) == 0 else TILE
    return pl.pallas_call(
        functools.partial(attend_kernel, layout, len(sources)),
        in_specs=[VMEM] * 4 + [ANY] * len(sources),
        out_specs=ANY,
        out_shape=jax.ShapeDtypeStruct((1, rows, model), bf16),
        scratch_shapes=[
            pltpu.VMEM((rows, WIDTH), bf16),
            pltpu.VMEM((WIDTH, model), bf16),
            pltpu.VMEM((model // width, rows, width), bf16),
            pltpu.SemaphoreType.DMA((len(layout()),)),
            pltpu.SemaphoreType.DMA((model // width,)),
        ],
        compiler_params=params(),
        cost_estimate=pl.CostEstimate(
            flops=2 * rows * WIDTH * (model + 2 * 5 * TILE),
            bytes_accessed=2 * (rows * model + WIDTH * model),
            transcendentals=rows * HEADS * 5 * TILE,
        ),
        name="attend_and_mix",
    )(queries, stacked, before, after, *sources)


def swap(x, axis, bits):
    return lax.ppermute(x, axis, [(i, i ^ bits) for i in range(lax.axis_size(axis))])


def swap_plane(x, turn):
    places = lax.axis_size("frame")
    pairs = []
    for i in range(lax.axis_size("fsdp")):
        for j in range(places):
            pairs.append((i * places + j, i * places + (j ^ (1 + (i + turn) % 2))))
    return lax.ppermute(x, ("fsdp", "frame"), pairs)


def hop_order(chips):
    odd = [k for k in range(chips - 1, 0, -1) if k % 2]
    return odd + [k for k in range(2, chips, 2)]


def split_plan(frames, modulation, w_qkv, w_out, qk_gain):
    chips = lax.axis_size("fsdp") // 2
    shard_rows, columns = w_qkv.shape
    shard_columns = w_out.shape[1]
    quarter = shard_rows // 4
    hops = hop_order(chips)
    odd, even = [k for k in hops if k % 2], [k for k in hops if k % 2 == 0]
    far = [k for k in hops if k != 1]
    ring = [1] + far
    fence = lax.optimization_barrier

    def where():
        place, index = lax.axis_index("frame"), lax.axis_index("fsdp")
        high = (place >> 1) & 1
        return index // 2, index % 2, 2 * ((place & 1) ^ high) + high

    def order(core):
        spot = where()[2]
        return spot, spot ^ (2 + core), spot ^ (3 - core), spot ^ 1

    def shard_places():
        chip, core, _ = where()
        cores = (core, 1 - core)
        return [[((chip ^ k) * 2 + c) * shard_rows for k in ring] for c in cores], cores

    def own_places():
        chip, core, _ = where()
        return [pl.multiple_of((2 * chip + c) * shard_rows, TILE) for c in (core, 1 - core)]

    def out_layout():
        chip, core, _ = where()
        place = 2 * chip + core
        pieces = []
        for slot, k in enumerate([0] + hops):
            for source, here in ((2 * slot, 2 * k), (2 * slot + 1, 2 * k + 1)):
                pieces.append((source, pl.multiple_of((place ^ here) * shard_columns, TILE)))
        return pieces

    spot = where()[2]
    part = lax.dynamic_slice_in_dim(w_qkv, spot * quarter, quarter, 0)
    come = {k: swap(part, "fsdp", 2 * k) for k in odd}
    other_qkv = swap(w_qkv, "fsdp", 1)
    other_out = swap(w_out, "fsdp", 1)
    normed = norm_rows(frames, modulation)
    normed, *got = fence((normed, *[come[k] for k in odd if k != 1]))
    come.update(zip([k for k in odd if k != 1], got))

    for k in even:
        come[k] = swap(come[k + 1], "fsdp", 2)
    total = project(
        [(normed, w_qkv), (normed, other_qkv)], qk_gain, (0, columns), "project_own", own_places
    )
    rest_part = lax.dynamic_slice_in_dim(w_qkv, (spot ^ 1) * quarter, quarter, 0)
    total, rest_part, *got = fence((total, rest_part, *[come[k] for k in [1] + even]))
    come.update(zip([1] + even, got))

    count = len(ring)
    first = jnp.concatenate([come[k] for k in ring], axis=0)
    first_rest = swap_plane(first, 0)
    across = swap(rest_part, "fsdp", 2)
    first_other = swap(first, "fsdp", 1)
    homes = [
        [(0, slot), (1, slot), (2, slot), (2, count + slot - 1) if slot else (3, 0)]
        for slot in range(count)
    ]
    widths = [count * quarter, count * quarter, (2 * count - 1) * quarter, quarter]
    arranged = arrange(shard_places, order, homes, widths, normed)
    first, first_rest, across, first_other, arranged = fence(
        (first, first_rest, across, first_other, arranged)
    )

    second = jnp.concatenate([first, first_rest[quarter:]], axis=0)
    second_rest = swap_plane(second, 1)
    outs = {k: swap(w_out, "fsdp", 2 * k) for k in odd}
    first_rest_other = swap(first_rest, "fsdp", 1)
    across_other = swap(across, "fsdp", 1)
    pieces = [first, first_other, first_rest, first_rest_other, across, across_other]
    lefts = [arranged[i] for i in (0, 1, 2, 3, 6, 7)]
    total = project(list(zip(lefts, pieces)), qk_gain, (0, columns), "project_mid", total=total)
    total, second_rest, *got = fence((total, second_rest, *[outs[k] for k in odd]))
    outs.update(zip(odd, got))

    second_rest_other = swap(second_rest, "fsdp", 1)
    last = [(arranged[4], second_rest), (arranged[5], second_rest_other)]
    stacked = project(
        last, qk_gain, (WIDTH, 2 * WIDTH), "project_keys_values", kinds=(1, None), total=total
    )
    queries = project(last, qk_gain, (0, WIDTH), "project_queries", kinds=(0,), total=total)
    for k in even:
        outs[k] = swap(outs[k + 1], "fsdp", 2)
    sources = [w_out, other_out]
    for k in hops:
        sources += [outs[k], swap(outs[k], "fsdp", 1)]
    return queries, stacked, out_layout, sources


def whole_plan(frames, modulation, w_qkv, w_out, qk_gain):
    rows = lax.all_gather(w_qkv, "fsdp", axis=0, tiled=True)
    columns = lax.all_gather(w_out, "fsdp", axis=1, tiled=True)
    normed = norm_rows(frames, modulation)
    stacked = project(
        [(normed, rows)], qk_gain, (WIDTH, 2 * WIDTH), "project_keys_values", kinds=(1, None)
    )
    queries = project([(normed, rows)], qk_gain, (0, WIDTH), "project_queries", kinds=(0,))
    return queries, stacked, lambda: [(0, 0)], [columns]


def on_device(frames, modulation, w_qkv, qk_gain, w_out):
    devices, places = lax.axis_size("fsdp"), lax.axis_size("frame")
    chips = devices // 2
    split = (
        devices % 2 == 0
        and chips > 1
        and chips & (chips - 1) == 0
        and places % 4 == 0
        and w_qkv.shape[0] % TILE == 0
        and w_out.shape[1] % TILE == 0
    )
    plan = split_plan if split else whole_plan
    queries, stacked, layout, sources = plan(frames[0], modulation[0], w_qkv, w_out, qk_gain)
    ends = places - 1
    before = lax.ppermute(stacked[-BORDER:], "frame", [(i, i + 1) for i in range(ends)])
    behind = lax.ppermute(stacked[:BORDER], "frame", [(i + 1, i) for i in range(ends)])
    return attend(layout, sources, queries, stacked, before, behind, frames.shape[2])


def solution(mesh):
    return jax.shard_map(
        on_device,
        mesh=mesh,
        in_specs=(
            P("fsdp", "frame", None),
            P("fsdp", None, None),
            P("fsdp", None),
            P(),
            P(None, "fsdp"),
        ),
        out_specs=P("fsdp", "frame", None),
        check_vma=False,
    )
```

time: 76.7 us -> 63.5 us (0.83)
  waiting for transfers between devices: 38.3 us -> 26.4 us
  starting transfers between devices: 27.6 us -> 21.6 us
  Pallas kernels: 9.22 us -> 11.6 us
  local copies, waits for them, and re-layouts: 1.22 us -> 3.51 us
    ppermute x20 -> x16, waiting for transfers between devices: 27.4 us -> 16.8 us  [swap(): lax.ppermute(x, axis, [(i, i ^ bits) for i in range(lax.axis_size(axis))])]
    ppermute x20 -> x16, starting transfers between devices: 24 us -> 13.7 us  [swap(): lax.ppermute(x, axis, [(i, i ^ bits) for i in range(lax.axis_size(axis))])]
    ppermute x0 -> x2, starting transfers between devices: none -> 3.14 us  [swap_plane(): return lax.ppermute(x, ('fsdp', 'frame'), pairs)]
    pallas_call x3 -> x7, Pallas kernels: 9.22 us -> 11.6 us  [the longest x4 3.56 us: project(): pl.pallas_call(functools.partial(project_kernel, len(pairs), starts, kind...]
    unnamed x16 -> x12, local copies, waits for them, and re-layouts: 0.11 us -> 2.44 us
    ppermute x1, waiting for transfers between devices: 8.76 us -> 6.55 us  [on_device(): lax.ppermute(stacked[:BORDER], 'frame', [(i + 1, i) for i in range(ends)])]
    ppermute x1, starting transfers between devices: 2.22 us -> 3.41 us  [on_device(): lax.ppermute(stacked[-BORDER:], 'frame', [(i, i + 1) for i in range(ends)])]
  transfers between devices with their start and end apart: 22 -> 20, of which waited for: 12 -> 11; matrix products, arithmetic and copies ran while one was open for 0% -> 2% of each run, Pallas kernels for 8% -> 13%
where the time goes in v2:
time: 63.5 us; the launch traced here: 63.3 us
  waiting for transfers between devices  26.4 us (42%)
  starting transfers between devices  21.6 us (34%)
  Pallas kernels  11.6 us (18%)
  local copies, waits for them, and re-layouts  3.51 us (6%)
    ppermute x16, waiting for transfers between devices, swap(): lax.ppermute(x, axis, [(i, i ^ bits) for i in range(lax.axis_size(axis))])  16.8 us
    ppermute x16, starting transfers between devices, swap(): lax.ppermute(x, axis, [(i, i ^ bits) for i in range(lax.axis_size(axis))])  13.7 us
    ppermute x1, waiting for transfers between devices, on_device(): lax.ppermute(stacked[:BORDER], 'frame', [(i + 1, i) for i in range(ends)])  6.55 us
    pallas_call x4, Pallas kernels, project(): pl.pallas_call(functools.partial(project_kernel, len(pairs), starts, kind...  3.56 us
    pallas_call x1, Pallas kernels, attend(): pl.pallas_call(functools.partial(attend_kernel, layout, len(sources)), in...  3.44 us
    ppermute x1, starting transfers between devices, on_device(): lax.ppermute(stacked[-BORDER:], 'frame', [(i, i + 1) for i in range(ends)])  3.41 us
    pallas_call x1, Pallas kernels, norm_rows(): pl.pallas_call(norm_kernel, in_specs=[ANY, ANY], out_specs=VMEM, out_shap...  3.18 us
    ppermute x2, starting transfers between devices, swap_plane(): return lax.ppermute(x, ('fsdp', 'frame'), pairs)  3.14 us
  transfers between devices with their start and end apart: 20, of which 11 were waited for; matrix products, arithmetic and copies ran while one was open for 2% of the time, Pallas kernels for 13%

profile of v2, /device:TPU:0, one launch (start us, length us, event | category | flops | bytes accessed | tf_op | source)
XLA Modules:
  0.0 63.3 jit_solution(10928396397277865971)
XLA Ops:
  0.5 1.0 %constant_dynamic-slice_fusion = (bf16[96,768]{1,0:T(8,128)(2,1)S(1)}, bf16[96,768]{1,0:T(8,128)(2,1)S(1)}) fusion(bf16[384,768]{1,0:T(8,128)(2,1)} %refs_2_.1, s32[]{:T(128)S(6)} %select_n.7, s32[]{:T(128)S(6)} %select_n.6), kind=kLoop, calls=%fused_computation.4 | loop fusion | bytes 589832 | tf_op jit(solution)/shard_map/dynamic_slice | solution.py:324
  1.5 4.7 %collective-permute-start = (bf16[96,768]{1,0:T(8,128)(2,1)S(1)}, bf16[96,768]{1,0:T(8,128)(2,1)S(1)}, u32[]{:S(2)}, u32[]{:S(2)}) collective-permute-start(bf16[96,768]{1,0:T(8,128)(2,1)S(1)} %get-tuple-element.66), channel_id=1, source_target_pairs={{0,24},{4,28},{8,16},{12,20},{16,8},{20,12},{24,0},{28,4},{1,25},{... | collective-permute-start | bytes 442376 | tf_op jit(solution)/shard_map/ppermute | solution.py:255
  6.1 1.7 %copy-done = bf16[1,384,3072]{2,1,0:T(8,128)(2,1)S(1)} copy-done((bf16[1,384,3072]{2,1,0:T(8,128)(2,1)S(1)}, bf16[1,384,3072]{2,1,0:T(8,128)(2,1)}, u32[]{:S(2)}) %copy-start) | copy-done | bytes 2359320
  7.8 0.7 %copy-done.3 = f32[1,2,3072]{2,1,0:T(2,128)S(1)} copy-done((f32[1,2,3072]{2,1,0:T(2,128)S(1)}, f32[1,2,3072]{2,1,0:T(2,128)}, u32[]{:S(2)}) %copy-start.3) | copy-done | bytes 24600
  8.5 3.2 %layer_norm.1.refs_0_.refs_1_.normed_ref = bf16[384,3072]{1,0:T(8,128)(2,1)S(1)} custom-call(bf16[384,3072]{1,0:T(8,128)(2,1)S(1)} %bitcast.2, f32[2,3072]{1,0:T(2,128)S(1)} %bitcast.3), custom_call_target="tpu_custom_call" | custom-call | flops 11796480 | bytes 4718592 | tf_op jit(solution)/shard_map/layer_norm/pallas_call | solution.py:63
  11.7 2.1 %collective-permute-start.3 = (bf16[96,768]{1,0:T(8,128)(2,1)S(1)}, bf16[96,768]{1,0:T(8,128)(2,1)S(1)}, u32[]{:S(2)}, u32[]{:S(2)}) collective-permute-start(bf16[96,768]{1,0:T(8,128)(2,1)S(1)} %collective-permute-done), channel_id=1, source_target_pairs={{0,8},{4,12},{8,0},{12,4},{16,24},{20,28},{24,16},{28,20},{1,9},{5... | collective-permute-start | bytes 442376 | tf_op jit(solution)/shard_map/ppermute | solution.py:255
  13.8 0.8 %project_own.1.refs_12_ = f32[384,768]{1,0:T(8,128)S(1)} custom-call(f32[2,128]{1,0:T(2,128)S(1)} %copy-done.4, bf16[384,3072]{1,0:T(8,128)(2,1)S(1)} %layer_norm.1.refs_0_.refs_1_.normed_ref, bf16[384,3072]{1,0:T(8,128)(2,1)S(1)} %layer_norm.1.refs_0_.refs_1_.normed_ref, bf16[384,768]{1,0:T(8,128)(2,1)S(1)} %copy-done.1, ...), custom_call_target="tpu_custom_call" | custom-call | flops 452984832 | bytes 1769472 | tf_op jit(solution)/shard_map/project_own/pallas_call | solution.py:114
  14.6 3.2 %collective-permute-done.3 = bf16[96,768]{1,0:T(8,128)(2,1)S(1)} collective-permute-done((bf16[96,768]{1,0:T(8,128)(2,1)S(1)}, bf16[96,768]{1,0:T(8,128)(2,1)S(1)}, u32[]{:S(2)}, u32[]{:S(2)}) %collective-permute-start.3) | collective-permute-done | bytes 147488 | tf_op jit(solution)/shard_map/ppermute | solution.py:255
  17.8 1.6 %collective-permute-start.4 = (bf16[288,768]{1,0:T(8,128)(2,1)S(1)}, bf16[288,768]{1,0:T(8,128)(2,1)S(1)}, u32[]{:S(2)}, u32[]{:S(2)}) collective-permute-start(bf16[288,768]{1,0:T(8,128)(2,1)S(1)} %constant_dynamic-update-slice_fusion.refs_6_), channel_id=1, source_target_pairs={{0,1},{1,0},{2,3},{3,2},{4,6},{5,7},{6,4},{7,5},{8,9},{9,8},{10,11... | collective-permute-start | bytes 1327112 | tf_op jit(solution)/shard_map/ppermute | solution.py:264
  19.4 1.7 %collective-permute-start.5 = (bf16[96,768]{1,0:T(8,128)(2,1)S(1)}, bf16[96,768]{1,0:T(8,128)(2,1)S(1)}, u32[]{:S(2)}, u32[]{:S(2)}) collective-permute-start(bf16[96,768]{1,0:T(8,128)(2,1)S(1)} %get-tuple-element.39), channel_id=1, source_target_pairs={{0,8},{4,12},{8,0},{12,4},{16,24},{20,28},{24,16},{28,20},{1,9},{5... | collective-permute-start | bytes 442376 | tf_op jit(solution)/shard_map/ppermute | solution.py:255
  21.1 1.4 %arrange.1 = (bf16[384,288]{1,0:T(8,128)(2,1)S(1)}, bf16[384,288]{1,0:T(8,128)(2,1)S(1)}, bf16[384,288]{1,0:T(8,128)(2,1)S(1)}, bf16[384,288]{1,0:T(8,128)(2,1)S...) custom-call(bf16[384,3072]{1,0:T(8,128)(2,1)S(1)} %layer_norm.1.refs, ...), custom_call_target="tpu_custom_call" | custom-call | flops 1207959552 | bytes 4718592 | tf_op jit(solution)/shard_map/arrange/pallas_call | solution.py:154
  22.6 3.1 %collective-permute-done.5.refs_10_ = bf16[96,768]{1,0:T(8,128)(2,1)S(1)} collective-permute-done((bf16[96,768]{1,0:T(8,128)(2,1)S(1)}, bf16[96,768]{1,0:T(8,128)(2,1)S(1)}, u32[]{:S(2)}, u32[]{:S(2)}) %collective-permute-start.5) | collective-permute-done | bytes 147488 | tf_op jit(solution)/shard_map/ppermute | solution.py:255
  26.3 1.6 %collective-permute-start.9 = (bf16[480,768]{1,0:T(8,128)(2,1)S(1)}, bf16[480,768]{1,0:T(8,128)(2,1)S(1)}, u32[]{:S(2)}, u32[]{:S(2)}) collective-permute-start(bf16[480,768]{1,0:T(8,128)(2,1)S(1)} %pad_maximum_fusion), channel_id=1, source_target_pairs={{0,2},{1,3},{2,0},{3,1},{4,5},{5,4},{6,7},{7,6},{8,10},{9,11},{10,... | collective-permute-start | bytes 2211848 | tf_op jit(solution)/shard_map/ppermute | solution.py:264
  28.4 2.0 %collective-permute-start.10 = (bf16[256,384]{1,0:T(8,128)(2,1)S(1)}, bf16[256,384]{1,0:T(8,128)(2,1)S(1)}, u32[]{:S(2)}, u32[]{:S(2)}) collective-permute-start(bf16[256,384]{1,0:T(8,128)(2,1)S(1)} %copy-done.2), channel_id=1, source_target_pairs={{0,24},{4,28},{8,16},{12,20},{16,8},{20,12},{24,0},{28,4},{1,25},{... | collective-permute-start | bytes 589832 | tf_op jit(solution)/shard_map/ppermute | solution.py:255
  30.4 0.8 %collective-permute-start.11 = (bf16[256,384]{1,0:T(8,128)(2,1)S(1)}, bf16[256,384]{1,0:T(8,128)(2,1)S(1)}, u32[]{:S(2)}, u32[]{:S(2)}) collective-permute-start(bf16[256,384]{1,0:T(8,128)(2,1)S(1)} %copy-done.2), channel_id=1, source_target_pairs={{0,8},{4,12},{8,0},{12,4},{16,24},{20,28},{24,16},{28,20},{1,9},{5... | collective-permute-start | bytes 589832 | tf_op jit(solution)/shard_map/ppermute | solution.py:255
  31.2 1.7 %project_mid.1.refs_4_ = f32[384,768]{1,0:T(8,128)S(1)} custom-call(f32[2,128]{1,0:T(2,128)S(1)} %copy-done.4, bf16[384,288]{1,0:T(8,128)(2,1)S(1)} %get-tuple-element.50.refs_0_, bf16[384,288]{1,0:T(8,128)(2,1)S(1)} %get-tuple-element.51.refs_1_, bf16[384,288]{1,0:T(8,128)(2,1)S(1)} %get-tuple-element.52.refs_2_, ...), custom_call_target="tpu_custom_call" | custom-call | flops 792723456 | bytes 3096576 | tf_op jit(solution)/shard_map/project_mid/pallas_call | solution.py:114
  32.9 5.1 %collective-permute-done.10.refs_2_ = bf16[256,384]{1,0:T(8,128)(2,1)S(1)} collective-permute-done((bf16[256,384]{1,0:T(8,128)(2,1)S(1)}, bf16[256,384]{1,0:T(8,128)(2,1)S(1)}, u32[]{:S(2)}, u32[]{:S(2)}) %collective-permute-start.10) | collective-permute-done | bytes 196640 | tf_op jit(solution)/shard_map/ppermute | solution.py:255
  38.0 3.1 %collective-permute-done.11.refs_4_ = bf16[256,384]{1,0:T(8,128)(2,1)S(1)} collective-permute-done((bf16[256,384]{1,0:T(8,128)(2,1)S(1)}, bf16[256,384]{1,0:T(8,128)(2,1)S(1)}, u32[]{:S(2)}, u32[]{:S(2)}) %collective-permute-start.11) | collective-permute-done | bytes 196640 | tf_op jit(solution)/shard_map/ppermute | solution.py:255
  41.9 1.4 %collective-permute-done.12.refs_3_ = bf16[480,768]{1,0:T(8,128)(2,1)S(1)} collective-permute-done((bf16[480,768]{1,0:T(8,128)(2,1)S(1)}, bf16[480,768]{1,0:T(8,128)(2,1)S(1)}, u32[]{:S(2)}, u32[]{:S(2)}) %collective-permute-start.12) | collective-permute-done | bytes 737312 | tf_op jit(solution)/shard_map/ppermute | solution.py:255
  44.0 3.4 %collective-permute-start.13 = (bf16[256,512]{1,0:T(8,128)(2,1)S(1)}, bf16[256,512]{1,0:T(8,128)(2,1)S(1)}, u32[]{:S(2)}, u32[]{:S(2)}) collective-permute-start(bf16[256,512]{1,0:T(8,128)(2,1)S(1)} %get-tuple-element.68), channel_id=1, source_target_pairs={{0,1},{1,2},{2,3},{4,5},{5,6},{6,7},{8,9},{9,10},{10,11},{12,13},{... | collective-permute-start | bytes 786440 | tf_op jit(solution)/shard_map/ppermute | solution.py:393
  47.5 1.3 %collective-permute-start.14 = (bf16[256,512]{1,0:T(8,128)(2,1)S(1)}, bf16[256,512]{1,0:T(8,128)(2,1)S(1)}, u32[]{:S(2)}, u32[]{:S(2)}) collective-permute-start(bf16[256,512]{1,0:T(8,128)(2,1)S(1)} %get-tuple-element.67), channel_id=1, source_target_pairs={{1,0},{2,1},{3,2},{5,4},{6,5},{7,6},{9,8},{10,9},{11,10},{13,12},{... | collective-permute-start | bytes 786440 | tf_op jit(solution)/shard_map/ppermute | solution.py:394
  50.8 2.5 %collective-permute-done.13.before_ref = bf16[256,512]{1,0:T(8,128)(2,1)S(1)} collective-permute-done((bf16[256,512]{1,0:T(8,128)(2,1)S(1)}, bf16[256,512]{1,0:T(8,128)(2,1)S(1)}, u32[]{:S(2)}, u32[]{:S(2)}) %collective-permute-start.13) | collective-permute-done | bytes 262176 | tf_op jit(solution)/shard_map/ppermute | solution.py:393
  53.3 6.5 %collective-permute-done.14.after_ref = bf16[256,512]{1,0:T(8,128)(2,1)S(1)} collective-permute-done((bf16[256,512]{1,0:T(8,128)(2,1)S(1)}, bf16[256,512]{1,0:T(8,128)(2,1)S(1)}, u32[]{:S(2)}, u32[]{:S(2)}) %collective-permute-start.14) | collective-permute-done | bytes 262176 | tf_op jit(solution)/shard_map/ppermute | solution.py:394
  59.8 3.4 %attend_and_mix.1 = bf16[1,384,3072]{2,1,0:T(8,128)(2,1)} custom-call(bf16[384,256]{1,0:T(8,128)(2,1)S(1)} %project_queries.1.queries_ref, bf16[384,512]{1,0:T(8,128)(2,1)S(1)} %project_keys_values.1.stacked_ref, bf16[256,512]{1,0:T(8,128)(2,1)S(1)} %collective-permute-done.13.before_ref, bf16[256,512]{1,0:T(8,128)(2,1)S(1)} %collective-permute-done.14.after_ref, ...), custom_call_target="tpu_custom_call" | custom-call | flops 855638016 | bytes 3932160 | tf_op jit(solution)/shard_map/attend_and_mix/pallas_call | solution.py:232
  (40 shorter events, 5.2 us)
Async XLA Ops:
  0.0 13.8 %collective-permute-start.1 = (bf16[384,768]{1,0:T(8,128)(2,1)}, bf16[384,768]{1,0:T(8,128)(2,1)S(1)}, u32[]{:S(2)}, u32[]{:S(2)}) collective-permute-start(bf16[384,768]{1,0:T(8,128)(2,1)} %refs_2_.1), channel_id=1, source_target_pairs={{0,4},{4,0},{8,12},{12,8},{16,20},{20,16},{24,28},{28,24},{1,5},{5... | collective-permute-start | bytes 1769480 | tf_op jit(solution)/shard_map/ppermute | solution.py:255
  1.5 10.3 %collective-permute-start = (bf16[96,768]{1,0:T(8,128)(2,1)S(1)}, bf16[96,768]{1,0:T(8,128)(2,1)S(1)}, u32[]{:S(2)}, u32[]{:S(2)}) collective-permute-start(bf16[96,768]{1,0:T(8,128)(2,1)S(1)} %get-tuple-element.66), channel_id=1, source_target_pairs={{0,24},{4,28},{8,16},{12,20},{16,8},{20,12},{24,0},{28,4},{1,25},{... | collective-permute-start | bytes 442376 | tf_op jit(solution)/shard_map/ppermute | solution.py:255
  6.1 8.5 %collective-permute-start.2 = (bf16[96,768]{1,0:T(8,128)(2,1)S(1)}, bf16[96,768]{1,0:T(8,128)(2,1)S(1)}, u32[]{:S(2)}, u32[]{:S(2)}) collective-permute-start(bf16[96,768]{1,0:T(8,128)(2,1)S(1)} %get-tuple-element.66), channel_id=1, source_target_pairs={{0,8},{4,12},{8,0},{12,4},{16,24},{20,28},{24,16},{28,20},{1,9},{5... | collective-permute-start | bytes 442376 | tf_op jit(solution)/shard_map/ppermute | solution.py:255
  6.1 1.7 %copy-start = (bf16[1,384,3072]{2,1,0:T(8,128)(2,1)S(1)}, bf16[1,384,3072]{2,1,0:T(8,128)(2,1)}, u32[]{:S(2)}) copy-start(bf16[1,384,3072]{2,1,0:T(8,128)(2,1)} %param.5) | copy-start | bytes 7077892
  8.5 5.3 %copy-start.1 = (bf16[384,768]{1,0:T(8,128)(2,1)S(1)}, bf16[384,768]{1,0:T(8,128)(2,1)}, u32[]{:S(2)}) copy-start(bf16[384,768]{1,0:T(8,128)(2,1)} %refs_2_.1) | copy-start | bytes 1769476
  8.5 5.3 %copy-start.4 = (f32[2,128]{1,0:T(2,128)S(1)}, f32[2,128]{1,0:T(2,128)}, u32[]{:S(2)}) copy-start(f32[2,128]{1,0:T(2,128)} %gain_ref.7) | copy-start | bytes 3076
  11.7 6.0 %collective-permute-start.3 = (bf16[96,768]{1,0:T(8,128)(2,1)S(1)}, bf16[96,768]{1,0:T(8,128)(2,1)S(1)}, u32[]{:S(2)}, u32[]{:S(2)}) collective-permute-start(bf16[96,768]{1,0:T(8,128)(2,1)S(1)} %collective-permute-done), channel_id=1, source_target_pairs={{0,8},{4,12},{8,0},{12,4},{16,24},{20,28},{24,16},{28,20},{1,9},{5... | collective-permute-start | bytes 442376 | tf_op jit(solution)/shard_map/ppermute | solution.py:255
  17.8 8.4 %collective-permute-start.4 = (bf16[288,768]{1,0:T(8,128)(2,1)S(1)}, bf16[288,768]{1,0:T(8,128)(2,1)S(1)}, u32[]{:S(2)}, u32[]{:S(2)}) collective-permute-start(bf16[288,768]{1,0:T(8,128)(2,1)S(1)} %constant_dynamic-update-slice_fusion.refs_6_), channel_id=1, source_target_pairs={{0,1},{1,0},{2,3},{3,2},{4,6},{5,7},{6,4},{7,5},{8,9},{9,8},{10,11... | collective-permute-start | bytes 1327112 | tf_op jit(solution)/shard_map/ppermute | solution.py:264
  19.4 6.8 %collective-permute-start.6 = (bf16[288,768]{1,0:T(8,128)(2,1)S(1)}, bf16[288,768]{1,0:T(8,128)(2,1)S(1)}, u32[]{:S(2)}, u32[]{:S(2)}) collective-permute-start(bf16[288,768]{1,0:T(8,128)(2,1)S(1)} %constant_dynamic-update-slice_fusion.refs_6_), channel_id=1, source_target_pairs={{0,4},{4,0},{8,12},{12,8},{16,20},{20,16},{24,28},{28,24},{1,5},{5... | collective-permute-start | bytes 1327112 | tf_op jit(solution)/shard_map/ppermute | solution.py:255
  19.4 6.3 %collective-permute-start.5 = (bf16[96,768]{1,0:T(8,128)(2,1)S(1)}, bf16[96,768]{1,0:T(8,128)(2,1)S(1)}, u32[]{:S(2)}, u32[]{:S(2)}) collective-permute-start(bf16[96,768]{1,0:T(8,128)(2,1)S(1)} %get-tuple-element.39), channel_id=1, source_target_pairs={{0,8},{4,12},{8,0},{12,4},{16,24},{20,28},{24,16},{28,20},{1,9},{5... | collective-permute-start | bytes 442376 | tf_op jit(solution)/shard_map/ppermute | solution.py:255
  22.6 5.8 %copy-start.2 = (bf16[256,384]{1,0:T(8,128)(2,1)S(1)}, bf16[256,384]{1,0:T(8,128)(2,1)}, u32[]{:S(2)}) copy-start(bf16[256,384]{1,0:T(8,128)(2,1)} %refs_0_.1) | copy-start | bytes 589828
  26.3 14.8 %collective-permute-start.9 = (bf16[480,768]{1,0:T(8,128)(2,1)S(1)}, bf16[480,768]{1,0:T(8,128)(2,1)S(1)}, u32[]{:S(2)}, u32[]{:S(2)}) collective-permute-start(bf16[480,768]{1,0:T(8,128)(2,1)S(1)} %pad_maximum_fusion), channel_id=1, source_target_pairs={{0,2},{1,3},{2,0},{3,1},{4,5},{5,4},{6,7},{7,6},{8,10},{9,11},{10,... | collective-permute-start | bytes 2211848 | tf_op jit(solution)/shard_map/ppermute | solution.py:264
  27.9 3.3 %collective-permute-start.7 = (bf16[288,768]{1,0:T(8,128)(2,1)S(1)}, bf16[288,768]{1,0:T(8,128)(2,1)S(1)}, u32[]{:S(2)}, u32[]{:S(2)}) collective-permute-start(bf16[288,768]{1,0:T(8,128)(2,1)S(1)} %collective-permute-done.4.refs_8_), channel_id=1, source_target_pairs={{0,4},{4,0},{8,12},{12,8},{16,20},{20,16},{24,28},{28,24},{1,5},{5... | collective-permute-start | bytes 1327112 | tf_op jit(solution)/shard_map/ppermute | solution.py:255
  27.9 3.3 %collective-permute-start.8 = (bf16[96,768]{1,0:T(8,128)(2,1)S(1)}, bf16[96,768]{1,0:T(8,128)(2,1)S(1)}, u32[]{:S(2)}, u32[]{:S(2)}) collective-permute-start(bf16[96,768]{1,0:T(8,128)(2,1)S(1)} %collective-permute-done.5.refs_10_), channel_id=1, source_target_pairs={{0,4},{4,0},{8,12},{12,8},{16,20},{20,16},{24,28},{28,24},{1,5},{5... | collective-permute-start | bytes 442376 | tf_op jit(solution)/shard_map/ppermute | solution.py:255
  28.4 9.6 %collective-permute-start.10 = (bf16[256,384]{1,0:T(8,128)(2,1)S(1)}, bf16[256,384]{1,0:T(8,128)(2,1)S(1)}, u32[]{:S(2)}, u32[]{:S(2)}) collective-permute-start(bf16[256,384]{1,0:T(8,128)(2,1)S(1)} %copy-done.2), channel_id=1, source_target_pairs={{0,24},{4,28},{8,16},{12,20},{16,8},{20,12},{24,0},{28,4},{1,25},{... | collective-permute-start | bytes 589832 | tf_op jit(solution)/shard_map/ppermute | solution.py:255
  30.4 10.7 %collective-permute-start.11 = (bf16[256,384]{1,0:T(8,128)(2,1)S(1)}, bf16[256,384]{1,0:T(8,128)(2,1)S(1)}, u32[]{:S(2)}, u32[]{:S(2)}) collective-permute-start(bf16[256,384]{1,0:T(8,128)(2,1)S(1)} %copy-done.2), channel_id=1, source_target_pairs={{0,8},{4,12},{8,0},{12,4},{16,24},{20,28},{24,16},{28,20},{1,9},{5... | collective-permute-start | bytes 589832 | tf_op jit(solution)/shard_map/ppermute | solution.py:255
  41.1 2.2 %collective-permute-start.12 = (bf16[480,768]{1,0:T(8,128)(2,1)S(1)}, bf16[480,768]{1,0:T(8,128)(2,1)S(1)}, u32[]{:S(2)}, u32[]{:S(2)}) collective-permute-start(bf16[480,768]{1,0:T(8,128)(2,1)S(1)} %collective-permute-done.9.refs_2_), channel_id=1, source_target_pairs={{0,4},{4,0},{8,12},{12,8},{16,20},{20,16},{24,28},{28,24},{1,5},{5... | collective-permute-start | bytes 2211848 | tf_op jit(solution)/shard_map/ppermute | solution.py:255
  41.1 7.7 %collective-permute-start.15 = (bf16[256,384]{1,0:T(8,128)(2,1)S(1)}, bf16[256,384]{1,0:T(8,128)(2,1)S(1)}, u32[]{:S(2)}, u32[]{:S(2)}) collective-permute-start(bf16[256,384]{1,0:T(8,128)(2,1)S(1)} %copy-done.2), channel_id=1, source_target_pairs={{0,4},{4,0},{8,12},{12,8},{16,20},{20,16},{24,28},{28,24},{1,5},{5... | collective-permute-start | bytes 589832 | tf_op jit(solution)/shard_map/ppermute | solution.py:255
  41.6 7.7 %collective-permute-start.18 = (bf16[256,384]{1,0:T(8,128)(2,1)S(1)}, bf16[256,384]{1,0:T(8,128)(2,1)S(1)}, u32[]{:S(2)}, u32[]{:S(2)}) collective-permute-start(bf16[256,384]{1,0:T(8,128)(2,1)S(1)} %collective-permute-done.10.refs_2_), channel_id=1, source_target_pairs={{0,8},{4,12},{8,0},{12,4},{16,24},{20,28},{24,16},{28,20},{1,9},{5... | collective-permute-start | bytes 589832 | tf_op jit(solution)/shard_map/ppermute | solution.py:255
  44.0 9.3 %collective-permute-start.13 = (bf16[256,512]{1,0:T(8,128)(2,1)S(1)}, bf16[256,512]{1,0:T(8,128)(2,1)S(1)}, u32[]{:S(2)}, u32[]{:S(2)}) collective-permute-start(bf16[256,512]{1,0:T(8,128)(2,1)S(1)} %get-tuple-element.68), channel_id=1, source_target_pairs={{0,1},{1,2},{2,3},{4,5},{5,6},{6,7},{8,9},{9,10},{10,11},{12,13},{... | collective-permute-start | bytes 786440 | tf_op jit(solution)/shard_map/ppermute | solution.py:393
  47.5 12.4 %collective-permute-start.14 = (bf16[256,512]{1,0:T(8,128)(2,1)S(1)}, bf16[256,512]{1,0:T(8,128)(2,1)S(1)}, u32[]{:S(2)}, u32[]{:S(2)}) collective-permute-start(bf16[256,512]{1,0:T(8,128)(2,1)S(1)} %get-tuple-element.67), channel_id=1, source_target_pairs={{1,0},{2,1},{3,2},{5,4},{6,5},{7,6},{9,8},{10,9},{11,10},{13,12},{... | collective-permute-start | bytes 786440 | tf_op jit(solution)/shard_map/ppermute | solution.py:394
  48.8 1.5 %collective-permute-start.16 = (bf16[256,384]{1,0:T(8,128)(2,1)S(1)}, bf16[256,384]{1,0:T(8,128)(2,1)S(1)}, u32[]{:S(2)}, u32[]{:S(2)}) collective-permute-start(bf16[256,384]{1,0:T(8,128)(2,1)S(1)} %collective-permute-done.10.refs_2_), channel_id=1, source_target_pairs={{0,4},{4,0},{8,12},{12,8},{16,20},{20,16},{24,28},{28,24},{1,5},{5... | collective-permute-start | bytes 589832 | tf_op jit(solution)/shard_map/ppermute | solution.py:255
  48.8 1.7 %collective-permute-start.17 = (bf16[256,384]{1,0:T(8,128)(2,1)S(1)}, bf16[256,384]{1,0:T(8,128)(2,1)S(1)}, u32[]{:S(2)}, u32[]{:S(2)}) collective-permute-start(bf16[256,384]{1,0:T(8,128)(2,1)S(1)} %collective-permute-done.11.refs_4_), channel_id=1, source_target_pairs={{0,4},{4,0},{8,12},{12,8},{16,20},{20,16},{24,28},{28,24},{1,5},{5... | collective-permute-start | bytes 589832 | tf_op jit(solution)/shard_map/ppermute | solution.py:255
  49.3 1.5 %collective-permute-start.19 = (bf16[256,384]{1,0:T(8,128)(2,1)S(1)}, bf16[256,384]{1,0:T(8,128)(2,1)S(1)}, u32[]{:S(2)}, u32[]{:S(2)}) collective-permute-start(bf16[256,384]{1,0:T(8,128)(2,1)S(1)} %collective-permute-done.18.refs_6_), channel_id=1, source_target_pairs={{0,4},{4,0},{8,12},{12,8},{16,20},{20,16},{24,28},{28,24},{1,5},{5... | collective-permute-start | bytes 589832 | tf_op jit(solution)/shard_map/ppermute | solution.py:255
  (1 other events, 0.7 us)

commit v3 on v2

v3 whole, which is shorter than its diff:
```python
import functools
import math

import jax
import jax.numpy as jnp
from jax import lax
from jax.experimental import pallas as pl
from jax.experimental.pallas import tpu as pltpu
from jax.sharding import PartitionSpec as P

HEAD_DIM = 128
HEADS = 2
WIDTH = HEADS * HEAD_DIM
TILE = 128
REACH = 2
BORDER = REACH * TILE
VMEM_BYTES = 40 * 1024 * 1024

f32 = jnp.float32
bf16 = jnp.bfloat16
ANY = pl.BlockSpec(memory_space=pl.ANY)
VMEM = pl.BlockSpec(memory_space=pltpu.VMEM)


def params():
    return pltpu.CompilerParams(vmem_limit_bytes=VMEM_BYTES)


def dot(a, b):
    return jnp.dot(a, b, preferred_element_type=f32)


def dot_t(a, b):
    return lax.dot_general(a, b, (((1,), (1,)), ((), ())), preferred_element_type=f32)


def norm_kernel(frames_ref, modulation_ref, normed_ref):
    values = frames_ref[...].astype(f32)
    average = jnp.mean(values, axis=-1, keepdims=True)
    centered = values - average
    spread = jnp.mean(centered * centered, axis=-1, keepdims=True)
    normed = centered * lax.rsqrt(spread + 1e-06)
    normed_ref[...] = (normed * (1.0 + modulation_ref[0:1]) + modulation_ref[1:2]).astype(bf16)


def norm_rows(frames, modulation):
    rows, width = frames.shape
    block = TILE // 2
    return pl.pallas_call(
        norm_kernel,
        grid=(rows // block,),
        in_specs=[
            pl.BlockSpec((block, width), lambda i: (i, 0)),
            pl.BlockSpec((2, width), lambda i: (0, 0)),
        ],
        out_specs=pl.BlockSpec((block, width), lambda i: (i, 0)),
        out_shape=jax.ShapeDtypeStruct((rows, width), bf16),
        compiler_params=params(),
        cost_estimate=pl.CostEstimate(
            flops=10 * rows * width, bytes_accessed=4 * rows * width, transcendentals=rows
        ),
        name="layer_norm",
    )(frames, modulation)


def head_norm(x, gain_row):
    squares = jnp.mean(x * x, axis=-1, keepdims=True)
    return (x * lax.rsqrt(squares + 1e-06) * gain_row).astype(bf16)


def project_kernel(count, starts, kinds, columns, resumed, gain_ref, *refs):
    lefts, rights = refs[:count], refs[count : 2 * count]
    total_ref, refs = refs[2 * count] if resumed else None, refs[2 * count + resumed :]
    out_ref = refs[0]
    first, number = columns
    total = total_ref[:, first : first + number] if resumed else None
    for i in range(count):
        depth = rights[i].shape[0]
        left = lefts[i][...] if starts is None else lefts[i][:, pl.ds(starts()[i], depth)]
        part = dot(left, rights[i][:, first : first + number])
        total = part if total is None else total + part
    if kinds is None:
        out_ref[...] = total
        return
    for block, kind in enumerate(kinds):
        for head in range(HEADS):
            begin = block * WIDTH + head * HEAD_DIM
            x = total[:, begin : begin + HEAD_DIM]
            out_ref[:, begin : begin + HEAD_DIM] = (
                x.astype(bf16) if kind is None else head_norm(x, gain_ref[kind : kind + 1])
            )


def project(pairs, qk_gain, columns, name, starts=None, kinds=None, total=None):
    lefts, rights = [list(side) for side in zip(*pairs)]
    rows = lefts[0].shape[0]
    depth = sum(right.shape[0] for right in rights)
    resumed = total is not None
    operands = [qk_gain, *lefts, *rights] + [total] * resumed
    return pl.pallas_call(
        functools.partial(project_kernel, len(pairs), starts, kinds, columns, resumed),
        in_specs=[VMEM] * len(operands),
        out_specs=VMEM,
        out_shape=jax.ShapeDtypeStruct((rows, columns[1]), f32 if kinds is None else bf16),
        compiler_params=params(),
        cost_estimate=pl.CostEstimate(
            flops=2 * rows * depth * columns[1],
            bytes_accessed=2 * depth * (rows + columns[1]),
            transcendentals=rows,
        ),
        name=name,
    )(*operands)


def arrange_kernel(starts, order, homes, normed_ref, *out_refs):
    rows = normed_ref.shape[0]
    places, cores = starts()
    depth = normed_ref.shape[1] // lax.axis_size("fsdp")
    quarter = depth // 4
    source = lax.broadcasted_iota(jnp.int32, (depth, depth), 0)
    target = lax.broadcasted_iota(jnp.int32, (depth, depth), 1)
    for here in range(2):
        wanted = target
        for i, number in enumerate(order(cores[here])):
            inside = (target >= i * quarter) & (target < (i + 1) * quarter)
            wanted = jnp.where(inside, target + (number - i) * quarter, wanted)
        chosen = (source == wanted).astype(f32).astype(bf16)
        for slot, place in enumerate(places[here]):
            strip = normed_ref[:, pl.ds(pl.multiple_of(place, TILE), depth)]
            moved = dot(strip, chosen).astype(bf16)
            for i, (out, at) in enumerate(homes[slot]):
                out_refs[2 * out + here][:, at * quarter : (at + 1) * quarter] = moved[
                    :, i * quarter : (i + 1) * quarter
                ]


def arrange(starts, order, homes, widths, normed):
    rows = normed.shape[0]
    shapes = [jax.ShapeDtypeStruct((rows, width), bf16) for width in widths for _ in range(2)]
    return pl.pallas_call(
        functools.partial(arrange_kernel, starts, order, homes),
        in_specs=[VMEM],
        out_specs=[VMEM] * len(shapes),
        out_shape=shapes,
        compiler_params=params(),
        cost_estimate=pl.CostEstimate(
            flops=8 * rows * normed.shape[1] * TILE, bytes_accessed=4 * rows * normed.shape[1],
            transcendentals=0,
        ),
        name="arrange",
    )(normed)


def load(sources, pieces, weights, sems):
    started = []
    for source, row, columns, place in pieces:
        copy = pltpu.make_async_copy(
            sources[source].at[pl.ds(row, weights.shape[0])],
            weights.at[:, pl.ds(pl.multiple_of(place, TILE), columns)],
            sems.at[len(started)],
        )
        copy.start()
        started.append(copy)
    return started


def heads():
    for head in range(HEADS):
        ks = slice(head * HEAD_DIM, (head + 1) * HEAD_DIM)
        yield ks, slice(WIDTH + head * HEAD_DIM, WIDTH + (head + 1) * HEAD_DIM)


def share(query, keys, values, flag=None):
    raised = jnp.exp(dot_t(query, keys) * (1.0 / math.sqrt(HEAD_DIM)))
    if flag is not None:
        raised = raised * flag
    return dot(raised.astype(bf16), values), jnp.sum(raised, axis=-1, keepdims=True)


def attend_own_kernel(queries_ref, stacked_ref, weighted_ref, mass_ref):
    tiles = queries_ref.shape[0] // TILE
    for ks, vs in heads():
        for tile in range(tiles):
            rows = slice(tile * TILE, (tile + 1) * TILE)
            span = slice(max(tile - REACH, 0) * TILE, min(tile + REACH + 1, tiles) * TILE)
            weighted, mass = share(queries_ref[rows, ks], stacked_ref[span, ks], stacked_ref[span, vs])
            weighted_ref[rows, ks] = weighted
            mass_ref[rows, ks] = jnp.broadcast_to(mass, (TILE, HEAD_DIM))


def attend_own(queries, stacked):
    rows = queries.shape[0]
    return pl.pallas_call(
        attend_own_kernel,
        in_specs=[VMEM] * 2,
        out_specs=[VMEM] * 2,
        out_shape=[jax.ShapeDtypeStruct((rows, WIDTH), f32)] * 2,
        compiler_params=params(),
        cost_estimate=pl.CostEstimate(
            flops=4 * rows * rows * WIDTH, bytes_accessed=14 * rows * WIDTH,
            transcendentals=rows * rows * HEADS,
        ),
        name="attend_own_slab",
    )(queries, stacked)


def attend_kernel(layout, count, arrivals, queries_ref, weighted_ref, mass_ref, *refs):
    near_ref, arrived, refs = refs[0], refs[1:arrivals], refs[arrivals:]
    sources = refs[:count]
    mixed_ref, before, behind, attended, weights, blocks, sems, out_sems = refs[count:]
    copies = load(sources, layout(), weights, sems)
    tiles = queries_ref.shape[0] // TILE
    place = lax.axis_index("frame")
    far = arrived[0][...]
    for ref in arrived[1:]:
        far = far + ref[...]
    odd = (place & 1) == 1
    before[...] = jnp.where(odd, near_ref[...], far)
    behind[...] = jnp.where(odd, far, near_ref[...])
    has_before = (place > 0).astype(f32)
    has_behind = (place < lax.axis_size("frame") - 1).astype(f32)
    for ks, vs in heads():
        for tile in range(tiles):
            rows = slice(tile * TILE, (tile + 1) * TILE)
            weighted, mass = weighted_ref[rows, ks], mass_ref[rows, ks]
            low, high = tile - REACH, tile + REACH + 1 - tiles
            spans = []
            if low < 0:
                spans.append((before, slice((low + REACH) * TILE, BORDER), has_before))
            if high > 0:
                spans.append((behind, slice(0, high * TILE), has_behind))
            for ref, span, flag in spans:
                more, extra = share(queries_ref[rows, ks], ref[span, ks], ref[span, vs], flag)
                weighted, mass = weighted + more, mass + extra
            attended[rows, ks] = (weighted / mass).astype(bf16)
    for copy in copies:
        copy.wait()
    number, width = blocks.shape[0], blocks.shape[2]
    copies = []
    for block in range(number):
        columns = slice(block * width, (block + 1) * width)
        blocks[block] = dot(attended[...], weights[:, columns]).astype(bf16)
        copy = pltpu.make_async_copy(
            blocks.at[block], mixed_ref.at[0, :, columns], out_sems.at[block]
        )
        copy.start()
        copies.append(copy)
    for copy in copies:
        copy.wait()


def attend(layout, sources, queries, own, edges, model):
    rows = queries.shape[0]
    width = 4 * TILE if model % (4 * TILE) == 0 else TILE
    return pl.pallas_call(
        functools.partial(attend_kernel, layout, len(sources), len(edges)),
        in_specs=[VMEM] * (3 + len(edges)) + [ANY] * len(sources),
        out_specs=ANY,
        out_shape=jax.ShapeDtypeStruct((1, rows, model), bf16),
        scratch_shapes=[
            pltpu.VMEM((BORDER, 2 * WIDTH), bf16),
            pltpu.VMEM((BORDER, 2 * WIDTH), bf16),
            pltpu.VMEM((rows, WIDTH), bf16),
            pltpu.VMEM((WIDTH, model), bf16),
            pltpu.VMEM((model // width, rows, width), bf16),
            pltpu.SemaphoreType.DMA((len(layout()),)),
            pltpu.SemaphoreType.DMA((model // width,)),
        ],
        compiler_params=params(),
        cost_estimate=pl.CostEstimate(
            flops=2 * rows * WIDTH * (model + 4 * TILE),
            bytes_accessed=2 * (rows * model + WIDTH * model),
            transcendentals=rows * HEADS * 2 * TILE,
        ),
        name="attend_and_mix",
    )(queries, *own, *edges, *sources)


def swap(x, axis, bits):
    return lax.ppermute(x, axis, [(i, i ^ bits) for i in range(lax.axis_size(axis))])


def swap_plane(x, turn):
    places = lax.axis_size("frame")
    pairs = []
    for i in range(lax.axis_size("fsdp")):
        for j in range(places):
            pairs.append((i * places + j, i * places + (j ^ (1 + (i + turn) % 2))))
    return lax.ppermute(x, ("fsdp", "frame"), pairs)


def hop_order(chips):
    odd = [k for k in range(chips - 1, 0, -1) if k % 2]
    return odd + [k - 1 for k in odd if k > 1]


def halos(stacked):
    places = lax.axis_size("frame")
    odd = lax.axis_index("frame") & 1
    tail = stacked.shape[0] - BORDER
    near = lax.dynamic_slice_in_dim(stacked, (1 - odd) * tail, BORDER, 0)
    far = lax.dynamic_slice_in_dim(stacked, odd * tail, BORDER, 0)
    straight, out, on = [], [], []
    for i in range(lax.axis_size("fsdp")):
        for j in range(0, places, 4):
            for source, way, target in ((1, 3, 2), (2, 0, 1)):
                place = i * places + j
                if i % 2:
                    out.append((place + source, place + way))
                    on.append((place + way, place + target))
                else:
                    straight.append((place + source, place + target))
    axes = ("fsdp", "frame")
    way = lax.ppermute(far, axes, out)
    arrived = [lax.ppermute(way, axes, on), lax.ppermute(far, axes, straight)]
    if places > 4:
        pairs = [(j, j + 1) for j in range(3, places - 1, 4)]
        arrived.append(lax.ppermute(far, "frame", pairs + [(b, a) for a, b in pairs]))
    return [swap(near, "frame", 1)] + arrived


def split_plan(frames, modulation, w_qkv, w_out, qk_gain):
    chips = lax.axis_size("fsdp") // 2
    shard_rows, columns = w_qkv.shape
    shard_columns = w_out.shape[1]
    quarter = shard_rows // 4
    hops = hop_order(chips)
    odd, even = [k for k in hops if k % 2], [k for k in hops if k % 2 == 0]
    front, back = [k for k in odd if k > 1], even
    ring = [1] + front + back
    fence = lax.optimization_barrier

    def where():
        place, index = lax.axis_index("frame"), lax.axis_index("fsdp")
        high = (place >> 1) & 1
        return index // 2, index % 2, 2 * ((place & 1) ^ high) + high

    def order(core):
        spot = where()[2]
        return spot, spot ^ (2 + core), spot ^ (3 - core), spot ^ 1

    def shard_places():
        chip, core, _ = where()
        cores = (core, 1 - core)
        return [[((chip ^ k) * 2 + c) * shard_rows for k in ring] for c in cores], cores

    def own_places():
        chip, core, _ = where()
        return [pl.multiple_of((2 * chip + c) * shard_rows, TILE) for c in (core, 1 - core)]

    def out_layout():
        chip, core, _ = where()
        place = 2 * chip + core
        return [
            (source, 0, shard_columns, (place ^ (2 * k + here)) * shard_columns)
            for source, (k, here) in enumerate((k, here) for k in [0] + ring for here in (0, 1))
        ]

    spot = where()[2]
    part = lax.dynamic_slice_in_dim(w_qkv, spot * quarter, quarter, 0)
    come = [swap(part, "fsdp", 2 * k) for k in front]
    near = swap(part, "fsdp", 2)
    other_qkv = swap(w_qkv, "fsdp", 1)
    other_out = swap(w_out, "fsdp", 1)
    normed = norm_rows(frames, modulation)
    normed, come = fence((normed, come))

    late = [swap(x, "fsdp", 2) for x in come]
    one = jnp.concatenate(come, axis=0)
    one_rest = swap_plane(one, 0)
    total = project(
        [(normed, w_qkv), (normed, other_qkv)], qk_gain, (0, columns), "project_own", own_places
    )
    nf, nb = len(front), len(back)
    homes = [[(4, nb), (5, 2 * nb), (2, 2 * nf + nb), (3, 0)]]
    homes += [[(0, i), (1, i), (2, i), (2, nf + i)] for i in range(nf)]
    homes += [[(4, i), (5, i), (2, 2 * nf + i), (5, nb + i)] for i in range(nb)]
    widths = [quarter * n for n in (nf, nf, 2 * nf + nb + 1, 1, nb + 1, 2 * nb + 1)]
    arranged = arrange(shard_places, order, homes, widths, normed)
    next_part = lax.dynamic_slice_in_dim(w_qkv, (spot ^ 1) * quarter, quarter, 0)
    one, one_rest, late, near, total, arranged, next_part = fence(
        (one, one_rest, late, near, total, arranged, next_part)
    )

    late = jnp.concatenate(late + [near], axis=0)
    two = swap_plane(jnp.concatenate([one, one_rest, late], axis=0), 1)
    across = swap(next_part, "fsdp", 2)
    cut = 2 * (shard_columns // TILE) // 3 * TILE
    wides = [swap(w_out[:, :cut], "fsdp", 2 * k) for k in front]
    one_other, one_rest_other = swap(one, "fsdp", 1), swap(one_rest, "fsdp", 1)
    late_other = swap(late, "fsdp", 1)
    two, across, late, one_other, one_rest_other, late_other, wides = fence(
        (two, across, late, one_other, one_rest_other, late_other, wides)
    )

    relayed = two[2 * nf * quarter : (2 * nf + nb) * quarter]
    three = swap_plane(
        jnp.concatenate([late[: nb * quarter], relayed, late[nb * quarter :]], axis=0), 0
    )
    narrows = [swap(w_out[:, cut:], "fsdp", 2 * k) for k in front]
    pieces = [one, one_other, one_rest, one_rest_other, two, swap(two, "fsdp", 1)]
    pieces += [across, swap(across, "fsdp", 1), late, late_other]
    total = project(
        list(zip(arranged[:10], pieces)), qk_gain, (0, columns), "project_mid", total=total
    )
    total, three, narrows = fence((total, three, narrows))

    last = [(arranged[10], three), (arranged[11], swap(three, "fsdp", 1))]
    stacked = project(
        last, qk_gain, (WIDTH, 2 * WIDTH), "project_keys_values", kinds=(1, None), total=total
    )
    queries = project(last, qk_gain, (0, WIDTH), "project_queries", kinds=(0,), total=total)

    joined = [jnp.concatenate(pair, axis=1) for pair in zip(wides, narrows)]
    sources = [w_out, other_out]
    edges = halos(stacked)
    for x in [swap(w_out, "fsdp", 2)] + joined + [swap(x, "fsdp", 2) for x in joined]:
        sources += [x, swap(fence((x, edges[0]))[0], "fsdp", 1)]
    return queries, stacked, edges, out_layout, sources


def whole_plan(frames, modulation, w_qkv, w_out, qk_gain):
    rows = lax.all_gather(w_qkv, "fsdp", axis=0, tiled=True)
    columns = lax.all_gather(w_out, "fsdp", axis=1, tiled=True)
    normed = norm_rows(frames, modulation)
    stacked = project(
        [(normed, rows)], qk_gain, (WIDTH, 2 * WIDTH), "project_keys_values", kinds=(1, None)
    )
    queries = project([(normed, rows)], qk_gain, (0, WIDTH), "project_queries", kinds=(0,))
    return queries, stacked, halos(stacked), lambda: [(0, 0, columns.shape[1], 0)], [columns]


def on_device(frames, modulation, w_qkv, qk_gain, w_out):
    devices, places = lax.axis_size("fsdp"), lax.axis_size("frame")
    chips = devices // 2
    split = (
        devices % 2 == 0
        and chips > 2
        and chips & (chips - 1) == 0
        and w_qkv.shape[0] % TILE == 0
        and w_out.shape[1] % TILE == 0
    )
    plan = split_plan if split else whole_plan
    queries, stacked, edges, layout, sources = plan(
        frames[0], modulation[0], w_qkv, w_out, qk_gain
    )
    own = attend_own(queries, stacked)
    return attend(layout, sources, queries, own, edges, frames.shape[2])


def solution(mesh):
    return jax.shard_map(
        on_device,
        mesh=mesh,
        in_specs=(
            P("fsdp", "frame", None),
            P("fsdp", None, None),
            P("fsdp", None),
            P(),
            P(None, "fsdp"),
        ),
        out_specs=P("fsdp", "frame", None),
        check_vma=False,
    )
```

time: 63.5 us -> 57.6 us (0.907)
  waiting for transfers between devices: 26.4 us -> 15.6 us
  starting transfers between devices: 21.6 us -> 25.8 us
    ppermute x2 -> x3, waiting for transfers between devices: 9.01 us -> 0.01 us  [the longest x2 0.01 us: halos(): arrived = [lax.ppermute(way, axes, on), lax.ppermute(far, axes, straight)]]
    ppermute x16 -> x20, starting transfers between devices: 13.7 us -> 20.1 us  [swap(): lax.ppermute(x, axis, [(i, i ^ bits) for i in range(lax.axis_size(axis))])]
    ppermute x2 -> x3, starting transfers between devices: 4.7 us -> 2.02 us  [the longest x2 1.34 us: halos(): arrived = [lax.ppermute(way, axes, on), lax.ppermute(far, axes, straight)]]
    ppermute x16 -> x20, waiting for transfers between devices: 16.8 us -> 14.4 us  [swap(): lax.ppermute(x, axis, [(i, i ^ bits) for i in range(lax.axis_size(axis))])]
    ppermute x2 -> x3, starting transfers between devices: 3.14 us -> 3.75 us  [swap_plane(): return lax.ppermute(x, ('fsdp', 'frame'), pairs)]
    pallas_call x2 -> x3, Pallas kernels: 6.62 us -> 6.51 us  [the longest x1 3.2 us: attend(): pl.pallas_call(functools.partial(attend_kernel, layout, len(sources), len...]
  transfers between devices with their start and end apart: 20 -> 26, of which waited for: 11 -> 9; matrix products, arithmetic and copies ran while one was open for 2% -> 2% of each run, Pallas kernels for 13% -> 15%
where the time goes in v3:
time: 57.6 us; the launch traced here: 57.2 us
  starting transfers between devices  25.8 us (45%)
  waiting for transfers between devices  15.6 us (27%)
  Pallas kernels  11.8 us (20%)
  local copies, waits for them, and re-layouts  3.57 us (6%)
    ppermute x20, starting transfers between devices, swap(): lax.ppermute(x, axis, [(i, i ^ bits) for i in range(lax.axis_size(axis))])  20.1 us
    ppermute x20, waiting for transfers between devices, swap(): lax.ppermute(x, axis, [(i, i ^ bits) for i in range(lax.axis_size(axis))])  14.4 us
    pallas_call x4, Pallas kernels, project(): pl.pallas_call(functools.partial(project_kernel, len(pairs), starts, kind...  3.86 us
    ppermute x3, starting transfers between devices, swap_plane(): return lax.ppermute(x, ('fsdp', 'frame'), pairs)  3.75 us
    pallas_call x1, Pallas kernels, attend(): pl.pallas_call(functools.partial(attend_kernel, layout, len(sources), len...  3.2 us
    unnamed x12, local copies, waits for them, and re-layouts  2.44 us
    pallas_call x1, Pallas kernels, norm_rows(): pl.pallas_call(norm_kernel, grid=(rows // block,), in_specs=[pl.BlockSpec...  2.15 us
    pallas_call x1, Pallas kernels, arrange(): pl.pallas_call(functools.partial(arrange_kernel, starts, order, homes), i...  1.44 us
  transfers between devices with their start and end apart: 26, of which 9 were waited for; matrix products, arithmetic and copies ran while one was open for 2% of the time, Pallas kernels for 15%

profile of v3, /device:TPU:0, one launch (start us, length us, event | category | flops | bytes accessed | tf_op | source)
XLA Modules:
  0.0 57.2 jit_solution(5502577540852744787)
XLA Ops:
  0.5 1.0 %constant_dynamic-slice_fusion.2 = (bf16[96,768]{1,0:T(8,128)(2,1)S(1)}, bf16[96,768]{1,0:T(8,128)(2,1)S(1)}) fusion(bf16[384,768]{1,0:T(8,128)(2,1)} %refs_2_.1, s32[]{:T(128)S(6)} %select_n.13, s32[]{:T(128)S(6)} %select_n.12), kind=kLoop, calls=%fused_computation.8 | loop fusion | bytes 589832 | tf_op jit(solution)/shard_map/dynamic_slice | solution.py:380
  1.5 4.7 %collective-permute-start = (bf16[96,768]{1,0:T(8,128)(2,1)S(1)}, bf16[96,768]{1,0:T(8,128)(2,1)S(1)}, u32[]{:S(2)}, u32[]{:S(2)}) collective-permute-start(bf16[96,768]{1,0:T(8,128)(2,1)S(1)} %get-tuple-element.100), channel_id=1, source_target_pairs={{0,24},{4,28},{8,16},{12,20},{16,8},{20,12},{24,0},{28,4},{1,25},{... | collective-permute-start | bytes 442376 | tf_op jit(solution)/shard_map/ppermute | solution.py:280
  6.1 1.7 %copy-done = bf16[1,384,3072]{2,1,0:T(8,128)(2,1)S(1)} copy-done((bf16[1,384,3072]{2,1,0:T(8,128)(2,1)S(1)}, bf16[1,384,3072]{2,1,0:T(8,128)(2,1)}, u32[]{:S(2)}) %copy-start) | copy-done | bytes 2359320
  8.5 2.1 %layer_norm.1.refs_0_.refs_1_.normed_ref = bf16[384,3072]{1,0:T(8,128)(2,1)S(1)} custom-call(bf16[384,3072]{1,0:T(8,128)(2,1)S(1)} %bitcast.2, f32[2,3072]{1,0:T(2,128)S(1)} %bitcast.3), custom_call_target="tpu_custom_call" | custom-call | flops 11796480 | bytes 4718592 | tf_op jit(solution)/shard_map/layer_norm/pallas_call | solution.py:49
  10.9 1.6 %collective-permute-start.1 = (bf16[96,768]{1,0:T(8,128)(2,1)S(1)}, bf16[96,768]{1,0:T(8,128)(2,1)S(1)}, u32[]{:S(2)}, u32[]{:S(2)}) collective-permute-start(bf16[96,768]{1,0:T(8,128)(2,1)S(1)} %collective-permute-done.refs_10_), channel_id=1, source_target_pairs={{0,1},{1,0},{2,3},{3,2},{4,6},{5,7},{6,4},{7,5},{8,9},{9,8},{10,11... | collective-permute-start | bytes 442376 | tf_op jit(solution)/shard_map/ppermute | solution.py:289
  12.5 2.5 %collective-permute-start.2 = (bf16[96,768]{1,0:T(8,128)(2,1)S(1)}, bf16[96,768]{1,0:T(8,128)(2,1)S(1)}, u32[]{:S(2)}, u32[]{:S(2)}) collective-permute-start(bf16[96,768]{1,0:T(8,128)(2,1)S(1)} %collective-permute-done.refs_10_), channel_id=1, source_target_pairs={{0,8},{4,12},{8,0},{12,4},{16,24},{20,28},{24,16},{28,20},{1,9},{5... | collective-permute-start | bytes 442376 | tf_op jit(solution)/shard_map/ppermute | solution.py:280
  15.0 1.4 %arrange.1 = (bf16[384,96]{1,0:T(8,128)(2,1)S(1)}, bf16[384,96]{1,0:T(8,128)(2,1)S(1)}, bf16[384,96]{1,0:T(8,128)(2,1)S(1)}, bf16[384,96]{1,0:T(8,128)(2,1)S(1)}...) custom-call(bf16[384,3072]{1,0:T(8,128)(2,1)S(1)} %layer_norm.1.refs, ...), custom_call_target="tpu_custom_call" | custom-call | flops 1207959552 | bytes 4718592 | tf_op jit(solution)/shard_map/arrange/pallas_call | solution.py:140
  17.3 1.2 %collective-permute-done.2 = bf16[96,768]{1,0:T(8,128)(2,1)S(1)} collective-permute-done((bf16[96,768]{1,0:T(8,128)(2,1)S(1)}, bf16[96,768]{1,0:T(8,128)(2,1)S(1)}, u32[]{:S(2)}, u32[]{:S(2)}) %collective-permute-start.2) | collective-permute-done | bytes 147488 | tf_op jit(solution)/shard_map/ppermute | solution.py:280
  18.5 1.2 %collective-permute-start.5 = (bf16[384,768]{1,0:T(8,128)(2,1)S(1)}, bf16[384,768]{1,0:T(8,128)(2,1)S(1)}, u32[]{:S(2)}, u32[]{:S(2)}) collective-permute-start(bf16[384,768]{1,0:T(8,128)(2,1)S(1)} %pad_maximum_fusion), channel_id=1, source_target_pairs={{0,2},{1,3},{2,0},{3,1},{4,5},{5,4},{6,7},{7,6},{8,10},{9,11},{10,... | collective-permute-start | bytes 1769480 | tf_op jit(solution)/shard_map/ppermute | solution.py:289
  19.9 3.2 %collective-permute-start.10 = (bf16[256,256]{1,0:T(8,128)(2,1)S(1)}, bf16[256,256]{1,0:T(8,128)(2,1)S(1)}, u32[]{:S(2)}, u32[]{:S(2)}) collective-permute-start(bf16[256,256]{1,0:T(8,128)(2,1)S(1)} %slice.15), channel_id=1, source_target_pairs={{0,24},{4,28},{8,16},{12,20},{16,8},{20,12},{24,0},{28,4},{1,25},{... | collective-permute-start | bytes 393224 | tf_op jit(solution)/shard_map/ppermute | solution.py:280
  23.8 4.3 %collective-permute-done.10 = bf16[256,256]{1,0:T(8,128)(2,1)S(1)} collective-permute-done((bf16[256,256]{1,0:T(8,128)(2,1)S(1)}, bf16[256,256]{1,0:T(8,128)(2,1)S(1)}, u32[]{:S(2)}, u32[]{:S(2)}) %collective-permute-start.10) | collective-permute-done | bytes 131104 | tf_op jit(solution)/shard_map/ppermute | solution.py:280
  28.1 2.8 %collective-permute-done.6.refs_16_ = bf16[96,768]{1,0:T(8,128)(2,1)S(1)} collective-permute-done((bf16[96,768]{1,0:T(8,128)(2,1)S(1)}, bf16[96,768]{1,0:T(8,128)(2,1)S(1)}, u32[]{:S(2)}, u32[]{:S(2)}) %collective-permute-start.6) | collective-permute-done | bytes 147488 | tf_op jit(solution)/shard_map/ppermute | solution.py:280
  31.1 0.9 %collective-permute-start.13 = (bf16[288,768]{1,0:T(8,128)(2,1)S(1)}, bf16[288,768]{1,0:T(8,128)(2,1)S(1)}, u32[]{:S(2)}, u32[]{:S(2)}) collective-permute-start(bf16[288,768]{1,0:T(8,128)(2,1)S(1)} %pad_maximum_fusion.1), channel_id=1, source_target_pairs={{0,1},{1,0},{2,3},{3,2},{4,6},{5,7},{6,4},{7,5},{8,9},{9,8},{10,11... | collective-permute-start | bytes 1327112 | tf_op jit(solution)/shard_map/ppermute | solution.py:289
  32.3 2.0 %collective-permute-start.14 = (bf16[256,128]{1,0:T(8,128)(2,1)S(1)}, bf16[256,128]{1,0:T(8,128)(2,1)S(1)}, u32[]{:S(2)}, u32[]{:S(2)}) collective-permute-start(bf16[256,128]{1,0:T(8,128)(2,1)S(1)} %slice.19), channel_id=1, source_target_pairs={{0,24},{4,28},{8,16},{12,20},{16,8},{20,12},{24,0},{28,4},{1,25},{... | collective-permute-start | bytes 196616 | tf_op jit(solution)/shard_map/ppermute | solution.py:280
  34.2 2.0 %project_mid.1.refs_4_ = f32[384,768]{1,0:T(8,128)S(1)} custom-call(f32[2,128]{1,0:T(2,128)S(1)} %copy-done.4, bf16[384,96]{1,0:T(8,128)(2,1)S(1)} %get-tuple-element.68.refs_0_, bf16[384,96]{1,0:T(8,128)(2,1)S(1)} %get-tuple-element.69.refs_1_, bf16[384,96]{1,0:T(8,128)(2,1)S(1)} %get-tuple-element.70.refs_2_, ...), custom_call_target="tpu_custom_call" | custom-call | flops 1019215872 | bytes 3981312 | tf_op jit(solution)/shard_map/project_mid/pallas_call | solution.py:100
  36.2 2.1 %collective-permute-done.14 = bf16[256,128]{1,0:T(8,128)(2,1)S(1)} collective-permute-done((bf16[256,128]{1,0:T(8,128)(2,1)S(1)}, bf16[256,128]{1,0:T(8,128)(2,1)S(1)}, u32[]{:S(2)}, u32[]{:S(2)}) %collective-permute-start.14) | collective-permute-done | bytes 65568 | tf_op jit(solution)/shard_map/ppermute | solution.py:280
  38.4 1.1 %collective-permute-done.13.refs_2_ = bf16[288,768]{1,0:T(8,128)(2,1)S(1)} collective-permute-done((bf16[288,768]{1,0:T(8,128)(2,1)S(1)}, bf16[288,768]{1,0:T(8,128)(2,1)S(1)}, u32[]{:S(2)}, u32[]{:S(2)}) %collective-permute-start.13) | collective-permute-done | bytes 442400 | tf_op jit(solution)/shard_map/ppermute | solution.py:289
  39.5 1.2 %collective-permute-start.21 = (bf16[256,384]{1,0:T(8,128)(2,1)S(1)}, bf16[256,384]{1,0:T(8,128)(2,1)S(1)}, u32[]{:S(2)}, u32[]{:S(2)}) collective-permute-start(bf16[256,384]{1,0:T(8,128)(2,1)S(1)} %copy-done.2), channel_id=1, source_target_pairs={{0,8},{4,12},{8,0},{12,4},{16,24},{20,28},{24,16},{28,20},{1,9},{5... | collective-permute-start | bytes 589832 | tf_op jit(solution)/shard_map/ppermute | solution.py:280
  42.7 0.9 %collective-permute-start.16 = (bf16[256,512]{1,0:T(8,128)(2,1)S(1)}, bf16[256,512]{1,0:T(8,128)(2,1)S(1)}, u32[]{:S(2)}, u32[]{:S(2)}) collective-permute-start(bf16[256,512]{1,0:T(8,128)(2,1)S(1)} %get-tuple-element.102), channel_id=1, source_target_pairs={{0,1},{1,0},{2,3},{3,2},{4,5},{5,4},{6,7},{7,6},{8,9},{9,8},{10,11... | collective-permute-start | bytes 786440 | tf_op jit(solution)/shard_map/ppermute | solution.py:280
  43.6 1.0 %collective-permute-start.24 = (bf16[256,384]{1,0:T(8,128)(2,1)S(1)}, bf16[256,384]{1,0:T(8,128)(2,1)S(1)}, u32[]{:S(2)}, u32[]{:S(2)}) collective-permute-start(bf16[256,384]{1,0:T(8,128)(2,1)S(1)} %constant_dynamic-update-slice_fusion.2.refs_7_), channel_id=1, source_target_pairs={{0,8},{4,12},{8,0},{12,4},{16,24},{20,28},{24,16},{28,20},{1,9},{5... | collective-permute-start | bytes 589832 | tf_op jit(solution)/shard_map/ppermute | solution.py:280
  44.6 2.0 %collective-permute-start.20 = (bf16[256,384]{1,0:T(8,128)(2,1)S(1)}, bf16[256,384]{1,0:T(8,128)(2,1)S(1)}, u32[]{:S(2)}, u32[]{:S(2)}) collective-permute-start(bf16[256,384]{1,0:T(8,128)(2,1)S(1)} %copy-done.2), channel_id=1, source_target_pairs={{0,4},{4,0},{8,12},{12,8},{16,20},{20,16},{24,28},{28,24},{1,5},{5... | collective-permute-start | bytes 589832 | tf_op jit(solution)/shard_map/ppermute | solution.py:280
  48.2 3.1 %collective-permute-done.16.refs_0_ = bf16[256,512]{1,0:T(8,128)(2,1)S(1)} collective-permute-done((bf16[256,512]{1,0:T(8,128)(2,1)S(1)}, bf16[256,512]{1,0:T(8,128)(2,1)S(1)}, u32[]{:S(2)}, u32[]{:S(2)}) %collective-permute-start.16) | collective-permute-done | bytes 262176 | tf_op jit(solution)/shard_map/ppermute | solution.py:280
  52.7 1.2 %attend_own_slab.1 = (f32[384,256]{1,0:T(8,128)S(1)}, f32[384,256]{1,0:T(8,128)S(1)}) custom-call(bf16[384,256]{1,0:T(8,128)(2,1)S(1)} %project_queries.1.queries_ref, bf16[384,512]{1,0:T(8,128)(2,1)S(1)} %project_keys_values.1.stacked_ref), custom_call_target="tpu_custom_call" | custom-call | flops 150994944 | bytes 1376256 | tf_op jit(solution)/shard_map/attend_own_slab/pallas_call | solution.py:193
  54.0 3.2 %attend_and_mix.1 = bf16[1,384,3072]{2,1,0:T(8,128)(2,1)} custom-call(bf16[384,256]{1,0:T(8,128)(2,1)S(1)} %project_queries.1.queries_ref, f32[384,256]{1,0:T(8,128)S(1)} %get-tuple-element.92.weighted_ref, f32[384,256]{1,0:T(8,128)S(1)} %get-tuple-element.93.mass_ref, bf16[256,512]{1,0:T(8,128)(2,1)S(1)} %collective-permute-done.16.refs_0_, ...), custom_call_target="tpu_custom_call" | custom-call | flops 704643072 | bytes 3932160 | tf_op jit(solution)/shard_map/attend_and_mix/pallas_call | solution.py:255
  (58 shorter events, 8.4 us)
Async XLA Ops:
  0.0 16.5 %collective-permute-start.4 = (bf16[384,768]{1,0:T(8,128)(2,1)}, bf16[384,768]{1,0:T(8,128)(2,1)S(1)}, u32[]{:S(2)}, u32[]{:S(2)}) collective-permute-start(bf16[384,768]{1,0:T(8,128)(2,1)} %refs_2_.1), channel_id=1, source_target_pairs={{0,4},{4,0},{8,12},{12,8},{16,20},{20,16},{24,28},{28,24},{1,5},{5... | collective-permute-start | bytes 1769480 | tf_op jit(solution)/shard_map/ppermute | solution.py:280
  1.5 9.4 %collective-permute-start = (bf16[96,768]{1,0:T(8,128)(2,1)S(1)}, bf16[96,768]{1,0:T(8,128)(2,1)S(1)}, u32[]{:S(2)}, u32[]{:S(2)}) collective-permute-start(bf16[96,768]{1,0:T(8,128)(2,1)S(1)} %get-tuple-element.100), channel_id=1, source_target_pairs={{0,24},{4,28},{8,16},{12,20},{16,8},{20,12},{24,0},{28,4},{1,25},{... | collective-permute-start | bytes 442376 | tf_op jit(solution)/shard_map/ppermute | solution.py:280
  6.1 11.1 %collective-permute-start.3 = (bf16[96,768]{1,0:T(8,128)(2,1)S(1)}, bf16[96,768]{1,0:T(8,128)(2,1)S(1)}, u32[]{:S(2)}, u32[]{:S(2)}) collective-permute-start(bf16[96,768]{1,0:T(8,128)(2,1)S(1)} %get-tuple-element.100), channel_id=1, source_target_pairs={{0,8},{4,12},{8,0},{12,4},{16,24},{20,28},{24,16},{28,20},{1,9},{5... | collective-permute-start | bytes 442376 | tf_op jit(solution)/shard_map/ppermute | solution.py:280
  10.9 6.4 %collective-permute-start.1 = (bf16[96,768]{1,0:T(8,128)(2,1)S(1)}, bf16[96,768]{1,0:T(8,128)(2,1)S(1)}, u32[]{:S(2)}, u32[]{:S(2)}) collective-permute-start(bf16[96,768]{1,0:T(8,128)(2,1)S(1)} %collective-permute-done.refs_10_), channel_id=1, source_target_pairs={{0,1},{1,0},{2,3},{3,2},{4,6},{5,7},{6,4},{7,5},{8,9},{9,8},{10,11... | collective-permute-start | bytes 442376 | tf_op jit(solution)/shard_map/ppermute | solution.py:289
  12.5 6.0 %collective-permute-start.2 = (bf16[96,768]{1,0:T(8,128)(2,1)S(1)}, bf16[96,768]{1,0:T(8,128)(2,1)S(1)}, u32[]{:S(2)}, u32[]{:S(2)}) collective-permute-start(bf16[96,768]{1,0:T(8,128)(2,1)S(1)} %collective-permute-done.refs_10_), channel_id=1, source_target_pairs={{0,8},{4,12},{8,0},{12,4},{16,24},{20,28},{24,16},{28,20},{1,9},{5... | collective-permute-start | bytes 442376 | tf_op jit(solution)/shard_map/ppermute | solution.py:280
  18.5 12.4 %collective-permute-start.5 = (bf16[384,768]{1,0:T(8,128)(2,1)S(1)}, bf16[384,768]{1,0:T(8,128)(2,1)S(1)}, u32[]{:S(2)}, u32[]{:S(2)}) collective-permute-start(bf16[384,768]{1,0:T(8,128)(2,1)S(1)} %pad_maximum_fusion), channel_id=1, source_target_pairs={{0,2},{1,3},{2,0},{3,1},{4,5},{5,4},{6,7},{7,6},{8,10},{9,11},{10,... | collective-permute-start | bytes 1769480 | tf_op jit(solution)/shard_map/ppermute | solution.py:289
  19.8 11.1 %collective-permute-start.9 = (bf16[192,768]{1,0:T(8,128)(2,1)S(1)}, bf16[192,768]{1,0:T(8,128)(2,1)S(1)}, u32[]{:S(2)}, u32[]{:S(2)}) collective-permute-start(bf16[192,768]{1,0:T(8,128)(2,1)S(1)} %constant_dynamic-update-slice_fusion.refs_18_), channel_id=1, source_target_pairs={{0,4},{4,0},{8,12},{12,8},{16,20},{20,16},{24,28},{28,24},{1,5},{5... | collective-permute-start | bytes 884744 | tf_op jit(solution)/shard_map/ppermute | solution.py:280
  19.9 8.2 %collective-permute-start.10 = (bf16[256,256]{1,0:T(8,128)(2,1)S(1)}, bf16[256,256]{1,0:T(8,128)(2,1)S(1)}, u32[]{:S(2)}, u32[]{:S(2)}) collective-permute-start(bf16[256,256]{1,0:T(8,128)(2,1)S(1)} %slice.15), channel_id=1, source_target_pairs={{0,24},{4,28},{8,16},{12,20},{16,8},{20,12},{24,0},{28,4},{1,25},{... | collective-permute-start | bytes 393224 | tf_op jit(solution)/shard_map/ppermute | solution.py:280
  23.1 7.8 %collective-permute-start.7 = (bf16[96,768]{1,0:T(8,128)(2,1)S(1)}, bf16[96,768]{1,0:T(8,128)(2,1)S(1)}, u32[]{:S(2)}, u32[]{:S(2)}) collective-permute-start(bf16[96,768]{1,0:T(8,128)(2,1)S(1)} %collective-permute-done.refs_10_), channel_id=1, source_target_pairs={{0,4},{4,0},{8,12},{12,8},{16,20},{20,16},{24,28},{28,24},{1,5},{5... | collective-permute-start | bytes 442376 | tf_op jit(solution)/shard_map/ppermute | solution.py:280
  23.3 7.6 %collective-permute-start.6 = (bf16[96,768]{1,0:T(8,128)(2,1)S(1)}, bf16[96,768]{1,0:T(8,128)(2,1)S(1)}, u32[]{:S(2)}, u32[]{:S(2)}) collective-permute-start(bf16[96,768]{1,0:T(8,128)(2,1)S(1)} %get-tuple-element.82), channel_id=1, source_target_pairs={{0,8},{4,12},{8,0},{12,4},{16,24},{20,28},{24,16},{28,20},{1,9},{5... | collective-permute-start | bytes 442376 | tf_op jit(solution)/shard_map/ppermute | solution.py:280
  28.1 2.8 %collective-permute-start.8 = (bf16[96,768]{1,0:T(8,128)(2,1)S(1)}, bf16[96,768]{1,0:T(8,128)(2,1)S(1)}, u32[]{:S(2)}, u32[]{:S(2)}) collective-permute-start(bf16[96,768]{1,0:T(8,128)(2,1)S(1)} %collective-permute-done.1.refs_12_), channel_id=1, source_target_pairs={{0,4},{4,0},{8,12},{12,8},{16,20},{20,16},{24,28},{28,24},{1,5},{5... | collective-permute-start | bytes 442376 | tf_op jit(solution)/shard_map/ppermute | solution.py:280
  30.9 3.3 %collective-permute-start.11 = (bf16[384,768]{1,0:T(8,128)(2,1)S(1)}, bf16[384,768]{1,0:T(8,128)(2,1)S(1)}, u32[]{:S(2)}, u32[]{:S(2)}) collective-permute-start(bf16[384,768]{1,0:T(8,128)(2,1)S(1)} %collective-permute-done.5.refs_14_), channel_id=1, source_target_pairs={{0,4},{4,0},{8,12},{12,8},{16,20},{20,16},{24,28},{28,24},{1,5},{5... | collective-permute-start | bytes 1769480 | tf_op jit(solution)/shard_map/ppermute | solution.py:280
  31.1 8.4 %collective-permute-start.13 = (bf16[288,768]{1,0:T(8,128)(2,1)S(1)}, bf16[288,768]{1,0:T(8,128)(2,1)S(1)}, u32[]{:S(2)}, u32[]{:S(2)}) collective-permute-start(bf16[288,768]{1,0:T(8,128)(2,1)S(1)} %pad_maximum_fusion.1), channel_id=1, source_target_pairs={{0,1},{1,0},{2,3},{3,2},{4,6},{5,7},{6,4},{7,5},{8,9},{9,8},{10,11... | collective-permute-start | bytes 1327112 | tf_op jit(solution)/shard_map/ppermute | solution.py:289
  32.0 2.2 %collective-permute-start.12 = (bf16[96,768]{1,0:T(8,128)(2,1)S(1)}, bf16[96,768]{1,0:T(8,128)(2,1)S(1)}, u32[]{:S(2)}, u32[]{:S(2)}) collective-permute-start(bf16[96,768]{1,0:T(8,128)(2,1)S(1)} %collective-permute-done.6.refs_16_), channel_id=1, source_target_pairs={{0,4},{4,0},{8,12},{12,8},{16,20},{20,16},{24,28},{28,24},{1,5},{5... | collective-permute-start | bytes 442376 | tf_op jit(solution)/shard_map/ppermute | solution.py:280
  32.3 6.1 %collective-permute-start.14 = (bf16[256,128]{1,0:T(8,128)(2,1)S(1)}, bf16[256,128]{1,0:T(8,128)(2,1)S(1)}, u32[]{:S(2)}, u32[]{:S(2)}) collective-permute-start(bf16[256,128]{1,0:T(8,128)(2,1)S(1)} %slice.19), channel_id=1, source_target_pairs={{0,24},{4,28},{8,16},{12,20},{16,8},{20,12},{24,0},{28,4},{1,25},{... | collective-permute-start | bytes 196616 | tf_op jit(solution)/shard_map/ppermute | solution.py:280
  39.5 7.3 %collective-permute-start.21 = (bf16[256,384]{1,0:T(8,128)(2,1)S(1)}, bf16[256,384]{1,0:T(8,128)(2,1)S(1)}, u32[]{:S(2)}, u32[]{:S(2)}) collective-permute-start(bf16[256,384]{1,0:T(8,128)(2,1)S(1)} %copy-done.2), channel_id=1, source_target_pairs={{0,8},{4,12},{8,0},{12,4},{16,24},{20,28},{24,16},{28,20},{1,9},{5... | collective-permute-start | bytes 589832 | tf_op jit(solution)/shard_map/ppermute | solution.py:280
  42.0 5.5 %collective-permute-start.17 = (bf16[256,512]{1,0:T(8,128)(2,1)S(1)}, bf16[256,512]{1,0:T(8,128)(2,1)S(1)}, u32[]{:S(2)}, u32[]{:S(2)}) collective-permute-start(bf16[256,512]{1,0:T(8,128)(2,1)S(1)} %get-tuple-element.101), channel_id=1, source_target_pairs={{5,7},{6,4},{13,15},{14,12},{21,23},{22,20},{29,31},{30,28}} | collective-permute-start | bytes 786440 | tf_op jit(solution)/shard_map/ppermute | solution.py:314
  42.7 8.5 %collective-permute-start.16 = (bf16[256,512]{1,0:T(8,128)(2,1)S(1)}, bf16[256,512]{1,0:T(8,128)(2,1)S(1)}, u32[]{:S(2)}, u32[]{:S(2)}) collective-permute-start(bf16[256,512]{1,0:T(8,128)(2,1)S(1)} %get-tuple-element.102), channel_id=1, source_target_pairs={{0,1},{1,0},{2,3},{3,2},{4,5},{5,4},{6,7},{7,6},{8,9},{9,8},{10,11... | collective-permute-start | bytes 786440 | tf_op jit(solution)/shard_map/ppermute | solution.py:280
  43.6 8.1 %collective-permute-start.24 = (bf16[256,384]{1,0:T(8,128)(2,1)S(1)}, bf16[256,384]{1,0:T(8,128)(2,1)S(1)}, u32[]{:S(2)}, u32[]{:S(2)}) collective-permute-start(bf16[256,384]{1,0:T(8,128)(2,1)S(1)} %constant_dynamic-update-slice_fusion.2.refs_7_), channel_id=1, source_target_pairs={{0,8},{4,12},{8,0},{12,4},{16,24},{20,28},{24,16},{28,20},{1,9},{5... | collective-permute-start | bytes 589832 | tf_op jit(solution)/shard_map/ppermute | solution.py:280
  44.6 7.2 %collective-permute-start.20 = (bf16[256,384]{1,0:T(8,128)(2,1)S(1)}, bf16[256,384]{1,0:T(8,128)(2,1)S(1)}, u32[]{:S(2)}, u32[]{:S(2)}) collective-permute-start(bf16[256,384]{1,0:T(8,128)(2,1)S(1)} %copy-done.2), channel_id=1, source_target_pairs={{0,4},{4,0},{8,12},{12,8},{16,20},{20,16},{24,28},{28,24},{1,5},{5... | collective-permute-start | bytes 589832 | tf_op jit(solution)/shard_map/ppermute | solution.py:280
  46.8 7.1 %collective-permute-start.19 = (bf16[256,512]{1,0:T(8,128)(2,1)S(1)}, bf16[256,512]{1,0:T(8,128)(2,1)S(1)}, u32[]{:S(2)}, u32[]{:S(2)}) collective-permute-start(bf16[256,512]{1,0:T(8,128)(2,1)S(1)} %get-tuple-element.101), channel_id=1, source_target_pairs={{1,2},{2,1},{9,10},{10,9},{17,18},{18,17},{25,26},{26,25}} | collective-permute-start | bytes 786440 | tf_op jit(solution)/shard_map/ppermute | solution.py:315
  47.5 6.5 %collective-permute-start.18 = (bf16[256,512]{1,0:T(8,128)(2,1)S(1)}, bf16[256,512]{1,0:T(8,128)(2,1)S(1)}, u32[]{:S(2)}, u32[]{:S(2)}) collective-permute-start(bf16[256,512]{1,0:T(8,128)(2,1)S(1)} %collective-permute-done.17), channel_id=1, source_target_pairs={{7,6},{4,5},{15,14},{12,13},{23,22},{20,21},{31,30},{28,29}} | collective-permute-start | bytes 786440 | tf_op jit(solution)/shard_map/ppermute | solution.py:315
  51.2 2.7 %collective-permute-start.22 = (bf16[256,384]{1,0:T(8,128)(2,1)S(1)}, bf16[256,384]{1,0:T(8,128)(2,1)S(1)}, u32[]{:S(2)}, u32[]{:S(2)}) collective-permute-start(bf16[256,384]{1,0:T(8,128)(2,1)S(1)} %collective-permute-done.21.refs_5_), channel_id=1, source_target_pairs={{0,4},{4,0},{8,12},{12,8},{16,20},{20,16},{24,28},{28,24},{1,5},{5... | collective-permute-start | bytes 589832 | tf_op jit(solution)/shard_map/ppermute | solution.py:280
  51.8 2.2 %collective-permute-start.25 = (bf16[256,384]{1,0:T(8,128)(2,1)S(1)}, bf16[256,384]{1,0:T(8,128)(2,1)S(1)}, u32[]{:S(2)}, u32[]{:S(2)}) collective-permute-start(bf16[256,384]{1,0:T(8,128)(2,1)S(1)} %collective-permute-done.24.refs_9_), channel_id=1, source_target_pairs={{0,4},{4,0},{8,12},{12,8},{16,20},{20,16},{24,28},{28,24},{1,5},{5... | collective-permute-start | bytes 589832 | tf_op jit(solution)/shard_map/ppermute | solution.py:280
  (7 other events, 20.5 us)

commit v4 on v3

--- a/solution.py
+++ b/solution.py
@@ -151,19 +151,6 @@
     )(normed)
 
 
-def load(sources, pieces, weights, sems):
-    started = []
-    for source, row, columns, place in pieces:
-        copy = pltpu.make_async_copy(
-            sources[source].at[pl.ds(row, weights.shape[0])],
-            weights.at[:, pl.ds(pl.multiple_of(place, TILE), columns)],
-            sems.at[len(started)],
-        )
-        copy.start()
-        started.append(copy)
-    return started
-
-
 def heads():
     for head in range(HEADS):
         ks = slice(head * HEAD_DIM, (head + 1) * HEAD_DIM)
@@ -207,8 +194,7 @@
 def attend_kernel(layout, count, arrivals, queries_ref, weighted_ref, mass_ref, *refs):
     near_ref, arrived, refs = refs[0], refs[1:arrivals], refs[arrivals:]
     sources = refs[:count]
-    mixed_ref, before, behind, attended, weights, blocks, sems, out_sems = refs[count:]
-    copies = load(sources, layout(), weights, sems)
+    mixed_ref, before, behind, attended, blocks, sems = refs[count:]
     tiles = queries_ref.shape[0] // TILE
     place = lax.axis_index("frame")
     far = arrived[0][...]
@@ -233,15 +219,14 @@
                 more, extra = share(queries_ref[rows, ks], ref[span, ks], ref[span, vs], flag)
                 weighted, mass = weighted + more, mass + extra
             attended[rows, ks] = (weighted / mass).astype(bf16)
-    for copy in copies:
-        copy.wait()
-    number, width = blocks.shape[0], blocks.shape[2]
+    width = blocks.shape[2]
     copies = []
-    for block in range(number):
-        columns = slice(block * width, (block + 1) * width)
-        blocks[block] = dot(attended[...], weights[:, columns]).astype(bf16)
+    for number, (source, begin, place) in enumerate(layout()):
+        blocks[number] = dot(attended[...], sources[source][:, begin : begin + width]).astype(bf16)
         copy = pltpu.make_async_copy(
-            blocks.at[block], mixed_ref.at[0, :, columns], out_sems.at[block]
+            blocks.at[number],
+            mixed_ref.at[0, :, pl.ds(pl.multiple_of(place, TILE), width)],
+            sems.at[number],
         )
         copy.start()
         copies.append(copy)
@@ -250,21 +235,19 @@
 
 
 def attend(layout, sources, queries, own, edges, model):
-    rows = queries.shape[0]
-    width = 4 * TILE if model % (4 * TILE) == 0 else TILE
+    rows, number = queries.shape[0], len(layout())
+    width = model // number
     return pl.pallas_call(
         functools.partial(attend_kernel, layout, len(sources), len(edges)),
-        in_specs=[VMEM] * (3 + len(edges)) + [ANY] * len(sources),
+        in_specs=[VMEM] * (3 + len(edges) + len(sources)),
         out_specs=ANY,
         out_shape=jax.ShapeDtypeStruct((1, rows, model), bf16),
         scratch_shapes=[
             pltpu.VMEM((BORDER, 2 * WIDTH), bf16),
             pltpu.VMEM((BORDER, 2 * WIDTH), bf16),
             pltpu.VMEM((rows, WIDTH), bf16),
-            pltpu.VMEM((WIDTH, model), bf16),
-            pltpu.VMEM((model // width, rows, width), bf16),
-            pltpu.SemaphoreType.DMA((len(layout()),)),
-            pltpu.SemaphoreType.DMA((model // width,)),
+            pltpu.VMEM((number, rows, width), bf16),
+            pltpu.SemaphoreType.DMA((number,)),
         ],
         compiler_params=params(),
         cost_estimate=pl.CostEstimate(
@@ -352,7 +335,7 @@
         chip, core, _ = where()
         place = 2 * chip + core
         return [
-            (source, 0, shard_columns, (place ^ (2 * k + here)) * shard_columns)
+            (source, 0, (place ^ (2 * k + here)) * shard_columns)
             for source, (k, here) in enumerate((k, here) for k in [0] + ring for here in (0, 1))
         ]
 
@@ -368,9 +351,6 @@
     late = [swap(x, "fsdp", 2) for x in come]
     one = jnp.concatenate(come, axis=0)
     one_rest = swap_plane(one, 0)
-    total = project(
-        [(normed, w_qkv), (normed, other_qkv)], qk_gain, (0, columns), "project_own", own_places
-    )
     nf, nb = len(front), len(back)
     homes = [[(4, nb), (5, 2 * nb), (2, 2 * nf + nb), (3, 0)]]
     homes += [[(0, i), (1, i), (2, i), (2, nf + i)] for i in range(nf)]
@@ -378,8 +358,8 @@
     widths = [quarter * n for n in (nf, nf, 2 * nf + nb + 1, 1, nb + 1, 2 * nb + 1)]
     arranged = arrange(shard_places, order, homes, widths, normed)
     next_part = lax.dynamic_slice_in_dim(w_qkv, (spot ^ 1) * quarter, quarter, 0)
-    one, one_rest, late, near, total, arranged, next_part = fence(
-        (one, one_rest, late, near, total, arranged, next_part)
+    one, one_rest, late, near, arranged, next_part = fence(
+        (one, one_rest, late, near, arranged, next_part)
     )
 
     late = jnp.concatenate(late + [near], axis=0)
@@ -387,10 +367,11 @@
     across = swap(next_part, "fsdp", 2)
     cut = 2 * (shard_columns // TILE) // 3 * TILE
     wides = [swap(w_out[:, :cut], "fsdp", 2 * k) for k in front]
-    one_other, one_rest_other = swap(one, "fsdp", 1), swap(one_rest, "fsdp", 1)
-    late_other = swap(late, "fsdp", 1)
-    two, across, late, one_other, one_rest_other, late_other, wides = fence(
-        (two, across, late, one_other, one_rest_other, late_other, wides)
+    total = project(
+        [(normed, w_qkv), (normed, other_qkv)], qk_gain, (0, columns), "project_own", own_places
+    )
+    two, across, late, one, one_rest, wides, total = fence(
+        (two, across, late, one, one_rest, wides, total)
     )
 
     relayed = two[2 * nf * quarter : (2 * nf + nb) * quarter]
@@ -398,8 +379,9 @@
         jnp.concatenate([late[: nb * quarter], relayed, late[nb * quarter :]], axis=0), 0
     )
     narrows = [swap(w_out[:, cut:], "fsdp", 2 * k) for k in front]
-    pieces = [one, one_other, one_rest, one_rest_other, two, swap(two, "fsdp", 1)]
-    pieces += [across, swap(across, "fsdp", 1), late, late_other]
+    pieces = []
+    for x in (one, one_rest, two, across, late):
+        pieces += [x, swap(x, "fsdp", 1)]
     total = project(
         list(zip(arranged[:10], pieces)), qk_gain, (0, columns), "project_mid", total=total
     )
@@ -427,7 +409,7 @@
         [(normed, rows)], qk_gain, (WIDTH, 2 * WIDTH), "project_keys_values", kinds=(1, None)
     )
     queries = project([(normed, rows)], qk_gain, (0, WIDTH), "project_queries", kinds=(0,))
-    return queries, stacked, halos(stacked), lambda: [(0, 0, columns.shape[1], 0)], [columns]
+    return queries, stacked, halos(stacked), lambda: [(0, i, i) for i in range(0, columns.shape[1], 3 * TILE)], [columns]
 
 
 def on_device(frames, modulation, w_qkv, qk_gain, w_out):

time: 57.6 us -> 55.4 us (0.962)
  waiting for transfers between devices: 15.6 us -> 12.5 us
  starting transfers between devices: 25.8 us -> 27.1 us
    ppermute x20, waiting for transfers between devices: 14.4 us -> 12.3 us  [swap(): lax.ppermute(x, axis, [(i, i ^ bits) for i in range(lax.axis_size(axis))])]
    ppermute x20, starting transfers between devices: 20.1 us -> 21.4 us  [swap(): lax.ppermute(x, axis, [(i, i ^ bits) for i in range(lax.axis_size(axis))])]
    ppermute x3, waiting for transfers between devices: 1.15 us -> 0.17 us  [swap_plane(): return lax.ppermute(x, ('fsdp', 'frame'), pairs)]
    unnamed x12 -> x11, local copies, waits for them, and re-layouts: 2.44 us -> 2.43 us
  transfers between devices with their start and end apart: 26 -> 26, of which waited for: 9 -> 11; matrix products, arithmetic and copies ran while one was open for 2% -> 0% of each run, Pallas kernels for 15% -> 16%
where the time goes in v4:
time: 55.4 us; the launch traced here: 54.8 us
  starting transfers between devices  27.1 us (49%)
  waiting for transfers between devices  12.5 us (23%)
  Pallas kernels  11.4 us (21%)
  local copies, waits for them, and re-layouts  3.54 us (6%)
    ppermute x20, starting transfers between devices, swap(): lax.ppermute(x, axis, [(i, i ^ bits) for i in range(lax.axis_size(axis))])  21.4 us
    ppermute x20, waiting for transfers between devices, swap(): lax.ppermute(x, axis, [(i, i ^ bits) for i in range(lax.axis_size(axis))])  12.3 us
    pallas_call x4, Pallas kernels, project(): pl.pallas_call(functools.partial(project_kernel, len(pairs), starts, kind...  3.87 us
    ppermute x3, starting transfers between devices, swap_plane(): return lax.ppermute(x, ('fsdp', 'frame'), pairs)  3.65 us
    pallas_call x1, Pallas kernels, attend(): pl.pallas_call(functools.partial(attend_kernel, layout, len(sources), len...  2.76 us
    unnamed x11, local copies, waits for them, and re-layouts  2.43 us
    pallas_call x1, Pallas kernels, norm_rows(): pl.pallas_call(norm_kernel, grid=(rows // block,), in_specs=[pl.BlockSpec...  2.15 us
    pallas_call x1, Pallas kernels, arrange(): pl.pallas_call(functools.partial(arrange_kernel, starts, order, homes), i...  1.44 us
  transfers between devices with their start and end apart: 26, of which 11 were waited for; matrix products, arithmetic and copies ran while one was open for 0% of the time, Pallas kernels for 16%

profile of v4, /device:TPU:0, one launch (start us, length us, event | category | flops | bytes accessed | tf_op | source)
XLA Modules:
  0.0 54.8 jit_solution(15672138862537269422)
XLA Ops:
  0.0 1.0 %constant_dynamic-slice_fusion.2 = (bf16[96,768]{1,0:T(8,128)(2,1)S(1)}, bf16[96,768]{1,0:T(8,128)(2,1)S(1)}) fusion(bf16[384,768]{1,0:T(8,128)(2,1)} %refs_2_.1, s32[]{:T(128)S(6)} %select_n.13, s32[]{:T(128)S(6)} %select_n.12), kind=kLoop, calls=%fused_computation.7 | loop fusion | bytes 589832 | tf_op jit(solution)/shard_map/dynamic_slice | solution.py:360
  1.0 5.1 %collective-permute-start = (bf16[96,768]{1,0:T(8,128)(2,1)S(1)}, bf16[96,768]{1,0:T(8,128)(2,1)S(1)}, u32[]{:S(2)}, u32[]{:S(2)}) collective-permute-start(bf16[96,768]{1,0:T(8,128)(2,1)S(1)} %get-tuple-element.98), channel_id=1, source_target_pairs={{0,24},{4,28},{8,16},{12,20},{16,8},{20,12},{24,0},{28,4},{1,25},{... | collective-permute-start | bytes 442376 | tf_op jit(solution)/shard_map/ppermute | solution.py:263
  6.1 1.7 %copy-done = bf16[1,384,3072]{2,1,0:T(8,128)(2,1)S(1)} copy-done((bf16[1,384,3072]{2,1,0:T(8,128)(2,1)S(1)}, bf16[1,384,3072]{2,1,0:T(8,128)(2,1)}, u32[]{:S(2)}) %copy-start) | copy-done | bytes 2359320
  7.8 0.7 %copy-done.3 = f32[1,2,3072]{2,1,0:T(2,128)S(1)} copy-done((f32[1,2,3072]{2,1,0:T(2,128)S(1)}, f32[1,2,3072]{2,1,0:T(2,128)}, u32[]{:S(2)}) %copy-start.3) | copy-done | bytes 24600
  8.5 2.2 %layer_norm.1.normed_ref.refs_0_.refs_1_ = bf16[384,3072]{1,0:T(8,128)(2,1)S(1)} custom-call(bf16[384,3072]{1,0:T(8,128)(2,1)S(1)} %bitcast.2, f32[2,3072]{1,0:T(2,128)S(1)} %bitcast.3), custom_call_target="tpu_custom_call" | custom-call | flops 11796480 | bytes 4718592 | tf_op jit(solution)/shard_map/layer_norm/pallas_call | solution.py:49
  10.8 1.7 %collective-permute-start.1 = (bf16[96,768]{1,0:T(8,128)(2,1)S(1)}, bf16[96,768]{1,0:T(8,128)(2,1)S(1)}, u32[]{:S(2)}, u32[]{:S(2)}) collective-permute-start(bf16[96,768]{1,0:T(8,128)(2,1)S(1)} %collective-permute-done.refs_10_), channel_id=1, source_target_pairs={{0,1},{1,0},{2,3},{3,2},{4,6},{5,7},{6,4},{7,5},{8,9},{9,8},{10,11... | collective-permute-start | bytes 442376 | tf_op jit(solution)/shard_map/ppermute | solution.py:272
  12.5 1.8 %collective-permute-start.2 = (bf16[96,768]{1,0:T(8,128)(2,1)S(1)}, bf16[96,768]{1,0:T(8,128)(2,1)S(1)}, u32[]{:S(2)}, u32[]{:S(2)}) collective-permute-start(bf16[96,768]{1,0:T(8,128)(2,1)S(1)} %collective-permute-done.refs_10_), channel_id=1, source_target_pairs={{0,8},{4,12},{8,0},{12,4},{16,24},{20,28},{24,16},{28,20},{1,9},{5... | collective-permute-start | bytes 442376 | tf_op jit(solution)/shard_map/ppermute | solution.py:263
  14.3 1.4 %arrange.1 = (bf16[384,96]{1,0:T(8,128)(2,1)S(1)}, bf16[384,96]{1,0:T(8,128)(2,1)S(1)}, bf16[384,96]{1,0:T(8,128)(2,1)S(1)}, bf16[384,96]{1,0:T(8,128)(2,1)S(1)}...) custom-call(bf16[384,3072]{1,0:T(8,128)(2,1)S(1)} %layer_norm.1.norm, ...), custom_call_target="tpu_custom_call" | custom-call | flops 1207959552 | bytes 4718592 | tf_op jit(solution)/shard_map/arrange/pallas_call | solution.py:140
  16.0 1.7 %collective-permute-done.2 = bf16[96,768]{1,0:T(8,128)(2,1)S(1)} collective-permute-done((bf16[96,768]{1,0:T(8,128)(2,1)S(1)}, bf16[96,768]{1,0:T(8,128)(2,1)S(1)}, u32[]{:S(2)}, u32[]{:S(2)}) %collective-permute-start.2) | collective-permute-done | bytes 147488 | tf_op jit(solution)/shard_map/ppermute | solution.py:263
  17.7 1.6 %collective-permute-start.4 = (bf16[384,768]{1,0:T(8,128)(2,1)S(1)}, bf16[384,768]{1,0:T(8,128)(2,1)S(1)}, u32[]{:S(2)}, u32[]{:S(2)}) collective-permute-start(bf16[384,768]{1,0:T(8,128)(2,1)S(1)} %pad_maximum_fusion), channel_id=1, source_target_pairs={{0,2},{1,3},{2,0},{3,1},{4,5},{5,4},{6,7},{7,6},{8,10},{9,11},{10,... | collective-permute-start | bytes 1769480 | tf_op jit(solution)/shard_map/ppermute | solution.py:272
  19.3 3.7 %collective-permute-start.6 = (bf16[256,256]{1,0:T(8,128)(2,1)S(1)}, bf16[256,256]{1,0:T(8,128)(2,1)S(1)}, u32[]{:S(2)}, u32[]{:S(2)}) collective-permute-start(bf16[256,256]{1,0:T(8,128)(2,1)S(1)} %slice.15), channel_id=1, source_target_pairs={{0,24},{4,28},{8,16},{12,20},{16,8},{20,12},{24,0},{28,4},{1,25},{... | collective-permute-start | bytes 393224 | tf_op jit(solution)/shard_map/ppermute | solution.py:263
  23.0 0.8 %project_own.1.refs_20_ = f32[384,768]{1,0:T(8,128)S(1)} custom-call(f32[2,128]{1,0:T(2,128)S(1)} %copy-done.4, bf16[384,3072]{1,0:T(8,128)(2,1)S(1)} %layer_norm.1.normed_ref.refs_0_.refs_1_, bf16[384,3072]{1,0:T(8,128)(2,1)S(1)} %layer_norm.1.normed_ref.refs_0_.refs_1_, bf16[384,768]{1,0:T(8,128)(2,1)S(1)} %copy-done.1, ...), custom_call_target="tpu_custom_call" | custom-call | flops 452984832 | bytes 1769472 | tf_op jit(solution)/shard_map/project_own/pallas_call | solution.py:100
  23.8 3.2 %collective-permute-done.6 = bf16[256,256]{1,0:T(8,128)(2,1)S(1)} collective-permute-done((bf16[256,256]{1,0:T(8,128)(2,1)S(1)}, bf16[256,256]{1,0:T(8,128)(2,1)S(1)}, u32[]{:S(2)}, u32[]{:S(2)}) %collective-permute-start.6) | collective-permute-done | bytes 131104 | tf_op jit(solution)/shard_map/ppermute | solution.py:263
  27.0 1.5 %collective-permute-done.5.refs_16_ = bf16[96,768]{1,0:T(8,128)(2,1)S(1)} collective-permute-done((bf16[96,768]{1,0:T(8,128)(2,1)S(1)}, bf16[96,768]{1,0:T(8,128)(2,1)S(1)}, u32[]{:S(2)}, u32[]{:S(2)}) %collective-permute-start.5) | collective-permute-done | bytes 147488 | tf_op jit(solution)/shard_map/ppermute | solution.py:263
  31.4 3.5 %collective-permute-start.14 = (bf16[256,128]{1,0:T(8,128)(2,1)S(1)}, bf16[256,128]{1,0:T(8,128)(2,1)S(1)}, u32[]{:S(2)}, u32[]{:S(2)}) collective-permute-start(bf16[256,128]{1,0:T(8,128)(2,1)S(1)} %slice.19), channel_id=1, source_target_pairs={{0,24},{4,28},{8,16},{12,20},{16,8},{20,12},{24,0},{28,4},{1,25},{... | collective-permute-start | bytes 196616 | tf_op jit(solution)/shard_map/ppermute | solution.py:263
  35.0 2.0 %project_mid.1.refs_4_ = f32[384,768]{1,0:T(8,128)S(1)} custom-call(f32[2,128]{1,0:T(2,128)S(1)} %copy-done.4, bf16[384,96]{1,0:T(8,128)(2,1)S(1)} %get-tuple-element.67.refs_0_, bf16[384,96]{1,0:T(8,128)(2,1)S(1)} %get-tuple-element.68.refs_1_, bf16[384,96]{1,0:T(8,128)(2,1)S(1)} %get-tuple-element.69.refs_2_, ...), custom_call_target="tpu_custom_call" | custom-call | flops 1019215872 | bytes 3981312 | tf_op jit(solution)/shard_map/project_mid/pallas_call | solution.py:100
  37.6 1.2 %collective-permute-start.21 = (bf16[256,384]{1,0:T(8,128)(2,1)S(1)}, bf16[256,384]{1,0:T(8,128)(2,1)S(1)}, u32[]{:S(2)}, u32[]{:S(2)}) collective-permute-start(bf16[256,384]{1,0:T(8,128)(2,1)S(1)} %copy-done.2), channel_id=1, source_target_pairs={{0,8},{4,12},{8,0},{12,4},{16,24},{20,28},{24,16},{28,20},{1,9},{5... | collective-permute-start | bytes 589832 | tf_op jit(solution)/shard_map/ppermute | solution.py:263
  40.1 0.7 %collective-permute-start.17 = (bf16[256,512]{1,0:T(8,128)(2,1)S(1)}, bf16[256,512]{1,0:T(8,128)(2,1)S(1)}, u32[]{:S(2)}, u32[]{:S(2)}) collective-permute-start(bf16[256,512]{1,0:T(8,128)(2,1)S(1)} %get-tuple-element.99), channel_id=1, source_target_pairs={{5,7},{6,4},{13,15},{14,12},{21,23},{22,20},{29,31},{30,28}} | collective-permute-start | bytes 786440 | tf_op jit(solution)/shard_map/ppermute | solution.py:297
  40.8 1.4 %collective-permute-start.16 = (bf16[256,512]{1,0:T(8,128)(2,1)S(1)}, bf16[256,512]{1,0:T(8,128)(2,1)S(1)}, u32[]{:S(2)}, u32[]{:S(2)}) collective-permute-start(bf16[256,512]{1,0:T(8,128)(2,1)S(1)} %get-tuple-element.100), channel_id=1, source_target_pairs={{0,1},{1,0},{2,3},{3,2},{4,5},{5,4},{6,7},{7,6},{8,9},{9,8},{10,11... | collective-permute-start | bytes 786440 | tf_op jit(solution)/shard_map/ppermute | solution.py:263
  42.5 2.3 %collective-permute-start.20 = (bf16[256,384]{1,0:T(8,128)(2,1)S(1)}, bf16[256,384]{1,0:T(8,128)(2,1)S(1)}, u32[]{:S(2)}, u32[]{:S(2)}) collective-permute-start(bf16[256,384]{1,0:T(8,128)(2,1)S(1)} %copy-done.2), channel_id=1, source_target_pairs={{0,4},{4,0},{8,12},{12,8},{16,20},{20,16},{24,28},{28,24},{1,5},{5... | collective-permute-start | bytes 589832 | tf_op jit(solution)/shard_map/ppermute | solution.py:263
  45.6 0.7 %collective-permute-start.18 = (bf16[256,512]{1,0:T(8,128)(2,1)S(1)}, bf16[256,512]{1,0:T(8,128)(2,1)S(1)}, u32[]{:S(2)}, u32[]{:S(2)}) collective-permute-start(bf16[256,512]{1,0:T(8,128)(2,1)S(1)} %collective-permute-done.17), channel_id=1, source_target_pairs={{7,6},{4,5},{15,14},{12,13},{23,22},{20,21},{31,30},{28,29}} | collective-permute-start | bytes 786440 | tf_op jit(solution)/shard_map/ppermute | solution.py:298
  46.3 3.4 %collective-permute-done.16.refs_0_ = bf16[256,512]{1,0:T(8,128)(2,1)S(1)} collective-permute-done((bf16[256,512]{1,0:T(8,128)(2,1)S(1)}, bf16[256,512]{1,0:T(8,128)(2,1)S(1)}, u32[]{:S(2)}, u32[]{:S(2)}) %collective-permute-start.16) | collective-permute-done | bytes 262176 | tf_op jit(solution)/shard_map/ppermute | solution.py:263
  50.8 1.2 %attend_own_slab.1 = (f32[384,256]{1,0:T(8,128)S(1)}, f32[384,256]{1,0:T(8,128)S(1)}) custom-call(bf16[384,256]{1,0:T(8,128)(2,1)S(1)} %project_queries.1.queries_ref, bf16[384,512]{1,0:T(8,128)(2,1)S(1)} %project_keys_values.1.stacked_ref), custom_call_target="tpu_custom_call" | custom-call | flops 150994944 | bytes 1376256 | tf_op jit(solution)/shard_map/attend_own_slab/pallas_call | solution.py:180
  52.1 2.8 %attend_and_mix.1 = bf16[1,384,3072]{2,1,0:T(8,128)(2,1)} custom-call(bf16[384,256]{1,0:T(8,128)(2,1)S(1)} %project_queries.1.queries_ref, f32[384,256]{1,0:T(8,128)S(1)} %get-tuple-element.90.weighted_ref, f32[384,256]{1,0:T(8,128)S(1)} %get-tuple-element.91.mass_ref, bf16[256,512]{1,0:T(8,128)(2,1)S(1)} %collective-permute-done.16.refs_0_, ...), custom_call_target="tpu_custom_call" | custom-call | flops 704643072 | bytes 3932160 | tf_op jit(solution)/shard_map/attend_and_mix/pallas_call | solution.py:240
  (57 shorter events, 7.4 us)
Async XLA Ops:
  1.0 9.8 %collective-permute-start = (bf16[96,768]{1,0:T(8,128)(2,1)S(1)}, bf16[96,768]{1,0:T(8,128)(2,1)S(1)}, u32[]{:S(2)}, u32[]{:S(2)}) collective-permute-start(bf16[96,768]{1,0:T(8,128)(2,1)S(1)} %get-tuple-element.98), channel_id=1, source_target_pairs={{0,24},{4,28},{8,16},{12,20},{16,8},{20,12},{24,0},{28,4},{1,25},{... | collective-permute-start | bytes 442376 | tf_op jit(solution)/shard_map/ppermute | solution.py:263
  6.1 9.7 %collective-permute-start.3 = (bf16[96,768]{1,0:T(8,128)(2,1)S(1)}, bf16[96,768]{1,0:T(8,128)(2,1)S(1)}, u32[]{:S(2)}, u32[]{:S(2)}) collective-permute-start(bf16[96,768]{1,0:T(8,128)(2,1)S(1)} %get-tuple-element.98), channel_id=1, source_target_pairs={{0,8},{4,12},{8,0},{12,4},{16,24},{20,28},{24,16},{28,20},{1,9},{5... | collective-permute-start | bytes 442376 | tf_op jit(solution)/shard_map/ppermute | solution.py:263
  10.8 5.1 %collective-permute-start.1 = (bf16[96,768]{1,0:T(8,128)(2,1)S(1)}, bf16[96,768]{1,0:T(8,128)(2,1)S(1)}, u32[]{:S(2)}, u32[]{:S(2)}) collective-permute-start(bf16[96,768]{1,0:T(8,128)(2,1)S(1)} %collective-permute-done.refs_10_), channel_id=1, source_target_pairs={{0,1},{1,0},{2,3},{3,2},{4,6},{5,7},{6,4},{7,5},{8,9},{9,8},{10,11... | collective-permute-start | bytes 442376 | tf_op jit(solution)/shard_map/ppermute | solution.py:272
  12.5 5.1 %collective-permute-start.2 = (bf16[96,768]{1,0:T(8,128)(2,1)S(1)}, bf16[96,768]{1,0:T(8,128)(2,1)S(1)}, u32[]{:S(2)}, u32[]{:S(2)}) collective-permute-start(bf16[96,768]{1,0:T(8,128)(2,1)S(1)} %collective-permute-done.refs_10_), channel_id=1, source_target_pairs={{0,8},{4,12},{8,0},{12,4},{16,24},{20,28},{24,16},{28,20},{1,9},{5... | collective-permute-start | bytes 442376 | tf_op jit(solution)/shard_map/ppermute | solution.py:263
  14.3 8.7 %collective-permute-start.7 = (bf16[384,768]{1,0:T(8,128)(2,1)S(1)}, bf16[384,768]{1,0:T(8,128)(2,1)S(1)}, u32[]{:S(2)}, u32[]{:S(2)}) collective-permute-start(bf16[384,768]{1,0:T(8,128)(2,1)S(1)} %copy-done.1), channel_id=1, source_target_pairs={{0,4},{4,0},{8,12},{12,8},{16,20},{20,16},{24,28},{28,24},{1,5},{5... | collective-permute-start | bytes 1769480 | tf_op jit(solution)/shard_map/ppermute | solution.py:263
  17.7 10.9 %collective-permute-start.4 = (bf16[384,768]{1,0:T(8,128)(2,1)S(1)}, bf16[384,768]{1,0:T(8,128)(2,1)S(1)}, u32[]{:S(2)}, u32[]{:S(2)}) collective-permute-start(bf16[384,768]{1,0:T(8,128)(2,1)S(1)} %pad_maximum_fusion), channel_id=1, source_target_pairs={{0,2},{1,3},{2,0},{3,1},{4,5},{5,4},{6,7},{7,6},{8,10},{9,11},{10,... | collective-permute-start | bytes 1769480 | tf_op jit(solution)/shard_map/ppermute | solution.py:272
  19.3 7.7 %collective-permute-start.6 = (bf16[256,256]{1,0:T(8,128)(2,1)S(1)}, bf16[256,256]{1,0:T(8,128)(2,1)S(1)}, u32[]{:S(2)}, u32[]{:S(2)}) collective-permute-start(bf16[256,256]{1,0:T(8,128)(2,1)S(1)} %slice.15), channel_id=1, source_target_pairs={{0,24},{4,28},{8,16},{12,20},{16,8},{20,12},{24,0},{28,4},{1,25},{... | collective-permute-start | bytes 393224 | tf_op jit(solution)/shard_map/ppermute | solution.py:263
  23.0 5.6 %collective-permute-start.5 = (bf16[96,768]{1,0:T(8,128)(2,1)S(1)}, bf16[96,768]{1,0:T(8,128)(2,1)S(1)}, u32[]{:S(2)}, u32[]{:S(2)}) collective-permute-start(bf16[96,768]{1,0:T(8,128)(2,1)S(1)} %get-tuple-element.81), channel_id=1, source_target_pairs={{0,8},{4,12},{8,0},{12,4},{16,24},{20,28},{24,16},{28,20},{1,9},{5... | collective-permute-start | bytes 442376 | tf_op jit(solution)/shard_map/ppermute | solution.py:263
  28.6 6.4 %collective-permute-start.10 = (bf16[384,768]{1,0:T(8,128)(2,1)S(1)}, bf16[384,768]{1,0:T(8,128)(2,1)S(1)}, u32[]{:S(2)}, u32[]{:S(2)}) collective-permute-start(bf16[384,768]{1,0:T(8,128)(2,1)S(1)} %collective-permute-done.4.refs_14_), channel_id=1, source_target_pairs={{0,4},{4,0},{8,12},{12,8},{16,20},{20,16},{24,28},{28,24},{1,5},{5... | collective-permute-start | bytes 1769480 | tf_op jit(solution)/shard_map/ppermute | solution.py:263
  28.7 8.9 %collective-permute-start.13 = (bf16[288,768]{1,0:T(8,128)(2,1)S(1)}, bf16[288,768]{1,0:T(8,128)(2,1)S(1)}, u32[]{:S(2)}, u32[]{:S(2)}) collective-permute-start(bf16[288,768]{1,0:T(8,128)(2,1)S(1)} %pad_maximum_fusion.1), channel_id=1, source_target_pairs={{0,1},{1,0},{2,3},{3,2},{4,6},{5,7},{6,4},{7,5},{8,9},{9,8},{10,11... | collective-permute-start | bytes 1327112 | tf_op jit(solution)/shard_map/ppermute | solution.py:272
  29.7 5.3 %collective-permute-start.12 = (bf16[192,768]{1,0:T(8,128)(2,1)S(1)}, bf16[192,768]{1,0:T(8,128)(2,1)S(1)}, u32[]{:S(2)}, u32[]{:S(2)}) collective-permute-start(bf16[192,768]{1,0:T(8,128)(2,1)S(1)} %pad_maximum_fusion.2.refs_18_), channel_id=1, source_target_pairs={{0,4},{4,0},{8,12},{12,8},{16,20},{20,16},{24,28},{28,24},{1,5},{5... | collective-permute-start | bytes 884744 | tf_op jit(solution)/shard_map/ppermute | solution.py:263
  30.8 4.2 %collective-permute-start.11 = (bf16[96,768]{1,0:T(8,128)(2,1)S(1)}, bf16[96,768]{1,0:T(8,128)(2,1)S(1)}, u32[]{:S(2)}, u32[]{:S(2)}) collective-permute-start(bf16[96,768]{1,0:T(8,128)(2,1)S(1)} %collective-permute-done.5.refs_16_), channel_id=1, source_target_pairs={{0,4},{4,0},{8,12},{12,8},{16,20},{20,16},{24,28},{28,24},{1,5},{5... | collective-permute-start | bytes 442376 | tf_op jit(solution)/shard_map/ppermute | solution.py:263
  31.4 6.1 %collective-permute-start.14 = (bf16[256,128]{1,0:T(8,128)(2,1)S(1)}, bf16[256,128]{1,0:T(8,128)(2,1)S(1)}, u32[]{:S(2)}, u32[]{:S(2)}) collective-permute-start(bf16[256,128]{1,0:T(8,128)(2,1)S(1)} %slice.19), channel_id=1, source_target_pairs={{0,24},{4,28},{8,16},{12,20},{16,8},{20,12},{24,0},{28,4},{1,25},{... | collective-permute-start | bytes 196616 | tf_op jit(solution)/shard_map/ppermute | solution.py:263
  37.6 1.8 %collective-permute-start.15 = (bf16[288,768]{1,0:T(8,128)(2,1)S(1)}, bf16[288,768]{1,0:T(8,128)(2,1)S(1)}, u32[]{:S(2)}, u32[]{:S(2)}) collective-permute-start(bf16[288,768]{1,0:T(8,128)(2,1)S(1)} %collective-permute-done.13.refs_2_), channel_id=1, source_target_pairs={{0,4},{4,0},{8,12},{12,8},{16,20},{20,16},{24,28},{28,24},{1,5},{5... | collective-permute-start | bytes 1327112 | tf_op jit(solution)/shard_map/ppermute | solution.py:263
  37.6 7.3 %collective-permute-start.21 = (bf16[256,384]{1,0:T(8,128)(2,1)S(1)}, bf16[256,384]{1,0:T(8,128)(2,1)S(1)}, u32[]{:S(2)}, u32[]{:S(2)}) collective-permute-start(bf16[256,384]{1,0:T(8,128)(2,1)S(1)} %copy-done.2), channel_id=1, source_target_pairs={{0,8},{4,12},{8,0},{12,4},{16,24},{20,28},{24,16},{28,20},{1,9},{5... | collective-permute-start | bytes 589832 | tf_op jit(solution)/shard_map/ppermute | solution.py:263
  40.1 5.5 %collective-permute-start.17 = (bf16[256,512]{1,0:T(8,128)(2,1)S(1)}, bf16[256,512]{1,0:T(8,128)(2,1)S(1)}, u32[]{:S(2)}, u32[]{:S(2)}) collective-permute-start(bf16[256,512]{1,0:T(8,128)(2,1)S(1)} %get-tuple-element.99), channel_id=1, source_target_pairs={{5,7},{6,4},{13,15},{14,12},{21,23},{22,20},{29,31},{30,28}} | collective-permute-start | bytes 786440 | tf_op jit(solution)/shard_map/ppermute | solution.py:297
  40.8 8.8 %collective-permute-start.16 = (bf16[256,512]{1,0:T(8,128)(2,1)S(1)}, bf16[256,512]{1,0:T(8,128)(2,1)S(1)}, u32[]{:S(2)}, u32[]{:S(2)}) collective-permute-start(bf16[256,512]{1,0:T(8,128)(2,1)S(1)} %get-tuple-element.100), channel_id=1, source_target_pairs={{0,1},{1,0},{2,3},{3,2},{4,5},{5,4},{6,7},{7,6},{8,9},{9,8},{10,11... | collective-permute-start | bytes 786440 | tf_op jit(solution)/shard_map/ppermute | solution.py:263
  42.2 7.7 %collective-permute-start.24 = (bf16[256,384]{1,0:T(8,128)(2,1)S(1)}, bf16[256,384]{1,0:T(8,128)(2,1)S(1)}, u32[]{:S(2)}, u32[]{:S(2)}) collective-permute-start(bf16[256,384]{1,0:T(8,128)(2,1)S(1)} %constant_dynamic-update-slice_fusion.refs_7_), channel_id=1, source_target_pairs={{0,8},{4,12},{8,0},{12,4},{16,24},{20,28},{24,16},{28,20},{1,9},{5... | collective-permute-start | bytes 589832 | tf_op jit(solution)/shard_map/ppermute | solution.py:263
  42.5 7.7 %collective-permute-start.20 = (bf16[256,384]{1,0:T(8,128)(2,1)S(1)}, bf16[256,384]{1,0:T(8,128)(2,1)S(1)}, u32[]{:S(2)}, u32[]{:S(2)}) collective-permute-start(bf16[256,384]{1,0:T(8,128)(2,1)S(1)} %copy-done.2), channel_id=1, source_target_pairs={{0,4},{4,0},{8,12},{12,8},{16,20},{20,16},{24,28},{28,24},{1,5},{5... | collective-permute-start | bytes 589832 | tf_op jit(solution)/shard_map/ppermute | solution.py:263
  44.9 7.1 %collective-permute-start.19 = (bf16[256,512]{1,0:T(8,128)(2,1)S(1)}, bf16[256,512]{1,0:T(8,128)(2,1)S(1)}, u32[]{:S(2)}, u32[]{:S(2)}) collective-permute-start(bf16[256,512]{1,0:T(8,128)(2,1)S(1)} %get-tuple-element.99), channel_id=1, source_target_pairs={{1,2},{2,1},{9,10},{10,9},{17,18},{18,17},{25,26},{26,25}} | collective-permute-start | bytes 786440 | tf_op jit(solution)/shard_map/ppermute | solution.py:298
  45.6 6.5 %collective-permute-start.18 = (bf16[256,512]{1,0:T(8,128)(2,1)S(1)}, bf16[256,512]{1,0:T(8,128)(2,1)S(1)}, u32[]{:S(2)}, u32[]{:S(2)}) collective-permute-start(bf16[256,512]{1,0:T(8,128)(2,1)S(1)} %collective-permute-done.17), channel_id=1, source_target_pairs={{7,6},{4,5},{15,14},{12,13},{23,22},{20,21},{31,30},{28,29}} | collective-permute-start | bytes 786440 | tf_op jit(solution)/shard_map/ppermute | solution.py:298
  49.6 2.4 %collective-permute-start.22 = (bf16[256,384]{1,0:T(8,128)(2,1)S(1)}, bf16[256,384]{1,0:T(8,128)(2,1)S(1)}, u32[]{:S(2)}, u32[]{:S(2)}) collective-permute-start(bf16[256,384]{1,0:T(8,128)(2,1)S(1)} %collective-permute-done.21.refs_5_), channel_id=1, source_target_pairs={{0,4},{4,0},{8,12},{12,8},{16,20},{20,16},{24,28},{28,24},{1,5},{5... | collective-permute-start | bytes 589832 | tf_op jit(solution)/shard_map/ppermute | solution.py:263
  49.9 2.2 %collective-permute-start.23 = (bf16[256,384]{1,0:T(8,128)(2,1)S(1)}, bf16[256,384]{1,0:T(8,128)(2,1)S(1)}, u32[]{:S(2)}, u32[]{:S(2)}) collective-permute-start(bf16[256,384]{1,0:T(8,128)(2,1)S(1)} %constant_dynamic-update-slice_fusion.refs_7_), channel_id=1, source_target_pairs={{0,4},{4,0},{8,12},{12,8},{16,20},{20,16},{24,28},{28,24},{1,5},{5... | collective-permute-start | bytes 589832 | tf_op jit(solution)/shard_map/ppermute | solution.py:263
  50.2 1.9 %collective-permute-start.25 = (bf16[256,384]{1,0:T(8,128)(2,1)S(1)}, bf16[256,384]{1,0:T(8,128)(2,1)S(1)}, u32[]{:S(2)}, u32[]{:S(2)}) collective-permute-start(bf16[256,384]{1,0:T(8,128)(2,1)S(1)} %collective-permute-done.24.refs_9_), channel_id=1, source_target_pairs={{0,4},{4,0},{8,12},{12,8},{16,20},{20,16},{24,28},{28,24},{1,5},{5... | collective-permute-start | bytes 589832 | tf_op jit(solution)/shard_map/ppermute | solution.py:263
  (7 other events, 22.5 us)

commit v5 on v4

--- a/solution.py
+++ b/solution.py
@@ -299,7 +299,7 @@
     if places > 4:
         pairs = [(j, j + 1) for j in range(3, places - 1, 4)]
         arrived.append(lax.ppermute(far, "frame", pairs + [(b, a) for a, b in pairs]))
-    return [swap(near, "frame", 1)] + arrived
+    return [swap(near, "frame", 1)] + arrived, way
 
 
 def split_plan(frames, modulation, w_qkv, w_out, qk_gain):
@@ -352,10 +352,10 @@
     one = jnp.concatenate(come, axis=0)
     one_rest = swap_plane(one, 0)
     nf, nb = len(front), len(back)
-    homes = [[(4, nb), (5, 2 * nb), (2, 2 * nf + nb), (3, 0)]]
-    homes += [[(0, i), (1, i), (2, i), (2, nf + i)] for i in range(nf)]
-    homes += [[(4, i), (5, i), (2, 2 * nf + i), (5, nb + i)] for i in range(nb)]
-    widths = [quarter * n for n in (nf, nf, 2 * nf + nb + 1, 1, nb + 1, 2 * nb + 1)]
+    homes = [[(0, 2 * nf + nb), (2, 2 * nb), (1, 2 * nf + nb), (0, 2 * nf + nb + 1)]]
+    homes += [[(0, i), (0, nf + i), (1, i), (1, nf + i)] for i in range(nf)]
+    homes += [[(0, 2 * nf + i), (2, i), (1, 2 * nf + i), (2, nb + i)] for i in range(nb)]
+    widths = [quarter * n for n in (2 * nf + nb + 2, 2 * nf + nb + 1, 2 * nb + 1)]
     arranged = arrange(shard_places, order, homes, widths, normed)
     next_part = lax.dynamic_slice_in_dim(w_qkv, (spot ^ 1) * quarter, quarter, 0)
     one, one_rest, late, near, arranged, next_part = fence(
@@ -379,15 +379,14 @@
         jnp.concatenate([late[: nb * quarter], relayed, late[nb * quarter :]], axis=0), 0
     )
     narrows = [swap(w_out[:, cut:], "fsdp", 2 * k) for k in front]
-    pieces = []
-    for x in (one, one_rest, two, across, late):
-        pieces += [x, swap(x, "fsdp", 1)]
+    kept = jnp.concatenate([one, one_rest, late, across], axis=0)
+    pieces = [kept, swap(kept, "fsdp", 1), two, swap(two, "fsdp", 1)]
     total = project(
-        list(zip(arranged[:10], pieces)), qk_gain, (0, columns), "project_mid", total=total
+        list(zip(arranged[:4], pieces)), qk_gain, (0, columns), "project_mid", total=total
     )
     total, three, narrows = fence((total, three, narrows))
 
-    last = [(arranged[10], three), (arranged[11], swap(three, "fsdp", 1))]
+    last = [(arranged[4], three), (arranged[5], swap(three, "fsdp", 1))]
     stacked = project(
         last, qk_gain, (WIDTH, 2 * WIDTH), "project_keys_values", kinds=(1, None), total=total
     )
@@ -395,9 +394,9 @@
 
     joined = [jnp.concatenate(pair, axis=1) for pair in zip(wides, narrows)]
     sources = [w_out, other_out]
-    edges = halos(stacked)
+    edges, way = halos(stacked)
     for x in [swap(w_out, "fsdp", 2)] + joined + [swap(x, "fsdp", 2) for x in joined]:
-        sources += [x, swap(fence((x, edges[0]))[0], "fsdp", 1)]
+        sources += [x, swap(fence((x, way))[0], "fsdp", 1)]
     return queries, stacked, edges, out_layout, sources
 
 
@@ -409,7 +408,7 @@
         [(normed, rows)], qk_gain, (WIDTH, 2 * WIDTH), "project_keys_values", kinds=(1, None)
     )
     queries = project([(normed, rows)], qk_gain, (0, WIDTH), "project_queries", kinds=(0,))
-    return queries, stacked, halos(stacked), lambda: [(0, i, i) for i in range(0, columns.shape[1], 3 * TILE)], [columns]
+    return queries, stacked, halos(stacked)[0], lambda: [(0, i, i) for i in range(0, columns.shape[1], 3 * TILE)], [columns]
 
 
 def on_device(frames, modulation, w_qkv, qk_gain, w_out):

time: 55.4 us -> 55.1 us (level)
  waiting for transfers between devices: 12.5 us -> 14.1 us
  starting transfers between devices: 27.1 us -> 25.8 us
  Pallas kernels: 11.4 us -> 10.8 us
    ppermute x3, waiting for transfers between devices: 0.17 us -> 2.05 us  [swap_plane(): return lax.ppermute(x, ('fsdp', 'frame'), pairs)]
    ppermute x20 -> x17, starting transfers between devices: 21.4 us -> 20.1 us  [swap(): lax.ppermute(x, axis, [(i, i ^ bits) for i in range(lax.axis_size(axis))])]
    pallas_call x4, Pallas kernels: 3.87 us -> 3.26 us  [project(): pl.pallas_call(functools.partial(project_kernel, len(pairs), starts, kind...]
    ppermute x20 -> x17, waiting for transfers between devices: 12.3 us -> 12.1 us  [swap(): lax.ppermute(x, axis, [(i, i ^ bits) for i in range(lax.axis_size(axis))])]
    unnamed x11 -> x14, local copies, waits for them, and re-layouts: 2.43 us -> 2.47 us
  transfers between devices with their start and end apart: 26 -> 23, of which waited for: 11 -> 11; matrix products, arithmetic and copies ran while one was open for 0% -> 0% of each run, Pallas kernels for 16% -> 15%
where the time goes in v5:
time: 55.1 us; the launch traced here: 54.6 us
  starting transfers between devices  25.8 us (47%)
  waiting for transfers between devices  14.1 us (26%)
  Pallas kernels  10.8 us (20%)
  local copies, waits for them, and re-layouts  3.6 us (7%)
    ppermute x17, starting transfers between devices, swap(): lax.ppermute(x, axis, [(i, i ^ bits) for i in range(lax.axis_size(axis))])  20.1 us
    ppermute x17, waiting for transfers between devices, swap(): lax.ppermute(x, axis, [(i, i ^ bits) for i in range(lax.axis_size(axis))])  12.1 us
    ppermute x3, starting transfers between devices, swap_plane(): return lax.ppermute(x, ('fsdp', 'frame'), pairs)  3.65 us
    pallas_call x4, Pallas kernels, project(): pl.pallas_call(functools.partial(project_kernel, len(pairs), starts, kind...  3.26 us
    pallas_call x1, Pallas kernels, attend(): pl.pallas_call(functools.partial(attend_kernel, layout, len(sources), len...  2.76 us
    unnamed x14, local copies, waits for them, and re-layouts  2.47 us
    pallas_call x1, Pallas kernels, norm_rows(): pl.pallas_call(norm_kernel, grid=(rows // block,), in_specs=[pl.BlockSpec...  2.15 us
    ppermute x3, waiting for transfers between devices, swap_plane(): return lax.ppermute(x, ('fsdp', 'frame'), pairs)  2.05 us
  transfers between devices with their start and end apart: 23, of which 11 were waited for; matrix products, arithmetic and copies ran while one was open for 0% of the time, Pallas kernels for 15%

profile of v5, /device:TPU:0, one launch (start us, length us, event | category | flops | bytes accessed | tf_op | source)
XLA Modules:
  0.0 54.6 jit_solution(12114704145795179329)
XLA Ops:
  0.0 1.0 %constant_dynamic-slice_fusion.2 = (bf16[96,768]{1,0:T(8,128)(2,1)S(1)}, bf16[96,768]{1,0:T(8,128)(2,1)S(1)}) fusion(bf16[384,768]{1,0:T(8,128)(2,1)} %refs_2_.1, s32[]{:T(128)S(6)} %select_n.13, s32[]{:T(128)S(6)} %select_n.12), kind=kLoop, calls=%fused_computation.11 | loop fusion | bytes 589832 | tf_op jit(solution)/shard_map/dynamic_slice | solution.py:360
  1.0 5.1 %collective-permute-start = (bf16[96,768]{1,0:T(8,128)(2,1)S(1)}, bf16[96,768]{1,0:T(8,128)(2,1)S(1)}, u32[]{:S(2)}, u32[]{:S(2)}) collective-permute-start(bf16[96,768]{1,0:T(8,128)(2,1)S(1)} %get-tuple-element.74), channel_id=1, source_target_pairs={{0,24},{4,28},{8,16},{12,20},{16,8},{20,12},{24,0},{28,4},{1,25},{... | collective-permute-start | bytes 442376 | tf_op jit(solution)/shard_map/ppermute | solution.py:263
  6.1 1.7 %copy-done = bf16[1,384,3072]{2,1,0:T(8,128)(2,1)S(1)} copy-done((bf16[1,384,3072]{2,1,0:T(8,128)(2,1)S(1)}, bf16[1,384,3072]{2,1,0:T(8,128)(2,1)}, u32[]{:S(2)}) %copy-start) | copy-done | bytes 2359320
  8.5 2.2 %layer_norm.1.normed_ref.refs_0_.refs_1_ = bf16[384,3072]{1,0:T(8,128)(2,1)S(1)} custom-call(bf16[384,3072]{1,0:T(8,128)(2,1)S(1)} %bitcast.2, f32[2,3072]{1,0:T(2,128)S(1)} %bitcast.3), custom_call_target="tpu_custom_call" | custom-call | flops 11796480 | bytes 4718592 | tf_op jit(solution)/shard_map/layer_norm/pallas_call | solution.py:49
  10.8 1.7 %collective-permute-start.1 = (bf16[96,768]{1,0:T(8,128)(2,1)S(1)}, bf16[96,768]{1,0:T(8,128)(2,1)S(1)}, u32[]{:S(2)}, u32[]{:S(2)}) collective-permute-start(bf16[96,768]{1,0:T(8,128)(2,1)S(1)} %collective-permute-done), channel_id=1, source_target_pairs={{0,1},{1,0},{2,3},{3,2},{4,6},{5,7},{6,4},{7,5},{8,9},{9,8},{10,11... | collective-permute-start | bytes 442376 | tf_op jit(solution)/shard_map/ppermute | solution.py:272
  12.5 1.8 %collective-permute-start.2 = (bf16[96,768]{1,0:T(8,128)(2,1)S(1)}, bf16[96,768]{1,0:T(8,128)(2,1)S(1)}, u32[]{:S(2)}, u32[]{:S(2)}) collective-permute-start(bf16[96,768]{1,0:T(8,128)(2,1)S(1)} %collective-permute-done), channel_id=1, source_target_pairs={{0,8},{4,12},{8,0},{12,4},{16,24},{20,28},{24,16},{28,20},{1,9},{5... | collective-permute-start | bytes 442376 | tf_op jit(solution)/shard_map/ppermute | solution.py:263
  14.3 1.4 %arrange.1 = (bf16[384,480]{1,0:T(8,128)(2,1)S(1)}, bf16[384,480]{1,0:T(8,128)(2,1)S(1)}, bf16[384,384]{1,0:T(8,128)(2,1)S(1)}, bf16[384,384]{1,0:T(8,128)(2,1)S...) custom-call(bf16[384,3072]{1,0:T(8,128)(2,1)S(1)} %layer_norm.1.normed_ref.refs_0_.refs_1_), custom_call_target="tpu_custom_call" | custom-call | flops 1207959552 | bytes 4718592 | tf_op jit(solution)/shard_map/arrange/pallas_call | solution.py:140
  16.0 1.7 %collective-permute-done.2 = bf16[96,768]{1,0:T(8,128)(2,1)S(1)} collective-permute-done((bf16[96,768]{1,0:T(8,128)(2,1)S(1)}, bf16[96,768]{1,0:T(8,128)(2,1)S(1)}, u32[]{:S(2)}, u32[]{:S(2)}) %collective-permute-start.2) | collective-permute-done | bytes 147488 | tf_op jit(solution)/shard_map/ppermute | solution.py:263
  17.7 1.6 %collective-permute-start.4 = (bf16[384,768]{1,0:T(8,128)(2,1)S(1)}, bf16[384,768]{1,0:T(8,128)(2,1)S(1)}, u32[]{:S(2)}, u32[]{:S(2)}) collective-permute-start(bf16[384,768]{1,0:T(8,128)(2,1)S(1)} %pad_maximum_fusion), channel_id=1, source_target_pairs={{0,2},{1,3},{2,0},{3,1},{4,5},{5,4},{6,7},{7,6},{8,10},{9,11},{10,... | collective-permute-start | bytes 1769480 | tf_op jit(solution)/shard_map/ppermute | solution.py:272
  19.3 3.7 %collective-permute-start.6 = (bf16[256,256]{1,0:T(8,128)(2,1)S(1)}, bf16[256,256]{1,0:T(8,128)(2,1)S(1)}, u32[]{:S(2)}, u32[]{:S(2)}) collective-permute-start(bf16[256,256]{1,0:T(8,128)(2,1)S(1)} %slice.15), channel_id=1, source_target_pairs={{0,24},{4,28},{8,16},{12,20},{16,8},{20,12},{24,0},{28,4},{1,25},{... | collective-permute-start | bytes 393224 | tf_op jit(solution)/shard_map/ppermute | solution.py:263
  23.8 3.2 %collective-permute-done.6 = bf16[256,256]{1,0:T(8,128)(2,1)S(1)} collective-permute-done((bf16[256,256]{1,0:T(8,128)(2,1)S(1)}, bf16[256,256]{1,0:T(8,128)(2,1)S(1)}, u32[]{:S(2)}, u32[]{:S(2)}) %collective-permute-start.6) | collective-permute-done | bytes 131104 | tf_op jit(solution)/shard_map/ppermute | solution.py:263
  27.0 1.5 %collective-permute-done.5 = bf16[96,768]{1,0:T(8,128)(2,1)S(1)} collective-permute-done((bf16[96,768]{1,0:T(8,128)(2,1)S(1)}, bf16[96,768]{1,0:T(8,128)(2,1)S(1)}, u32[]{:S(2)}, u32[]{:S(2)}) %collective-permute-start.5) | collective-permute-done | bytes 147488 | tf_op jit(solution)/shard_map/ppermute | solution.py:263
  29.7 2.9 %collective-permute-start.11 = (bf16[256,128]{1,0:T(8,128)(2,1)S(1)}, bf16[256,128]{1,0:T(8,128)(2,1)S(1)}, u32[]{:S(2)}, u32[]{:S(2)}) collective-permute-start(bf16[256,128]{1,0:T(8,128)(2,1)S(1)} %slice.19), channel_id=1, source_target_pairs={{0,24},{4,28},{8,16},{12,20},{16,8},{20,12},{24,0},{28,4},{1,25},{... | collective-permute-start | bytes 196616 | tf_op jit(solution)/shard_map/ppermute | solution.py:263
  32.6 1.4 %project_mid.1.refs_4_ = f32[384,768]{1,0:T(8,128)S(1)} custom-call(f32[2,128]{1,0:T(2,128)S(1)} %copy-done.4, bf16[384,480]{1,0:T(8,128)(2,1)S(1)} %get-tuple-element.49.refs_0_, bf16[384,480]{1,0:T(8,128)(2,1)S(1)} %get-tuple-element.50.refs_1_, bf16[384,384]{1,0:T(8,128)(2,1)S(1)} %get-tuple-element.51.refs_2_, ...), custom_call_target="tpu_custom_call" | custom-call | flops 1019215872 | bytes 3981312 | tf_op jit(solution)/shard_map/project_mid/pallas_call | solution.py:100
  34.1 1.8 %collective-permute-done.11 = bf16[256,128]{1,0:T(8,128)(2,1)S(1)} collective-permute-done((bf16[256,128]{1,0:T(8,128)(2,1)S(1)}, bf16[256,128]{1,0:T(8,128)(2,1)S(1)}, u32[]{:S(2)}, u32[]{:S(2)}) %collective-permute-start.11) | collective-permute-done | bytes 65568 | tf_op jit(solution)/shard_map/ppermute | solution.py:263
  35.8 1.9 %collective-permute-done.10.refs_2_ = bf16[288,768]{1,0:T(8,128)(2,1)S(1)} collective-permute-done((bf16[288,768]{1,0:T(8,128)(2,1)S(1)}, bf16[288,768]{1,0:T(8,128)(2,1)S(1)}, u32[]{:S(2)}, u32[]{:S(2)}) %collective-permute-start.10) | collective-permute-done | bytes 442400 | tf_op jit(solution)/shard_map/ppermute | solution.py:272
  37.7 1.0 %collective-permute-start.18 = (bf16[256,384]{1,0:T(8,128)(2,1)S(1)}, bf16[256,384]{1,0:T(8,128)(2,1)S(1)}, u32[]{:S(2)}, u32[]{:S(2)}) collective-permute-start(bf16[256,384]{1,0:T(8,128)(2,1)S(1)} %copy-done.2), channel_id=1, source_target_pairs={{0,8},{4,12},{8,0},{12,4},{16,24},{20,28},{24,16},{28,20},{1,9},{5... | collective-permute-start | bytes 589832 | tf_op jit(solution)/shard_map/ppermute | solution.py:263
  38.7 0.8 %collective-permute-done.12.refs_3_ = bf16[288,768]{1,0:T(8,128)(2,1)S(1)} collective-permute-done((bf16[288,768]{1,0:T(8,128)(2,1)S(1)}, bf16[288,768]{1,0:T(8,128)(2,1)S(1)}, u32[]{:S(2)}, u32[]{:S(2)}) %collective-permute-start.12) | collective-permute-done | bytes 442400 | tf_op jit(solution)/shard_map/ppermute | solution.py:263
  41.3 1.7 %collective-permute-start.21 = (bf16[256,384]{1,0:T(8,128)(2,1)S(1)}, bf16[256,384]{1,0:T(8,128)(2,1)S(1)}, u32[]{:S(2)}, u32[]{:S(2)}) collective-permute-start(bf16[256,384]{1,0:T(8,128)(2,1)S(1)} %constant_dynamic-update-slice_fusion.4.refs_7_), channel_id=1, source_target_pairs={{0,8},{4,12},{8,0},{12,4},{16,24},{20,28},{24,16},{28,20},{1,9},{5... | collective-permute-start | bytes 589832 | tf_op jit(solution)/shard_map/ppermute | solution.py:263
  43.0 1.5 %collective-permute-start.17 = (bf16[256,384]{1,0:T(8,128)(2,1)S(1)}, bf16[256,384]{1,0:T(8,128)(2,1)S(1)}, u32[]{:S(2)}, u32[]{:S(2)}) collective-permute-start(bf16[256,384]{1,0:T(8,128)(2,1)S(1)} %copy-done.2), channel_id=1, source_target_pairs={{0,4},{4,0},{8,12},{12,8},{16,20},{20,16},{24,28},{28,24},{1,5},{5... | collective-permute-start | bytes 589832 | tf_op jit(solution)/shard_map/ppermute | solution.py:263
  46.4 1.6 %collective-permute-done.21.refs_9_ = bf16[256,384]{1,0:T(8,128)(2,1)S(1)} collective-permute-done((bf16[256,384]{1,0:T(8,128)(2,1)S(1)}, bf16[256,384]{1,0:T(8,128)(2,1)S(1)}, u32[]{:S(2)}, u32[]{:S(2)}) %collective-permute-start.21) | collective-permute-done | bytes 196640 | tf_op jit(solution)/shard_map/ppermute | solution.py:263
  48.0 1.3 %collective-permute-start.19 = (bf16[256,384]{1,0:T(8,128)(2,1)S(1)}, bf16[256,384]{1,0:T(8,128)(2,1)S(1)}, u32[]{:S(2)}, u32[]{:S(2)}) collective-permute-start(bf16[256,384]{1,0:T(8,128)(2,1)S(1)} %collective-permute-done.18.refs_5_), channel_id=1, source_target_pairs={{0,4},{4,0},{8,12},{12,8},{16,20},{20,16},{24,28},{28,24},{1,5},{5... | collective-permute-start | bytes 589832 | tf_op jit(solution)/shard_map/ppermute | solution.py:263
  50.7 1.2 %attend_own_slab.1 = (f32[384,256]{1,0:T(8,128)S(1)}, f32[384,256]{1,0:T(8,128)S(1)}) custom-call(bf16[384,256]{1,0:T(8,128)(2,1)S(1)} %project_queries.1.queries_ref, bf16[384,512]{1,0:T(8,128)(2,1)S(1)} %project_keys_values.1.stacked_ref), custom_call_target="tpu_custom_call" | custom-call | flops 150994944 | bytes 1376256 | tf_op jit(solution)/shard_map/attend_own_slab/pallas_call | solution.py:180
  51.9 2.8 %attend_and_mix.1 = bf16[1,384,3072]{2,1,0:T(8,128)(2,1)} custom-call(bf16[384,256]{1,0:T(8,128)(2,1)S(1)} %project_queries.1.queries_ref, f32[384,256]{1,0:T(8,128)S(1)} %get-tuple-element.66.weighted_ref, f32[384,256]{1,0:T(8,128)S(1)} %get-tuple-element.67.mass_ref, bf16[256,512]{1,0:T(8,128)(2,1)S(1)} %collective-permute-done.13.refs_0_, ...), custom_call_target="tpu_custom_call" | custom-call | flops 704643072 | bytes 3932160 | tf_op jit(solution)/shard_map/attend_and_mix/pallas_call | solution.py:240
  (55 shorter events, 7.9 us)
Async XLA Ops:
  1.0 9.8 %collective-permute-start = (bf16[96,768]{1,0:T(8,128)(2,1)S(1)}, bf16[96,768]{1,0:T(8,128)(2,1)S(1)}, u32[]{:S(2)}, u32[]{:S(2)}) collective-permute-start(bf16[96,768]{1,0:T(8,128)(2,1)S(1)} %get-tuple-element.74), channel_id=1, source_target_pairs={{0,24},{4,28},{8,16},{12,20},{16,8},{20,12},{24,0},{28,4},{1,25},{... | collective-permute-start | bytes 442376 | tf_op jit(solution)/shard_map/ppermute | solution.py:263
  6.1 9.7 %collective-permute-start.3 = (bf16[96,768]{1,0:T(8,128)(2,1)S(1)}, bf16[96,768]{1,0:T(8,128)(2,1)S(1)}, u32[]{:S(2)}, u32[]{:S(2)}) collective-permute-start(bf16[96,768]{1,0:T(8,128)(2,1)S(1)} %get-tuple-element.74), channel_id=1, source_target_pairs={{0,8},{4,12},{8,0},{12,4},{16,24},{20,28},{24,16},{28,20},{1,9},{5... | collective-permute-start | bytes 442376 | tf_op jit(solution)/shard_map/ppermute | solution.py:263
  10.8 5.1 %collective-permute-start.1 = (bf16[96,768]{1,0:T(8,128)(2,1)S(1)}, bf16[96,768]{1,0:T(8,128)(2,1)S(1)}, u32[]{:S(2)}, u32[]{:S(2)}) collective-permute-start(bf16[96,768]{1,0:T(8,128)(2,1)S(1)} %collective-permute-done), channel_id=1, source_target_pairs={{0,1},{1,0},{2,3},{3,2},{4,6},{5,7},{6,4},{7,5},{8,9},{9,8},{10,11... | collective-permute-start | bytes 442376 | tf_op jit(solution)/shard_map/ppermute | solution.py:272
  12.5 5.1 %collective-permute-start.2 = (bf16[96,768]{1,0:T(8,128)(2,1)S(1)}, bf16[96,768]{1,0:T(8,128)(2,1)S(1)}, u32[]{:S(2)}, u32[]{:S(2)}) collective-permute-start(bf16[96,768]{1,0:T(8,128)(2,1)S(1)} %collective-permute-done), channel_id=1, source_target_pairs={{0,8},{4,12},{8,0},{12,4},{16,24},{20,28},{24,16},{28,20},{1,9},{5... | collective-permute-start | bytes 442376 | tf_op jit(solution)/shard_map/ppermute | solution.py:263
  14.3 8.7 %collective-permute-start.7 = (bf16[384,768]{1,0:T(8,128)(2,1)S(1)}, bf16[384,768]{1,0:T(8,128)(2,1)S(1)}, u32[]{:S(2)}, u32[]{:S(2)}) collective-permute-start(bf16[384,768]{1,0:T(8,128)(2,1)S(1)} %copy-done.1), channel_id=1, source_target_pairs={{0,4},{4,0},{8,12},{12,8},{16,20},{20,16},{24,28},{28,24},{1,5},{5... | collective-permute-start | bytes 1769480 | tf_op jit(solution)/shard_map/ppermute | solution.py:263
  15.8 7.3 %copy-start.4 = (f32[2,128]{1,0:T(2,128)S(1)}, f32[2,128]{1,0:T(2,128)}, u32[]{:S(2)}) copy-start(f32[2,128]{1,0:T(2,128)} %gain_ref.7) | copy-start | bytes 3076
  17.7 10.9 %collective-permute-start.4 = (bf16[384,768]{1,0:T(8,128)(2,1)S(1)}, bf16[384,768]{1,0:T(8,128)(2,1)S(1)}, u32[]{:S(2)}, u32[]{:S(2)}) collective-permute-start(bf16[384,768]{1,0:T(8,128)(2,1)S(1)} %pad_maximum_fusion), channel_id=1, source_target_pairs={{0,2},{1,3},{2,0},{3,1},{4,5},{5,4},{6,7},{7,6},{8,10},{9,11},{10,... | collective-permute-start | bytes 1769480 | tf_op jit(solution)/shard_map/ppermute | solution.py:272
  19.3 7.7 %collective-permute-start.6 = (bf16[256,256]{1,0:T(8,128)(2,1)S(1)}, bf16[256,256]{1,0:T(8,128)(2,1)S(1)}, u32[]{:S(2)}, u32[]{:S(2)}) collective-permute-start(bf16[256,256]{1,0:T(8,128)(2,1)S(1)} %slice.15), channel_id=1, source_target_pairs={{0,24},{4,28},{8,16},{12,20},{16,8},{20,12},{24,0},{28,4},{1,25},{... | collective-permute-start | bytes 393224 | tf_op jit(solution)/shard_map/ppermute | solution.py:263
  23.0 5.6 %collective-permute-start.5 = (bf16[96,768]{1,0:T(8,128)(2,1)S(1)}, bf16[96,768]{1,0:T(8,128)(2,1)S(1)}, u32[]{:S(2)}, u32[]{:S(2)}) collective-permute-start(bf16[96,768]{1,0:T(8,128)(2,1)S(1)} %get-tuple-element.57), channel_id=1, source_target_pairs={{0,8},{4,12},{8,0},{12,4},{16,24},{20,28},{24,16},{28,20},{1,9},{5... | collective-permute-start | bytes 442376 | tf_op jit(solution)/shard_map/ppermute | solution.py:263
  28.7 4.0 %collective-permute-start.8 = (bf16[480,768]{1,0:T(8,128)(2,1)S(1)}, bf16[480,768]{1,0:T(8,128)(2,1)S(1)}, u32[]{:S(2)}, u32[]{:S(2)}) collective-permute-start(bf16[480,768]{1,0:T(8,128)(2,1)S(1)} %constant_dynamic-update-slice_fusion.refs_4_), channel_id=1, source_target_pairs={{0,4},{4,0},{8,12},{12,8},{16,20},{20,16},{24,28},{28,24},{1,5},{5... | collective-permute-start | bytes 2211848 | tf_op jit(solution)/shard_map/ppermute | solution.py:263
  28.7 3.9 %collective-permute-start.9 = (bf16[384,768]{1,0:T(8,128)(2,1)S(1)}, bf16[384,768]{1,0:T(8,128)(2,1)S(1)}, u32[]{:S(2)}, u32[]{:S(2)}) collective-permute-start(bf16[384,768]{1,0:T(8,128)(2,1)S(1)} %collective-permute-done.4.refs_6_), channel_id=1, source_target_pairs={{0,4},{4,0},{8,12},{12,8},{16,20},{20,16},{24,28},{28,24},{1,5},{5... | collective-permute-start | bytes 1769480 | tf_op jit(solution)/shard_map/ppermute | solution.py:263
  29.3 8.4 %collective-permute-start.10 = (bf16[288,768]{1,0:T(8,128)(2,1)S(1)}, bf16[288,768]{1,0:T(8,128)(2,1)S(1)}, u32[]{:S(2)}, u32[]{:S(2)}) collective-permute-start(bf16[288,768]{1,0:T(8,128)(2,1)S(1)} %pad_maximum_fusion.1), channel_id=1, source_target_pairs={{0,1},{1,0},{2,3},{3,2},{4,6},{5,7},{6,4},{7,5},{8,9},{9,8},{10,11... | collective-permute-start | bytes 1327112 | tf_op jit(solution)/shard_map/ppermute | solution.py:272
  29.7 6.1 %collective-permute-start.11 = (bf16[256,128]{1,0:T(8,128)(2,1)S(1)}, bf16[256,128]{1,0:T(8,128)(2,1)S(1)}, u32[]{:S(2)}, u32[]{:S(2)}) collective-permute-start(bf16[256,128]{1,0:T(8,128)(2,1)S(1)} %slice.19), channel_id=1, source_target_pairs={{0,24},{4,28},{8,16},{12,20},{16,8},{20,12},{24,0},{28,4},{1,25},{... | collective-permute-start | bytes 196616 | tf_op jit(solution)/shard_map/ppermute | solution.py:263
  37.7 1.8 %collective-permute-start.12 = (bf16[288,768]{1,0:T(8,128)(2,1)S(1)}, bf16[288,768]{1,0:T(8,128)(2,1)S(1)}, u32[]{:S(2)}, u32[]{:S(2)}) collective-permute-start(bf16[288,768]{1,0:T(8,128)(2,1)S(1)} %collective-permute-done.10.refs_2_), channel_id=1, source_target_pairs={{0,4},{4,0},{8,12},{12,8},{16,20},{20,16},{24,28},{28,24},{1,5},{5... | collective-permute-start | bytes 1327112 | tf_op jit(solution)/shard_map/ppermute | solution.py:263
  37.7 7.3 %collective-permute-start.18 = (bf16[256,384]{1,0:T(8,128)(2,1)S(1)}, bf16[256,384]{1,0:T(8,128)(2,1)S(1)}, u32[]{:S(2)}, u32[]{:S(2)}) collective-permute-start(bf16[256,384]{1,0:T(8,128)(2,1)S(1)} %copy-done.2), channel_id=1, source_target_pairs={{0,8},{4,12},{8,0},{12,4},{16,24},{20,28},{24,16},{28,20},{1,9},{5... | collective-permute-start | bytes 589832 | tf_op jit(solution)/shard_map/ppermute | solution.py:263
  40.2 5.5 %collective-permute-start.14 = (bf16[256,512]{1,0:T(8,128)(2,1)S(1)}, bf16[256,512]{1,0:T(8,128)(2,1)S(1)}, u32[]{:S(2)}, u32[]{:S(2)}) collective-permute-start(bf16[256,512]{1,0:T(8,128)(2,1)S(1)} %get-tuple-element.75), channel_id=1, source_target_pairs={{5,7},{6,4},{13,15},{14,12},{21,23},{22,20},{29,31},{30,28}} | collective-permute-start | bytes 786440 | tf_op jit(solution)/shard_map/ppermute | solution.py:297
  40.9 9.2 %collective-permute-start.13 = (bf16[256,512]{1,0:T(8,128)(2,1)S(1)}, bf16[256,512]{1,0:T(8,128)(2,1)S(1)}, u32[]{:S(2)}, u32[]{:S(2)}) collective-permute-start(bf16[256,512]{1,0:T(8,128)(2,1)S(1)} %get-tuple-element.76), channel_id=1, source_target_pairs={{0,1},{1,0},{2,3},{3,2},{4,5},{5,4},{6,7},{7,6},{8,9},{9,8},{10,11... | collective-permute-start | bytes 786440 | tf_op jit(solution)/shard_map/ppermute | solution.py:263
  41.3 6.7 %collective-permute-start.21 = (bf16[256,384]{1,0:T(8,128)(2,1)S(1)}, bf16[256,384]{1,0:T(8,128)(2,1)S(1)}, u32[]{:S(2)}, u32[]{:S(2)}) collective-permute-start(bf16[256,384]{1,0:T(8,128)(2,1)S(1)} %constant_dynamic-update-slice_fusion.4.refs_7_), channel_id=1, source_target_pairs={{0,8},{4,12},{8,0},{12,4},{16,24},{20,28},{24,16},{28,20},{1,9},{5... | collective-permute-start | bytes 589832 | tf_op jit(solution)/shard_map/ppermute | solution.py:263
  43.0 6.3 %collective-permute-start.17 = (bf16[256,384]{1,0:T(8,128)(2,1)S(1)}, bf16[256,384]{1,0:T(8,128)(2,1)S(1)}, u32[]{:S(2)}, u32[]{:S(2)}) collective-permute-start(bf16[256,384]{1,0:T(8,128)(2,1)S(1)} %copy-done.2), channel_id=1, source_target_pairs={{0,4},{4,0},{8,12},{12,8},{16,20},{20,16},{24,28},{28,24},{1,5},{5... | collective-permute-start | bytes 589832 | tf_op jit(solution)/shard_map/ppermute | solution.py:263
  45.0 6.8 %collective-permute-start.16 = (bf16[256,512]{1,0:T(8,128)(2,1)S(1)}, bf16[256,512]{1,0:T(8,128)(2,1)S(1)}, u32[]{:S(2)}, u32[]{:S(2)}) collective-permute-start(bf16[256,512]{1,0:T(8,128)(2,1)S(1)} %get-tuple-element.75), channel_id=1, source_target_pairs={{1,2},{2,1},{9,10},{10,9},{17,18},{18,17},{25,26},{26,25}} | collective-permute-start | bytes 786440 | tf_op jit(solution)/shard_map/ppermute | solution.py:298
  45.7 6.2 %collective-permute-start.15 = (bf16[256,512]{1,0:T(8,128)(2,1)S(1)}, bf16[256,512]{1,0:T(8,128)(2,1)S(1)}, u32[]{:S(2)}, u32[]{:S(2)}) collective-permute-start(bf16[256,512]{1,0:T(8,128)(2,1)S(1)} %collective-permute-done.14), channel_id=1, source_target_pairs={{7,6},{4,5},{15,14},{12,13},{23,22},{20,21},{31,30},{28,29}} | collective-permute-start | bytes 786440 | tf_op jit(solution)/shard_map/ppermute | solution.py:298
  48.0 3.8 %collective-permute-start.19 = (bf16[256,384]{1,0:T(8,128)(2,1)S(1)}, bf16[256,384]{1,0:T(8,128)(2,1)S(1)}, u32[]{:S(2)}, u32[]{:S(2)}) collective-permute-start(bf16[256,384]{1,0:T(8,128)(2,1)S(1)} %collective-permute-done.18.refs_5_), channel_id=1, source_target_pairs={{0,4},{4,0},{8,12},{12,8},{16,20},{20,16},{24,28},{28,24},{1,5},{5... | collective-permute-start | bytes 589832 | tf_op jit(solution)/shard_map/ppermute | solution.py:263
  49.3 2.5 %collective-permute-start.20 = (bf16[256,384]{1,0:T(8,128)(2,1)S(1)}, bf16[256,384]{1,0:T(8,128)(2,1)S(1)}, u32[]{:S(2)}, u32[]{:S(2)}) collective-permute-start(bf16[256,384]{1,0:T(8,128)(2,1)S(1)} %constant_dynamic-update-slice_fusion.4.refs_7_), channel_id=1, source_target_pairs={{0,4},{4,0},{8,12},{12,8},{16,20},{20,16},{24,28},{28,24},{1,5},{5... | collective-permute-start | bytes 589832 | tf_op jit(solution)/shard_map/ppermute | solution.py:263
  50.1 1.8 %collective-permute-start.22 = (bf16[256,384]{1,0:T(8,128)(2,1)S(1)}, bf16[256,384]{1,0:T(8,128)(2,1)S(1)}, u32[]{:S(2)}, u32[]{:S(2)}) collective-permute-start(bf16[256,384]{1,0:T(8,128)(2,1)S(1)} %collective-permute-done.21.refs_9_), channel_id=1, source_target_pairs={{0,4},{4,0},{8,12},{12,8},{16,20},{20,16},{24,28},{28,24},{1,5},{5... | collective-permute-start | bytes 589832 | tf_op jit(solution)/shard_map/ppermute | solution.py:263
  (4 other events, 11.8 us)

commit v6 on v5

--- a/solution.py
+++ b/solution.py
@@ -164,22 +164,46 @@
     return dot(raised.astype(bf16), values), jnp.sum(raised, axis=-1, keepdims=True)
 
 
-def attend_own_kernel(queries_ref, stacked_ref, weighted_ref, mass_ref):
+def edge_span(tile, tiles, ahead):
+    if ahead:
+        return slice(0, max(tile + REACH + 1 - tiles, 0) * TILE)
+    return slice(BORDER - max(REACH - tile, 0) * TILE, BORDER)
+
+
+def edge_share(queries_ref, edge_ref, tile, tiles, ahead, ks, vs, flag=None):
+    span = edge_span(tile, tiles, ahead)
+    if span.start == span.stop:
+        return None
+    query = queries_ref[tile * TILE : (tile + 1) * TILE, ks]
+    return share(query, edge_ref[span, ks], edge_ref[span, vs], flag)
+
+
+def attend_own_kernel(queries_ref, stacked_ref, near_ref, weighted_ref, mass_ref):
     tiles = queries_ref.shape[0] // TILE
-    for ks, vs in heads():
-        for tile in range(tiles):
-            rows = slice(tile * TILE, (tile + 1) * TILE)
-            span = slice(max(tile - REACH, 0) * TILE, min(tile + REACH + 1, tiles) * TILE)
-            weighted, mass = share(queries_ref[rows, ks], stacked_ref[span, ks], stacked_ref[span, vs])
-            weighted_ref[rows, ks] = weighted
-            mass_ref[rows, ks] = jnp.broadcast_to(mass, (TILE, HEAD_DIM))
-
-
-def attend_own(queries, stacked):
+    place = lax.axis_index("frame")
+    inside = ((place ^ 1) < lax.axis_size("frame")).astype(f32)
+    for odd in (0, 1):
+
+        @pl.when((place & 1) == odd)
+        def _():
+            for ks, vs in heads():
+                for tile in range(tiles):
+                    rows = slice(tile * TILE, (tile + 1) * TILE)
+                    span = slice(max(tile - REACH, 0) * TILE, min(tile + REACH + 1, tiles) * TILE)
+                    keys, values = stacked_ref[span, ks], stacked_ref[span, vs]
+                    weighted, mass = share(queries_ref[rows, ks], keys, values)
+                    more = edge_share(queries_ref, near_ref, tile, tiles, odd == 0, ks, vs, inside)
+                    if more is not None:
+                        weighted, mass = weighted + more[0], mass + more[1]
+                    weighted_ref[rows, ks] = weighted
+                    mass_ref[rows, ks] = jnp.broadcast_to(mass, (TILE, HEAD_DIM))
+
+
+def attend_own(queries, stacked, near):
     rows = queries.shape[0]
     return pl.pallas_call(
         attend_own_kernel,
-        in_specs=[VMEM] * 2,
+        in_specs=[VMEM] * 3,
         out_specs=[VMEM] * 2,
         out_shape=[jax.ShapeDtypeStruct((rows, WIDTH), f32)] * 2,
         compiler_params=params(),
@@ -188,37 +212,39 @@
             transcendentals=rows * rows * HEADS,
         ),
         name="attend_own_slab",
-    )(queries, stacked)
+    )(queries, stacked, near)
 
 
 def attend_kernel(layout, count, arrivals, queries_ref, weighted_ref, mass_ref, *refs):
-    near_ref, arrived, refs = refs[0], refs[1:arrivals], refs[arrivals:]
+    arrived, refs = refs[:arrivals], refs[arrivals:]
     sources = refs[:count]
-    mixed_ref, before, behind, attended, blocks, sems = refs[count:]
+    mixed_ref, far, attended, blocks, sems = refs[count:]
     tiles = queries_ref.shape[0] // TILE
     place = lax.axis_index("frame")
-    far = arrived[0][...]
-    for ref in arrived[1:]:
-        far = far + ref[...]
-    odd = (place & 1) == 1
-    before[...] = jnp.where(odd, near_ref[...], far)
-    behind[...] = jnp.where(odd, far, near_ref[...])
-    has_before = (place > 0).astype(f32)
-    has_behind = (place < lax.axis_size("frame") - 1).astype(f32)
-    for ks, vs in heads():
-        for tile in range(tiles):
-            rows = slice(tile * TILE, (tile + 1) * TILE)
-            weighted, mass = weighted_ref[rows, ks], mass_ref[rows, ks]
-            low, high = tile - REACH, tile + REACH + 1 - tiles
-            spans = []
-            if low < 0:
-                spans.append((before, slice((low + REACH) * TILE, BORDER), has_before))
-            if high > 0:
-                spans.append((behind, slice(0, high * TILE), has_behind))
-            for ref, span, flag in spans:
-                more, extra = share(queries_ref[rows, ks], ref[span, ks], ref[span, vs], flag)
-                weighted, mass = weighted + more, mass + extra
-            attended[rows, ks] = (weighted / mass).astype(bf16)
+    parity = place & 1
+    exists = jnp.where(parity == 1, place < lax.axis_size("frame") - 1, place > 0)
+
+    @pl.when(jnp.logical_not(exists))
+    def _():
+        attended[...] = (weighted_ref[...] / mass_ref[...]).astype(bf16)
+
+    for odd in (0, 1):
+
+        @pl.when(jnp.logical_and(exists, parity == odd))
+        def _():
+            total = arrived[0][...]
+            for ref in arrived[1:]:
+                total = total + ref[...]
+            far[...] = total
+            for ks, vs in heads():
+                for tile in range(tiles):
+                    rows = slice(tile * TILE, (tile + 1) * TILE)
+                    weighted, mass = weighted_ref[rows, ks], mass_ref[rows, ks]
+                    more = edge_share(queries_ref, far, tile, tiles, odd == 1, ks, vs)
+                    if more is not None:
+                        weighted, mass = weighted + more[0], mass + more[1]
+                    attended[rows, ks] = (weighted / mass).astype(bf16)
+
     width = blocks.shape[2]
     copies = []
     for number, (source, begin, place) in enumerate(layout()):
@@ -234,16 +260,15 @@
         copy.wait()
 
 
-def attend(layout, sources, queries, own, edges, model):
+def attend(layout, sources, queries, own, arrived, model):
     rows, number = queries.shape[0], len(layout())
     width = model // number
     return pl.pallas_call(
-        functools.partial(attend_kernel, layout, len(sources), len(edges)),
-        in_specs=[VMEM] * (3 + len(edges) + len(sources)),
+        functools.partial(attend_kernel, layout, len(sources), len(arrived)),
+        in_specs=[VMEM] * (3 + len(arrived) + len(sources)),
         out_specs=ANY,
         out_shape=jax.ShapeDtypeStruct((1, rows, model), bf16),
         scratch_shapes=[
-            pltpu.VMEM((BORDER, 2 * WIDTH), bf16),
             pltpu.VMEM((BORDER, 2 * WIDTH), bf16),
             pltpu.VMEM((rows, WIDTH), bf16),
             pltpu.VMEM((number, rows, width), bf16),
@@ -256,7 +281,7 @@
             transcendentals=rows * HEADS * 2 * TILE,
         ),
         name="attend_and_mix",
-    )(queries, *own, *edges, *sources)
+    )(queries, *own, *arrived, *sources)
 
 
 def swap(x, axis, bits):
@@ -344,7 +369,6 @@
     come = [swap(part, "fsdp", 2 * k) for k in front]
     near = swap(part, "fsdp", 2)
     other_qkv = swap(w_qkv, "fsdp", 1)
-    other_out = swap(w_out, "fsdp", 1)
     normed = norm_rows(frames, modulation)
     normed, come = fence((normed, come))
 
@@ -352,10 +376,10 @@
     one = jnp.concatenate(come, axis=0)
     one_rest = swap_plane(one, 0)
     nf, nb = len(front), len(back)
-    homes = [[(0, 2 * nf + nb), (2, 2 * nb), (1, 2 * nf + nb), (0, 2 * nf + nb + 1)]]
+    homes = [[(0, 2 * nf + nb), (0, 2 * nf + nb + 2), (1, 2 * nf + nb), (0, 2 * nf + nb + 1)]]
     homes += [[(0, i), (0, nf + i), (1, i), (1, nf + i)] for i in range(nf)]
     homes += [[(0, 2 * nf + i), (2, i), (1, 2 * nf + i), (2, nb + i)] for i in range(nb)]
-    widths = [quarter * n for n in (2 * nf + nb + 2, 2 * nf + nb + 1, 2 * nb + 1)]
+    widths = [quarter * n for n in (2 * nf + nb + 3, 2 * nf + nb + 1, 2 * nb)]
     arranged = arrange(shard_places, order, homes, widths, normed)
     next_part = lax.dynamic_slice_in_dim(w_qkv, (spot ^ 1) * quarter, quarter, 0)
     one, one_rest, late, near, arranged, next_part = fence(
@@ -364,27 +388,27 @@
 
     late = jnp.concatenate(late + [near], axis=0)
     two = swap_plane(jnp.concatenate([one, one_rest, late], axis=0), 1)
+    near_rest = swap_plane(near, 0)
     across = swap(next_part, "fsdp", 2)
     cut = 2 * (shard_columns // TILE) // 3 * TILE
     wides = [swap(w_out[:, :cut], "fsdp", 2 * k) for k in front]
     total = project(
         [(normed, w_qkv), (normed, other_qkv)], qk_gain, (0, columns), "project_own", own_places
     )
-    two, across, late, one, one_rest, wides, total = fence(
-        (two, across, late, one, one_rest, wides, total)
+    two, near_rest, across, late, one, one_rest, wides, total = fence(
+        (two, near_rest, across, late, one, one_rest, wides, total)
     )
 
     relayed = two[2 * nf * quarter : (2 * nf + nb) * quarter]
-    three = swap_plane(
-        jnp.concatenate([late[: nb * quarter], relayed, late[nb * quarter :]], axis=0), 0
-    )
+    three = swap_plane(jnp.concatenate([late[: nb * quarter], relayed], axis=0), 0)
     narrows = [swap(w_out[:, cut:], "fsdp", 2 * k) for k in front]
-    kept = jnp.concatenate([one, one_rest, late, across], axis=0)
+    kept = jnp.concatenate([one, one_rest, late, across, near_rest], axis=0)
     pieces = [kept, swap(kept, "fsdp", 1), two, swap(two, "fsdp", 1)]
     total = project(
         list(zip(arranged[:4], pieces)), qk_gain, (0, columns), "project_mid", total=total
     )
-    total, three, narrows = fence((total, three, narrows))
+    other_out = swap(w_out, "fsdp", 1)
+    total, three, narrows, other_out = fence((total, three, narrows, other_out))
 
     last = [(arranged[4], three), (arranged[5], swap(three, "fsdp", 1))]
     stacked = project(
@@ -425,8 +449,8 @@
     queries, stacked, edges, layout, sources = plan(
         frames[0], modulation[0], w_qkv, w_out, qk_gain
     )
-    own = attend_own(queries, stacked)
-    return attend(layout, sources, queries, own, edges, frames.shape[2])
+    own = attend_own(queries, stacked, edges[0])
+    return attend(layout, sources, queries, own, edges[1:], frames.shape[2])
 
 
 def solution(mesh):

time: 55.1 us -> 54.4 us (0.987)
  waiting for transfers between devices: 14.1 us -> 11.7 us
  starting transfers between devices: 25.8 us -> 28.2 us
  Pallas kernels: 10.8 us -> 9.98 us
    ppermute x17, waiting for transfers between devices: 12.1 us -> 9.78 us  [swap(): lax.ppermute(x, axis, [(i, i ^ bits) for i in range(lax.axis_size(axis))])]
    ppermute x3 -> x4, starting transfers between devices: 3.65 us -> 5 us  [swap_plane(): return lax.ppermute(x, ('fsdp', 'frame'), pairs)]
    ppermute x17, starting transfers between devices: 20.1 us -> 21.2 us  [swap(): lax.ppermute(x, axis, [(i, i ^ bits) for i in range(lax.axis_size(axis))])]
    pallas_call x1, Pallas kernels: 2.76 us -> 1.85 us  [attend(): pl.pallas_call(functools.partial(attend_kernel, layout, len(sources), len...]
    ppermute x3 -> x4, waiting for transfers between devices: 2.05 us -> 1.9 us  [swap_plane(): return lax.ppermute(x, ('fsdp', 'frame'), pairs)]
    unnamed x14 -> x15, local copies, waits for them, and re-layouts: 2.47 us -> 2.49 us
  transfers between devices with their start and end apart: 23 -> 24, of which waited for: 11 -> 10; matrix products, arithmetic and copies ran while one was open for 0% -> 0% of each run, Pallas kernels for 15% -> 15%
where the time goes in v6:
time: 54.4 us; the launch traced here: 53.8 us
  starting transfers between devices  28.2 us (52%)
  waiting for transfers between devices  11.7 us (22%)
  Pallas kernels  9.98 us (18%)
  local copies, waits for them, and re-layouts  3.6 us (7%)
    ppermute x17, starting transfers between devices, swap(): lax.ppermute(x, axis, [(i, i ^ bits) for i in range(lax.axis_size(axis))])  21.2 us
    ppermute x17, waiting for transfers between devices, swap(): lax.ppermute(x, axis, [(i, i ^ bits) for i in range(lax.axis_size(axis))])  9.78 us
    ppermute x4, starting transfers between devices, swap_plane(): return lax.ppermute(x, ('fsdp', 'frame'), pairs)  5 us
    pallas_call x4, Pallas kernels, project(): pl.pallas_call(functools.partial(project_kernel, len(pairs), starts, kind...  3.26 us
    unnamed x15, local copies, waits for them, and re-layouts  2.49 us
    pallas_call x1, Pallas kernels, norm_rows(): pl.pallas_call(norm_kernel, grid=(rows // block,), in_specs=[pl.BlockSpec...  2.15 us
    ppermute x4, waiting for transfers between devices, swap_plane(): return lax.ppermute(x, ('fsdp', 'frame'), pairs)  1.9 us
    pallas_call x1, Pallas kernels, attend(): pl.pallas_call(functools.partial(attend_kernel, layout, len(sources), len...  1.85 us
  transfers between devices with their start and end apart: 24, of which 10 were waited for; matrix products, arithmetic and copies ran while one was open for 0% of the time, Pallas kernels for 15%

profile of v6, /device:TPU:0, one launch (start us, length us, event | category | flops | bytes accessed | tf_op | source)
XLA Modules:
  0.0 53.8 jit_solution(15417409237897208215)
XLA Ops:
  0.0 1.0 %constant_dynamic-slice_fusion.2 = (bf16[96,768]{1,0:T(8,128)(2,1)S(1)}, bf16[96,768]{1,0:T(8,128)(2,1)S(1)}) fusion(bf16[384,768]{1,0:T(8,128)(2,1)} %refs_2_.2, s32[]{:T(128)S(6)} %select_n.13, s32[]{:T(128)S(6)} %select_n.12), kind=kLoop, calls=%fused_computation.12 | loop fusion | bytes 589832 | tf_op jit(solution)/shard_map/dynamic_slice | solution.py:384
  1.0 5.1 %collective-permute-start = (bf16[96,768]{1,0:T(8,128)(2,1)S(1)}, bf16[96,768]{1,0:T(8,128)(2,1)S(1)}, u32[]{:S(2)}, u32[]{:S(2)}) collective-permute-start(bf16[96,768]{1,0:T(8,128)(2,1)S(1)} %get-tuple-element.78), channel_id=1, source_target_pairs={{0,24},{4,28},{8,16},{12,20},{16,8},{20,12},{24,0},{28,4},{1,25},{... | collective-permute-start | bytes 442376 | tf_op jit(solution)/shard_map/ppermute | solution.py:288
  6.1 1.7 %copy-done = bf16[1,384,3072]{2,1,0:T(8,128)(2,1)S(1)} copy-done((bf16[1,384,3072]{2,1,0:T(8,128)(2,1)S(1)}, bf16[1,384,3072]{2,1,0:T(8,128)(2,1)}, u32[]{:S(2)}) %copy-start) | copy-done | bytes 2359320
  8.5 2.2 %layer_norm.1.normed_ref.refs_0_.refs_1_ = bf16[384,3072]{1,0:T(8,128)(2,1)S(1)} custom-call(bf16[384,3072]{1,0:T(8,128)(2,1)S(1)} %bitcast.2, f32[2,3072]{1,0:T(2,128)S(1)} %bitcast.3), custom_call_target="tpu_custom_call" | custom-call | flops 11796480 | bytes 4718592 | tf_op jit(solution)/shard_map/layer_norm/pallas_call | solution.py:49
  10.8 1.7 %collective-permute-start.1 = (bf16[96,768]{1,0:T(8,128)(2,1)S(1)}, bf16[96,768]{1,0:T(8,128)(2,1)S(1)}, u32[]{:S(2)}, u32[]{:S(2)}) collective-permute-start(bf16[96,768]{1,0:T(8,128)(2,1)S(1)} %collective-permute-done), channel_id=1, source_target_pairs={{0,1},{1,0},{2,3},{3,2},{4,6},{5,7},{6,4},{7,5},{8,9},{9,8},{10,11... | collective-permute-start | bytes 442376 | tf_op jit(solution)/shard_map/ppermute | solution.py:297
  12.5 1.8 %collective-permute-start.2 = (bf16[96,768]{1,0:T(8,128)(2,1)S(1)}, bf16[96,768]{1,0:T(8,128)(2,1)S(1)}, u32[]{:S(2)}, u32[]{:S(2)}) collective-permute-start(bf16[96,768]{1,0:T(8,128)(2,1)S(1)} %collective-permute-done), channel_id=1, source_target_pairs={{0,8},{4,12},{8,0},{12,4},{16,24},{20,28},{24,16},{28,20},{1,9},{5... | collective-permute-start | bytes 442376 | tf_op jit(solution)/shard_map/ppermute | solution.py:288
  14.3 1.4 %arrange.1 = (bf16[384,576]{1,0:T(8,128)(2,1)S(1)}, bf16[384,576]{1,0:T(8,128)(2,1)S(1)}, bf16[384,384]{1,0:T(8,128)(2,1)S(1)}, bf16[384,384]{1,0:T(8,128)(2,1)S...) custom-call(bf16[384,3072]{1,0:T(8,128)(2,1)S(1)} %layer_norm.1.normed_ref.refs_0_.refs_1_), custom_call_target="tpu_custom_call" | custom-call | flops 1207959552 | bytes 4718592 | tf_op jit(solution)/shard_map/arrange/pallas_call | solution.py:140
  16.0 1.7 %collective-permute-done.2 = bf16[96,768]{1,0:T(8,128)(2,1)S(1)} collective-permute-done((bf16[96,768]{1,0:T(8,128)(2,1)S(1)}, bf16[96,768]{1,0:T(8,128)(2,1)S(1)}, u32[]{:S(2)}, u32[]{:S(2)}) %collective-permute-start.2) | collective-permute-done | bytes 147488 | tf_op jit(solution)/shard_map/ppermute | solution.py:288
  17.7 1.6 %collective-permute-start.4 = (bf16[384,768]{1,0:T(8,128)(2,1)S(1)}, bf16[384,768]{1,0:T(8,128)(2,1)S(1)}, u32[]{:S(2)}, u32[]{:S(2)}) collective-permute-start(bf16[384,768]{1,0:T(8,128)(2,1)S(1)} %pad_maximum_fusion), channel_id=1, source_target_pairs={{0,2},{1,3},{2,0},{3,1},{4,5},{5,4},{6,7},{7,6},{8,10},{9,11},{10,... | collective-permute-start | bytes 1769480 | tf_op jit(solution)/shard_map/ppermute | solution.py:297
  19.3 3.7 %collective-permute-start.7 = (bf16[256,256]{1,0:T(8,128)(2,1)S(1)}, bf16[256,256]{1,0:T(8,128)(2,1)S(1)}, u32[]{:S(2)}, u32[]{:S(2)}) collective-permute-start(bf16[256,256]{1,0:T(8,128)(2,1)S(1)} %slice.12), channel_id=1, source_target_pairs={{0,24},{4,28},{8,16},{12,20},{16,8},{20,12},{24,0},{28,4},{1,25},{... | collective-permute-start | bytes 393224 | tf_op jit(solution)/shard_map/ppermute | solution.py:288
  24.4 2.7 %collective-permute-done.7 = bf16[256,256]{1,0:T(8,128)(2,1)S(1)} collective-permute-done((bf16[256,256]{1,0:T(8,128)(2,1)S(1)}, bf16[256,256]{1,0:T(8,128)(2,1)S(1)}, u32[]{:S(2)}, u32[]{:S(2)}) %collective-permute-start.7) | collective-permute-done | bytes 131104 | tf_op jit(solution)/shard_map/ppermute | solution.py:288
  27.0 1.1 %collective-permute-done.5 = bf16[96,768]{1,0:T(8,128)(2,1)S(1)} collective-permute-done((bf16[96,768]{1,0:T(8,128)(2,1)S(1)}, bf16[96,768]{1,0:T(8,128)(2,1)S(1)}, u32[]{:S(2)}, u32[]{:S(2)}) %collective-permute-start.5) | collective-permute-done | bytes 147488 | tf_op jit(solution)/shard_map/ppermute | solution.py:297
  30.0 1.2 %collective-permute-start.11 = (bf16[192,768]{1,0:T(8,128)(2,1)S(1)}, bf16[192,768]{1,0:T(8,128)(2,1)S(1)}, u32[]{:S(2)}, u32[]{:S(2)}) collective-permute-start(bf16[192,768]{1,0:T(8,128)(2,1)S(1)} %pad_maximum_fusion.2), channel_id=1, source_target_pairs={{0,1},{1,0},{2,3},{3,2},{4,6},{5,7},{6,4},{7,5},{8,9},{9,8},{10,11... | collective-permute-start | bytes 884744 | tf_op jit(solution)/shard_map/ppermute | solution.py:297
  31.4 2.1 %collective-permute-start.12 = (bf16[256,128]{1,0:T(8,128)(2,1)S(1)}, bf16[256,128]{1,0:T(8,128)(2,1)S(1)}, u32[]{:S(2)}, u32[]{:S(2)}) collective-permute-start(bf16[256,128]{1,0:T(8,128)(2,1)S(1)} %slice.15), channel_id=1, source_target_pairs={{0,24},{4,28},{8,16},{12,20},{16,8},{20,12},{24,0},{28,4},{1,25},{... | collective-permute-start | bytes 196616 | tf_op jit(solution)/shard_map/ppermute | solution.py:288
  33.4 1.7 %project_mid.1.refs_4_ = f32[384,768]{1,0:T(8,128)S(1)} custom-call(f32[2,128]{1,0:T(2,128)S(1)} %copy-done.4, bf16[384,576]{1,0:T(8,128)(2,1)S(1)} %get-tuple-element.51.refs_0_, bf16[384,576]{1,0:T(8,128)(2,1)S(1)} %get-tuple-element.52.refs_1_, bf16[384,384]{1,0:T(8,128)(2,1)S(1)} %get-tuple-element.53.refs_2_, ...), custom_call_target="tpu_custom_call" | custom-call | flops 1132462080 | bytes 4423680 | tf_op jit(solution)/shard_map/project_mid/pallas_call | solution.py:100
  35.2 2.5 %collective-permute-done.12 = bf16[256,128]{1,0:T(8,128)(2,1)S(1)} collective-permute-done((bf16[256,128]{1,0:T(8,128)(2,1)S(1)}, bf16[256,128]{1,0:T(8,128)(2,1)S(1)}, u32[]{:S(2)}, u32[]{:S(2)}) %collective-permute-start.12) | collective-permute-done | bytes 65568 | tf_op jit(solution)/shard_map/ppermute | solution.py:288
  38.3 0.9 %collective-permute-done.14.refs_3_ = bf16[192,768]{1,0:T(8,128)(2,1)S(1)} collective-permute-done((bf16[192,768]{1,0:T(8,128)(2,1)S(1)}, bf16[192,768]{1,0:T(8,128)(2,1)S(1)}, u32[]{:S(2)}, u32[]{:S(2)}) %collective-permute-start.14) | collective-permute-done | bytes 294944 | tf_op jit(solution)/shard_map/ppermute | solution.py:288
  40.4 1.0 %collective-permute-start.15 = (bf16[256,512]{1,0:T(8,128)(2,1)S(1)}, bf16[256,512]{1,0:T(8,128)(2,1)S(1)}, u32[]{:S(2)}, u32[]{:S(2)}) collective-permute-start(bf16[256,512]{1,0:T(8,128)(2,1)S(1)} %get-tuple-element.80), channel_id=1, source_target_pairs={{0,1},{1,0},{2,3},{3,2},{4,5},{5,4},{6,7},{7,6},{8,9},{9,8},{10,11... | collective-permute-start | bytes 786440 | tf_op jit(solution)/shard_map/ppermute | solution.py:288
  41.4 0.8 %collective-permute-start.22 = (bf16[256,384]{1,0:T(8,128)(2,1)S(1)}, bf16[256,384]{1,0:T(8,128)(2,1)S(1)}, u32[]{:S(2)}, u32[]{:S(2)}) collective-permute-start(bf16[256,384]{1,0:T(8,128)(2,1)S(1)} %constant_dynamic-update-slice_fusion.5.refs_6_), channel_id=1, source_target_pairs={{0,8},{4,12},{8,0},{12,4},{16,24},{20,28},{24,16},{28,20},{1,9},{5... | collective-permute-start | bytes 589832 | tf_op jit(solution)/shard_map/ppermute | solution.py:288
  43.5 1.4 %collective-permute-done.19.refs_4_ = bf16[256,384]{1,0:T(8,128)(2,1)S(1)} collective-permute-done((bf16[256,384]{1,0:T(8,128)(2,1)S(1)}, bf16[256,384]{1,0:T(8,128)(2,1)S(1)}, u32[]{:S(2)}, u32[]{:S(2)}) %collective-permute-start.19) | collective-permute-done | bytes 196640 | tf_op jit(solution)/shard_map/ppermute | solution.py:288
  44.9 4.0 %collective-permute-start.20 = (bf16[256,384]{1,0:T(8,128)(2,1)S(1)}, bf16[256,384]{1,0:T(8,128)(2,1)S(1)}, u32[]{:S(2)}, u32[]{:S(2)}) collective-permute-start(bf16[256,384]{1,0:T(8,128)(2,1)S(1)} %collective-permute-done.19.refs_4_), channel_id=1, source_target_pairs={{0,4},{4,0},{8,12},{12,8},{16,20},{20,16},{24,28},{28,24},{1,5},{5... | collective-permute-start | bytes 589832 | tf_op jit(solution)/shard_map/ppermute | solution.py:288
  49.1 1.2 %collective-permute-start.23 = (bf16[256,384]{1,0:T(8,128)(2,1)S(1)}, bf16[256,384]{1,0:T(8,128)(2,1)S(1)}, u32[]{:S(2)}, u32[]{:S(2)}) collective-permute-start(bf16[256,384]{1,0:T(8,128)(2,1)S(1)} %collective-permute-done.22.refs_8_), channel_id=1, source_target_pairs={{0,4},{4,0},{8,12},{12,8},{16,20},{20,16},{24,28},{28,24},{1,5},{5... | collective-permute-start | bytes 589832 | tf_op jit(solution)/shard_map/ppermute | solution.py:288
  50.6 1.3 %attend_own_slab.1 = (f32[384,256]{1,0:T(8,128)S(1)}, f32[384,256]{1,0:T(8,128)S(1)}) custom-call(bf16[384,256]{1,0:T(8,128)(2,1)S(1)} %project_queries.1.queries_ref, bf16[384,512]{1,0:T(8,128)(2,1)S(1)} %project_keys_values.1.stacked_ref, bf16[256,512]{1,0:T(8,128)(2,1)S(1)} %collective-permute-done.15.near_ref), custom_call_target="tpu_custom_call" | custom-call | flops 150994944 | bytes 1376256 | tf_op jit(solution)/shard_map/attend_own_slab/pallas_call | solution.py:204
  52.0 1.9 %attend_and_mix.1 = bf16[1,384,3072]{2,1,0:T(8,128)(2,1)} custom-call(bf16[384,256]{1,0:T(8,128)(2,1)S(1)} %project_queries.1.queries_ref, f32[384,256]{1,0:T(8,128)S(1)} %get-tuple-element.69.weighted_ref, f32[384,256]{1,0:T(8,128)S(1)} %get-tuple-element.70.mass_ref, bf16[256,512]{1,0:T(8,128)(2,1)S(1)} %collective-permute-done.17.refs_0_, ...), custom_call_target="tpu_custom_call" | custom-call | flops 704643072 | bytes 3932160 | tf_op jit(solution)/shard_map/attend_and_mix/pallas_call | solution.py:266
  (58 shorter events, 8.2 us)
Async XLA Ops:
  1.0 9.8 %collective-permute-start = (bf16[96,768]{1,0:T(8,128)(2,1)S(1)}, bf16[96,768]{1,0:T(8,128)(2,1)S(1)}, u32[]{:S(2)}, u32[]{:S(2)}) collective-permute-start(bf16[96,768]{1,0:T(8,128)(2,1)S(1)} %get-tuple-element.78), channel_id=1, source_target_pairs={{0,24},{4,28},{8,16},{12,20},{16,8},{20,12},{24,0},{28,4},{1,25},{... | collective-permute-start | bytes 442376 | tf_op jit(solution)/shard_map/ppermute | solution.py:288
  6.1 9.7 %collective-permute-start.3 = (bf16[96,768]{1,0:T(8,128)(2,1)S(1)}, bf16[96,768]{1,0:T(8,128)(2,1)S(1)}, u32[]{:S(2)}, u32[]{:S(2)}) collective-permute-start(bf16[96,768]{1,0:T(8,128)(2,1)S(1)} %get-tuple-element.78), channel_id=1, source_target_pairs={{0,8},{4,12},{8,0},{12,4},{16,24},{20,28},{24,16},{28,20},{1,9},{5... | collective-permute-start | bytes 442376 | tf_op jit(solution)/shard_map/ppermute | solution.py:288
  10.8 5.1 %collective-permute-start.1 = (bf16[96,768]{1,0:T(8,128)(2,1)S(1)}, bf16[96,768]{1,0:T(8,128)(2,1)S(1)}, u32[]{:S(2)}, u32[]{:S(2)}) collective-permute-start(bf16[96,768]{1,0:T(8,128)(2,1)S(1)} %collective-permute-done), channel_id=1, source_target_pairs={{0,1},{1,0},{2,3},{3,2},{4,6},{5,7},{6,4},{7,5},{8,9},{9,8},{10,11... | collective-permute-start | bytes 442376 | tf_op jit(solution)/shard_map/ppermute | solution.py:297
  12.5 5.1 %collective-permute-start.2 = (bf16[96,768]{1,0:T(8,128)(2,1)S(1)}, bf16[96,768]{1,0:T(8,128)(2,1)S(1)}, u32[]{:S(2)}, u32[]{:S(2)}) collective-permute-start(bf16[96,768]{1,0:T(8,128)(2,1)S(1)} %collective-permute-done), channel_id=1, source_target_pairs={{0,8},{4,12},{8,0},{12,4},{16,24},{20,28},{24,16},{28,20},{1,9},{5... | collective-permute-start | bytes 442376 | tf_op jit(solution)/shard_map/ppermute | solution.py:288
  14.3 9.2 %collective-permute-start.8 = (bf16[384,768]{1,0:T(8,128)(2,1)S(1)}, bf16[384,768]{1,0:T(8,128)(2,1)S(1)}, u32[]{:S(2)}, u32[]{:S(2)}) collective-permute-start(bf16[384,768]{1,0:T(8,128)(2,1)S(1)} %copy-done.1), channel_id=1, source_target_pairs={{0,4},{4,0},{8,12},{12,8},{16,20},{20,16},{24,28},{28,24},{1,5},{5... | collective-permute-start | bytes 1769480 | tf_op jit(solution)/shard_map/ppermute | solution.py:288
  17.7 11.5 %collective-permute-start.4 = (bf16[384,768]{1,0:T(8,128)(2,1)S(1)}, bf16[384,768]{1,0:T(8,128)(2,1)S(1)}, u32[]{:S(2)}, u32[]{:S(2)}) collective-permute-start(bf16[384,768]{1,0:T(8,128)(2,1)S(1)} %pad_maximum_fusion), channel_id=1, source_target_pairs={{0,2},{1,3},{2,0},{3,1},{4,5},{5,4},{6,7},{7,6},{8,10},{9,11},{10,... | collective-permute-start | bytes 1769480 | tf_op jit(solution)/shard_map/ppermute | solution.py:297
  19.3 7.7 %collective-permute-start.7 = (bf16[256,256]{1,0:T(8,128)(2,1)S(1)}, bf16[256,256]{1,0:T(8,128)(2,1)S(1)}, u32[]{:S(2)}, u32[]{:S(2)}) collective-permute-start(bf16[256,256]{1,0:T(8,128)(2,1)S(1)} %slice.12), channel_id=1, source_target_pairs={{0,24},{4,28},{8,16},{12,20},{16,8},{20,12},{24,0},{28,4},{1,25},{... | collective-permute-start | bytes 393224 | tf_op jit(solution)/shard_map/ppermute | solution.py:288
  23.0 5.1 %collective-permute-start.5 = (bf16[96,768]{1,0:T(8,128)(2,1)S(1)}, bf16[96,768]{1,0:T(8,128)(2,1)S(1)}, u32[]{:S(2)}, u32[]{:S(2)}) collective-permute-start(bf16[96,768]{1,0:T(8,128)(2,1)S(1)} %collective-permute-done.3), channel_id=1, source_target_pairs={{0,1},{1,0},{2,3},{3,2},{4,6},{5,7},{6,4},{7,5},{8,9},{9,8},{10,11... | collective-permute-start | bytes 442376 | tf_op jit(solution)/shard_map/ppermute | solution.py:297
  23.5 5.1 %collective-permute-start.6 = (bf16[96,768]{1,0:T(8,128)(2,1)S(1)}, bf16[96,768]{1,0:T(8,128)(2,1)S(1)}, u32[]{:S(2)}, u32[]{:S(2)}) collective-permute-start(bf16[96,768]{1,0:T(8,128)(2,1)S(1)} %get-tuple-element.59), channel_id=1, source_target_pairs={{0,8},{4,12},{8,0},{12,4},{16,24},{20,28},{24,16},{28,20},{1,9},{5... | collective-permute-start | bytes 442376 | tf_op jit(solution)/shard_map/ppermute | solution.py:288
  29.4 4.1 %collective-permute-start.9 = (bf16[576,768]{1,0:T(8,128)(2,1)S(1)}, bf16[576,768]{1,0:T(8,128)(2,1)S(1)}, u32[]{:S(2)}, u32[]{:S(2)}) collective-permute-start(bf16[576,768]{1,0:T(8,128)(2,1)S(1)} %constant_dynamic-update-slice_fusion.refs_4_), channel_id=1, source_target_pairs={{0,4},{4,0},{8,12},{12,8},{16,20},{20,16},{24,28},{28,24},{1,5},{5... | collective-permute-start | bytes 2654216 | tf_op jit(solution)/shard_map/ppermute | solution.py:288
  29.4 4.0 %collective-permute-start.10 = (bf16[384,768]{1,0:T(8,128)(2,1)S(1)}, bf16[384,768]{1,0:T(8,128)(2,1)S(1)}, u32[]{:S(2)}, u32[]{:S(2)}) collective-permute-start(bf16[384,768]{1,0:T(8,128)(2,1)S(1)} %collective-permute-done.4.refs_6_), channel_id=1, source_target_pairs={{0,4},{4,0},{8,12},{12,8},{16,20},{20,16},{24,28},{28,24},{1,5},{5... | collective-permute-start | bytes 1769480 | tf_op jit(solution)/shard_map/ppermute | solution.py:288
  30.0 7.6 %collective-permute-start.11 = (bf16[192,768]{1,0:T(8,128)(2,1)S(1)}, bf16[192,768]{1,0:T(8,128)(2,1)S(1)}, u32[]{:S(2)}, u32[]{:S(2)}) collective-permute-start(bf16[192,768]{1,0:T(8,128)(2,1)S(1)} %pad_maximum_fusion.2), channel_id=1, source_target_pairs={{0,1},{1,0},{2,3},{3,2},{4,6},{5,7},{6,4},{7,5},{8,9},{9,8},{10,11... | collective-permute-start | bytes 884744 | tf_op jit(solution)/shard_map/ppermute | solution.py:297
  31.2 6.4 %collective-permute-start.13 = (bf16[256,384]{1,0:T(8,128)(2,1)S(1)}, bf16[256,384]{1,0:T(8,128)(2,1)S(1)}, u32[]{:S(2)}, u32[]{:S(2)}) collective-permute-start(bf16[256,384]{1,0:T(8,128)(2,1)S(1)} %copy-done.2), channel_id=1, source_target_pairs={{0,4},{4,0},{8,12},{12,8},{16,20},{20,16},{24,28},{28,24},{1,5},{5... | collective-permute-start | bytes 589832 | tf_op jit(solution)/shard_map/ppermute | solution.py:288
  31.4 6.2 %collective-permute-start.12 = (bf16[256,128]{1,0:T(8,128)(2,1)S(1)}, bf16[256,128]{1,0:T(8,128)(2,1)S(1)}, u32[]{:S(2)}, u32[]{:S(2)}) collective-permute-start(bf16[256,128]{1,0:T(8,128)(2,1)S(1)} %slice.15), channel_id=1, source_target_pairs={{0,24},{4,28},{8,16},{12,20},{16,8},{20,12},{24,0},{28,4},{1,25},{... | collective-permute-start | bytes 196616 | tf_op jit(solution)/shard_map/ppermute | solution.py:288
  37.6 1.6 %collective-permute-start.14 = (bf16[192,768]{1,0:T(8,128)(2,1)S(1)}, bf16[192,768]{1,0:T(8,128)(2,1)S(1)}, u32[]{:S(2)}, u32[]{:S(2)}) collective-permute-start(bf16[192,768]{1,0:T(8,128)(2,1)S(1)} %collective-permute-done.11.refs_2_), channel_id=1, source_target_pairs={{0,4},{4,0},{8,12},{12,8},{16,20},{20,16},{24,28},{28,24},{1,5},{5... | collective-permute-start | bytes 884744 | tf_op jit(solution)/shard_map/ppermute | solution.py:288
  37.6 7.3 %collective-permute-start.19 = (bf16[256,384]{1,0:T(8,128)(2,1)S(1)}, bf16[256,384]{1,0:T(8,128)(2,1)S(1)}, u32[]{:S(2)}, u32[]{:S(2)}) collective-permute-start(bf16[256,384]{1,0:T(8,128)(2,1)S(1)} %copy-done.2), channel_id=1, source_target_pairs={{0,8},{4,12},{8,0},{12,4},{16,24},{20,28},{24,16},{28,20},{1,9},{5... | collective-permute-start | bytes 589832 | tf_op jit(solution)/shard_map/ppermute | solution.py:288
  39.7 3.1 %collective-permute-start.16 = (bf16[256,512]{1,0:T(8,128)(2,1)S(1)}, bf16[256,512]{1,0:T(8,128)(2,1)S(1)}, u32[]{:S(2)}, u32[]{:S(2)}) collective-permute-start(bf16[256,512]{1,0:T(8,128)(2,1)S(1)} %get-tuple-element.79), channel_id=1, source_target_pairs={{5,7},{6,4},{13,15},{14,12},{21,23},{22,20},{29,31},{30,28}} | collective-permute-start | bytes 786440 | tf_op jit(solution)/shard_map/ppermute | solution.py:322
  40.4 8.7 %collective-permute-start.15 = (bf16[256,512]{1,0:T(8,128)(2,1)S(1)}, bf16[256,512]{1,0:T(8,128)(2,1)S(1)}, u32[]{:S(2)}, u32[]{:S(2)}) collective-permute-start(bf16[256,512]{1,0:T(8,128)(2,1)S(1)} %get-tuple-element.80), channel_id=1, source_target_pairs={{0,1},{1,0},{2,3},{3,2},{4,5},{5,4},{6,7},{7,6},{8,9},{9,8},{10,11... | collective-permute-start | bytes 786440 | tf_op jit(solution)/shard_map/ppermute | solution.py:288
  41.4 7.5 %collective-permute-start.22 = (bf16[256,384]{1,0:T(8,128)(2,1)S(1)}, bf16[256,384]{1,0:T(8,128)(2,1)S(1)}, u32[]{:S(2)}, u32[]{:S(2)}) collective-permute-start(bf16[256,384]{1,0:T(8,128)(2,1)S(1)} %constant_dynamic-update-slice_fusion.5.refs_6_), channel_id=1, source_target_pairs={{0,8},{4,12},{8,0},{12,4},{16,24},{20,28},{24,16},{28,20},{1,9},{5... | collective-permute-start | bytes 589832 | tf_op jit(solution)/shard_map/ppermute | solution.py:288
  42.2 9.7 %collective-permute-start.18 = (bf16[256,512]{1,0:T(8,128)(2,1)S(1)}, bf16[256,512]{1,0:T(8,128)(2,1)S(1)}, u32[]{:S(2)}, u32[]{:S(2)}) collective-permute-start(bf16[256,512]{1,0:T(8,128)(2,1)S(1)} %get-tuple-element.79), channel_id=1, source_target_pairs={{1,2},{2,1},{9,10},{10,9},{17,18},{18,17},{25,26},{26,25}} | collective-permute-start | bytes 786440 | tf_op jit(solution)/shard_map/ppermute | solution.py:323
  42.9 9.1 %collective-permute-start.17 = (bf16[256,512]{1,0:T(8,128)(2,1)S(1)}, bf16[256,512]{1,0:T(8,128)(2,1)S(1)}, u32[]{:S(2)}, u32[]{:S(2)}) collective-permute-start(bf16[256,512]{1,0:T(8,128)(2,1)S(1)} %collective-permute-done.16), channel_id=1, source_target_pairs={{7,6},{4,5},{15,14},{12,13},{23,22},{20,21},{31,30},{28,29}} | collective-permute-start | bytes 786440 | tf_op jit(solution)/shard_map/ppermute | solution.py:323
  44.9 7.0 %collective-permute-start.20 = (bf16[256,384]{1,0:T(8,128)(2,1)S(1)}, bf16[256,384]{1,0:T(8,128)(2,1)S(1)}, u32[]{:S(2)}, u32[]{:S(2)}) collective-permute-start(bf16[256,384]{1,0:T(8,128)(2,1)S(1)} %collective-permute-done.19.refs_4_), channel_id=1, source_target_pairs={{0,4},{4,0},{8,12},{12,8},{16,20},{20,16},{24,28},{28,24},{1,5},{5... | collective-permute-start | bytes 589832 | tf_op jit(solution)/shard_map/ppermute | solution.py:288
  48.9 3.0 %collective-permute-start.21 = (bf16[256,384]{1,0:T(8,128)(2,1)S(1)}, bf16[256,384]{1,0:T(8,128)(2,1)S(1)}, u32[]{:S(2)}, u32[]{:S(2)}) collective-permute-start(bf16[256,384]{1,0:T(8,128)(2,1)S(1)} %constant_dynamic-update-slice_fusion.5.refs_6_), channel_id=1, source_target_pairs={{0,4},{4,0},{8,12},{12,8},{16,20},{20,16},{24,28},{28,24},{1,5},{5... | collective-permute-start | bytes 589832 | tf_op jit(solution)/shard_map/ppermute | solution.py:288
  49.1 2.9 %collective-permute-start.23 = (bf16[256,384]{1,0:T(8,128)(2,1)S(1)}, bf16[256,384]{1,0:T(8,128)(2,1)S(1)}, u32[]{:S(2)}, u32[]{:S(2)}) collective-permute-start(bf16[256,384]{1,0:T(8,128)(2,1)S(1)} %collective-permute-done.22.refs_8_), channel_id=1, source_target_pairs={{0,4},{4,0},{8,12},{12,8},{16,20},{20,16},{24,28},{28,24},{1,5},{5... | collective-permute-start | bytes 589832 | tf_op jit(solution)/shard_map/ppermute | solution.py:288
  (5 other events, 19.6 us)

commit v7 on v6

--- a/solution.py
+++ b/solution.py
@@ -215,10 +215,25 @@
     )(queries, stacked, near)
 
 
+def mix(layout, sources, attended, rows, blocks, sems, mixed_ref):
+    width, copies = blocks.shape[2], []
+    for number, (source, begin, place) in enumerate(layout()):
+        held = sources[source][:, begin : begin + width]
+        blocks[number, rows] = dot(attended[rows], held).astype(bf16)
+        copy = pltpu.make_async_copy(
+            blocks.at[number, rows],
+            mixed_ref.at[0, rows, pl.ds(pl.multiple_of(place, TILE), width)],
+            sems.at[number],
+        )
+        copy.start()
+        copies.append(copy)
+    return copies
+
+
 def attend_kernel(layout, count, arrivals, queries_ref, weighted_ref, mass_ref, *refs):
     arrived, refs = refs[:arrivals], refs[arrivals:]
     sources = refs[:count]
-    mixed_ref, far, attended, blocks, sems = refs[count:]
+    mixed_ref, far, attended, blocks, sems, late_sems = refs[count:]
     tiles = queries_ref.shape[0] // TILE
     place = lax.axis_index("frame")
     parity = place & 1
@@ -227,37 +242,36 @@
     @pl.when(jnp.logical_not(exists))
     def _():
         attended[...] = (weighted_ref[...] / mass_ref[...]).astype(bf16)
+        whole = slice(0, tiles * TILE)
+        for copy in mix(layout, sources, attended, whole, blocks, sems, mixed_ref):
+            copy.wait()
 
     for odd in (0, 1):
+        spans = [edge_span(tile, tiles, odd == 1) for tile in range(tiles)]
+        waiting = [tile for tile in range(tiles) if spans[tile].start != spans[tile].stop]
+        ready = [tile for tile in range(tiles) if tile not in waiting]
 
         @pl.when(jnp.logical_and(exists, parity == odd))
         def _():
+            copies = []
+            if ready:
+                rows = slice(ready[0] * TILE, (ready[-1] + 1) * TILE)
+                attended[rows] = (weighted_ref[rows] / mass_ref[rows]).astype(bf16)
+                copies += mix(layout, sources, attended, rows, blocks, sems, mixed_ref)
             total = arrived[0][...]
             for ref in arrived[1:]:
                 total = total + ref[...]
             far[...] = total
             for ks, vs in heads():
-                for tile in range(tiles):
+                for tile in waiting:
                     rows = slice(tile * TILE, (tile + 1) * TILE)
-                    weighted, mass = weighted_ref[rows, ks], mass_ref[rows, ks]
-                    more = edge_share(queries_ref, far, tile, tiles, odd == 1, ks, vs)
-                    if more is not None:
-                        weighted, mass = weighted + more[0], mass + more[1]
+                    more, extra = edge_share(queries_ref, far, tile, tiles, odd == 1, ks, vs)
+                    weighted, mass = weighted_ref[rows, ks] + more, mass_ref[rows, ks] + extra
                     attended[rows, ks] = (weighted / mass).astype(bf16)
-
-    width = blocks.shape[2]
-    copies = []
-    for number, (source, begin, place) in enumerate(layout()):
-        blocks[number] = dot(attended[...], sources[source][:, begin : begin + width]).astype(bf16)
-        copy = pltpu.make_async_copy(
-            blocks.at[number],
-            mixed_ref.at[0, :, pl.ds(pl.multiple_of(place, TILE), width)],
-            sems.at[number],
-        )
-        copy.start()
-        copies.append(copy)
-    for copy in copies:
-        copy.wait()
+            rows = slice(waiting[0] * TILE, (waiting[-1] + 1) * TILE)
+            copies += mix(layout, sources, attended, rows, blocks, late_sems, mixed_ref)
+            for copy in copies:
+                copy.wait()
 
 
 def attend(layout, sources, queries, own, arrived, model):
@@ -273,6 +287,7 @@
             pltpu.VMEM((rows, WIDTH), bf16),
             pltpu.VMEM((number, rows, width), bf16),
             pltpu.SemaphoreType.DMA((number,)),
+            pltpu.SemaphoreType.DMA((number,)),
         ],
         compiler_params=params(),
         cost_estimate=pl.CostEstimate(
@@ -308,9 +323,10 @@
     tail = stacked.shape[0] - BORDER
     near = lax.dynamic_slice_in_dim(stacked, (1 - odd) * tail, BORDER, 0)
     far = lax.dynamic_slice_in_dim(stacked, odd * tail, BORDER, 0)
+    axes = ("fsdp", "frame")
     straight, out, on = [], [], []
     for i in range(lax.axis_size("fsdp")):
-        for j in range(0, places, 4):
+        for j in range(0, places - 3, 4):
             for source, way, target in ((1, 3, 2), (2, 0, 1)):
                 place = i * places + j
                 if i % 2:
@@ -318,13 +334,15 @@
                     on.append((place + way, place + target))
                 else:
                     straight.append((place + source, place + target))
-    axes = ("fsdp", "frame")
     way = lax.ppermute(far, axes, out)
     arrived = [lax.ppermute(way, axes, on), lax.ppermute(far, axes, straight)]
-    if places > 4:
-        pairs = [(j, j + 1) for j in range(3, places - 1, 4)]
-        arrived.append(lax.ppermute(far, "frame", pairs + [(b, a) for a, b in pairs]))
-    return [swap(near, "frame", 1)] + arrived, way
+    rest = [j for j in range(1, places - 1, 2) if j % 4 == 3 or j >= places // 4 * 4]
+    if rest:
+        arrived.append(
+            lax.ppermute(far, "frame", [(j, j + 1) for j in rest] + [(j + 1, j) for j in rest])
+        )
+    near_pairs = [(j, j ^ 1) for j in range(places) if j ^ 1 < places]
+    return [lax.ppermute(near, "frame", near_pairs)] + arrived, way
 
 
 def split_plan(frames, modulation, w_qkv, w_out, qk_gain):

time: 54.4 us -> 54.2 us (level)
    ppermute x0 -> x1, starting transfers between devices: none -> 0.97 us  [halos(): return ([lax.ppermute(near, 'frame', near_pairs)] + arrived, way)]
    ppermute x17 -> x16, starting transfers between devices: 21.2 us -> 20.2 us  [swap(): lax.ppermute(x, axis, [(i, i ^ bits) for i in range(lax.axis_size(axis))])]
    ppermute x17 -> x16, waiting for transfers between devices: 9.78 us -> 9.77 us  [swap(): lax.ppermute(x, axis, [(i, i ^ bits) for i in range(lax.axis_size(axis))])]
where the time goes in v7:
time: 54.2 us; the launch traced here: 53.8 us
  starting transfers between devices  28.2 us (52%)
  waiting for transfers between devices  11.7 us (22%)
  Pallas kernels  9.98 us (18%)
  local copies, waits for them, and re-layouts  3.6 us (7%)
    ppermute x16, starting transfers between devices, swap(): lax.ppermute(x, axis, [(i, i ^ bits) for i in range(lax.axis_size(axis))])  20.2 us
    ppermute x16, waiting for transfers between devices, swap(): lax.ppermute(x, axis, [(i, i ^ bits) for i in range(lax.axis_size(axis))])  9.77 us
    ppermute x4, starting transfers between devices, swap_plane(): return lax.ppermute(x, ('fsdp', 'frame'), pairs)  5 us
    pallas_call x4, Pallas kernels, project(): pl.pallas_call(functools.partial(project_kernel, len(pairs), starts, kind...  3.26 us
    unnamed x15, local copies, waits for them, and re-layouts  2.49 us
    pallas_call x1, Pallas kernels, norm_rows(): pl.pallas_call(norm_kernel, grid=(rows // block,), in_specs=[pl.BlockSpec...  2.15 us
    ppermute x4, waiting for transfers between devices, swap_plane(): return lax.ppermute(x, ('fsdp', 'frame'), pairs)  1.9 us
    pallas_call x1, Pallas kernels, attend(): pl.pallas_call(functools.partial(attend_kernel, layout, len(sources), len...  1.86 us
  transfers between devices with their start and end apart: 24, of which 10 were waited for; matrix products, arithmetic and copies ran while one was open for 0% of the time, Pallas kernels for 15%

profile of v7, /device:TPU:0, one launch (start us, length us, event | category | flops | bytes accessed | tf_op | source)
XLA Modules:
  0.0 53.8 jit_solution(13145860252492227316)
XLA Ops:
  0.0 1.0 %constant_dynamic-slice_fusion.2 = (bf16[96,768]{1,0:T(8,128)(2,1)S(1)}, bf16[96,768]{1,0:T(8,128)(2,1)S(1)}) fusion(bf16[384,768]{1,0:T(8,128)(2,1)} %refs_2_.2, s32[]{:T(128)S(6)} %select_n.13, s32[]{:T(128)S(6)} %select_n.12), kind=kLoop, calls=%fused_computation.12 | loop fusion | bytes 589832 | tf_op jit(solution)/shard_map/dynamic_slice | solution.py:402
  1.0 5.1 %collective-permute-start = (bf16[96,768]{1,0:T(8,128)(2,1)S(1)}, bf16[96,768]{1,0:T(8,128)(2,1)S(1)}, u32[]{:S(2)}, u32[]{:S(2)}) collective-permute-start(bf16[96,768]{1,0:T(8,128)(2,1)S(1)} %get-tuple-element.78), channel_id=1, source_target_pairs={{0,24},{4,28},{8,16},{12,20},{16,8},{20,12},{24,0},{28,4},{1,25},{... | collective-permute-start | bytes 442376 | tf_op jit(solution)/shard_map/ppermute | solution.py:303
  6.1 1.7 %copy-done = bf16[1,384,3072]{2,1,0:T(8,128)(2,1)S(1)} copy-done((bf16[1,384,3072]{2,1,0:T(8,128)(2,1)S(1)}, bf16[1,384,3072]{2,1,0:T(8,128)(2,1)}, u32[]{:S(2)}) %copy-start) | copy-done | bytes 2359320
  8.5 2.2 %layer_norm.1.normed_ref.refs_0_.refs_1_ = bf16[384,3072]{1,0:T(8,128)(2,1)S(1)} custom-call(bf16[384,3072]{1,0:T(8,128)(2,1)S(1)} %bitcast.2, f32[2,3072]{1,0:T(2,128)S(1)} %bitcast.3), custom_call_target="tpu_custom_call" | custom-call | flops 11796480 | bytes 4718592 | tf_op jit(solution)/shard_map/layer_norm/pallas_call | solution.py:49
  10.8 1.7 %collective-permute-start.1 = (bf16[96,768]{1,0:T(8,128)(2,1)S(1)}, bf16[96,768]{1,0:T(8,128)(2,1)S(1)}, u32[]{:S(2)}, u32[]{:S(2)}) collective-permute-start(bf16[96,768]{1,0:T(8,128)(2,1)S(1)} %collective-permute-done), channel_id=1, source_target_pairs={{0,1},{1,0},{2,3},{3,2},{4,6},{5,7},{6,4},{7,5},{8,9},{9,8},{10,11... | collective-permute-start | bytes 442376 | tf_op jit(solution)/shard_map/ppermute | solution.py:312
  12.5 1.8 %collective-permute-start.2 = (bf16[96,768]{1,0:T(8,128)(2,1)S(1)}, bf16[96,768]{1,0:T(8,128)(2,1)S(1)}, u32[]{:S(2)}, u32[]{:S(2)}) collective-permute-start(bf16[96,768]{1,0:T(8,128)(2,1)S(1)} %collective-permute-done), channel_id=1, source_target_pairs={{0,8},{4,12},{8,0},{12,4},{16,24},{20,28},{24,16},{28,20},{1,9},{5... | collective-permute-start | bytes 442376 | tf_op jit(solution)/shard_map/ppermute | solution.py:303
  14.3 1.4 %arrange.1 = (bf16[384,576]{1,0:T(8,128)(2,1)S(1)}, bf16[384,576]{1,0:T(8,128)(2,1)S(1)}, bf16[384,384]{1,0:T(8,128)(2,1)S(1)}, bf16[384,384]{1,0:T(8,128)(2,1)S...) custom-call(bf16[384,3072]{1,0:T(8,128)(2,1)S(1)} %layer_norm.1.normed_ref.refs_0_.refs_1_), custom_call_target="tpu_custom_call" | custom-call | flops 1207959552 | bytes 4718592 | tf_op jit(solution)/shard_map/arrange/pallas_call | solution.py:140
  16.0 1.7 %collective-permute-done.2 = bf16[96,768]{1,0:T(8,128)(2,1)S(1)} collective-permute-done((bf16[96,768]{1,0:T(8,128)(2,1)S(1)}, bf16[96,768]{1,0:T(8,128)(2,1)S(1)}, u32[]{:S(2)}, u32[]{:S(2)}) %collective-permute-start.2) | collective-permute-done | bytes 147488 | tf_op jit(solution)/shard_map/ppermute | solution.py:303
  17.7 1.6 %collective-permute-start.4 = (bf16[384,768]{1,0:T(8,128)(2,1)S(1)}, bf16[384,768]{1,0:T(8,128)(2,1)S(1)}, u32[]{:S(2)}, u32[]{:S(2)}) collective-permute-start(bf16[384,768]{1,0:T(8,128)(2,1)S(1)} %pad_maximum_fusion), channel_id=1, source_target_pairs={{0,2},{1,3},{2,0},{3,1},{4,5},{5,4},{6,7},{7,6},{8,10},{9,11},{10,... | collective-permute-start | bytes 1769480 | tf_op jit(solution)/shard_map/ppermute | solution.py:312
  19.3 3.7 %collective-permute-start.7 = (bf16[256,256]{1,0:T(8,128)(2,1)S(1)}, bf16[256,256]{1,0:T(8,128)(2,1)S(1)}, u32[]{:S(2)}, u32[]{:S(2)}) collective-permute-start(bf16[256,256]{1,0:T(8,128)(2,1)S(1)} %slice.12), channel_id=1, source_target_pairs={{0,24},{4,28},{8,16},{12,20},{16,8},{20,12},{24,0},{28,4},{1,25},{... | collective-permute-start | bytes 393224 | tf_op jit(solution)/shard_map/ppermute | solution.py:303
  24.4 2.7 %collective-permute-done.7 = bf16[256,256]{1,0:T(8,128)(2,1)S(1)} collective-permute-done((bf16[256,256]{1,0:T(8,128)(2,1)S(1)}, bf16[256,256]{1,0:T(8,128)(2,1)S(1)}, u32[]{:S(2)}, u32[]{:S(2)}) %collective-permute-start.7) | collective-permute-done | bytes 131104 | tf_op jit(solution)/shard_map/ppermute | solution.py:303
  27.0 1.1 %collective-permute-done.5 = bf16[96,768]{1,0:T(8,128)(2,1)S(1)} collective-permute-done((bf16[96,768]{1,0:T(8,128)(2,1)S(1)}, bf16[96,768]{1,0:T(8,128)(2,1)S(1)}, u32[]{:S(2)}, u32[]{:S(2)}) %collective-permute-start.5) | collective-permute-done | bytes 147488 | tf_op jit(solution)/shard_map/ppermute | solution.py:312
  30.0 1.2 %collective-permute-start.11 = (bf16[192,768]{1,0:T(8,128)(2,1)S(1)}, bf16[192,768]{1,0:T(8,128)(2,1)S(1)}, u32[]{:S(2)}, u32[]{:S(2)}) collective-permute-start(bf16[192,768]{1,0:T(8,128)(2,1)S(1)} %pad_maximum_fusion.2), channel_id=1, source_target_pairs={{0,1},{1,0},{2,3},{3,2},{4,6},{5,7},{6,4},{7,5},{8,9},{9,8},{10,11... | collective-permute-start | bytes 884744 | tf_op jit(solution)/shard_map/ppermute | solution.py:312
  31.4 2.1 %collective-permute-start.12 = (bf16[256,128]{1,0:T(8,128)(2,1)S(1)}, bf16[256,128]{1,0:T(8,128)(2,1)S(1)}, u32[]{:S(2)}, u32[]{:S(2)}) collective-permute-start(bf16[256,128]{1,0:T(8,128)(2,1)S(1)} %slice.15), channel_id=1, source_target_pairs={{0,24},{4,28},{8,16},{12,20},{16,8},{20,12},{24,0},{28,4},{1,25},{... | collective-permute-start | bytes 196616 | tf_op jit(solution)/shard_map/ppermute | solution.py:303
  33.4 1.7 %project_mid.1.refs_4_ = f32[384,768]{1,0:T(8,128)S(1)} custom-call(f32[2,128]{1,0:T(2,128)S(1)} %copy-done.4, bf16[384,576]{1,0:T(8,128)(2,1)S(1)} %get-tuple-element.51.refs_0_, bf16[384,576]{1,0:T(8,128)(2,1)S(1)} %get-tuple-element.52.refs_1_, bf16[384,384]{1,0:T(8,128)(2,1)S(1)} %get-tuple-element.53.refs_2_, ...), custom_call_target="tpu_custom_call" | custom-call | flops 1132462080 | bytes 4423680 | tf_op jit(solution)/shard_map/project_mid/pallas_call | solution.py:100
  35.2 2.5 %collective-permute-done.12 = bf16[256,128]{1,0:T(8,128)(2,1)S(1)} collective-permute-done((bf16[256,128]{1,0:T(8,128)(2,1)S(1)}, bf16[256,128]{1,0:T(8,128)(2,1)S(1)}, u32[]{:S(2)}, u32[]{:S(2)}) %collective-permute-start.12) | collective-permute-done | bytes 65568 | tf_op jit(solution)/shard_map/ppermute | solution.py:303
  38.3 0.9 %collective-permute-done.14.refs_3_ = bf16[192,768]{1,0:T(8,128)(2,1)S(1)} collective-permute-done((bf16[192,768]{1,0:T(8,128)(2,1)S(1)}, bf16[192,768]{1,0:T(8,128)(2,1)S(1)}, u32[]{:S(2)}, u32[]{:S(2)}) %collective-permute-start.14) | collective-permute-done | bytes 294944 | tf_op jit(solution)/shard_map/ppermute | solution.py:303
  40.4 1.0 %collective-permute-start.15 = (bf16[256,512]{1,0:T(8,128)(2,1)S(1)}, bf16[256,512]{1,0:T(8,128)(2,1)S(1)}, u32[]{:S(2)}, u32[]{:S(2)}) collective-permute-start(bf16[256,512]{1,0:T(8,128)(2,1)S(1)} %get-tuple-element.80), channel_id=1, source_target_pairs={{0,1},{1,0},{2,3},{3,2},{4,5},{5,4},{6,7},{7,6},{8,9},{9,8},{10,11... | collective-permute-start | bytes 786440 | tf_op jit(solution)/shard_map/ppermute | solution.py:345
  41.4 0.8 %collective-permute-start.22 = (bf16[256,384]{1,0:T(8,128)(2,1)S(1)}, bf16[256,384]{1,0:T(8,128)(2,1)S(1)}, u32[]{:S(2)}, u32[]{:S(2)}) collective-permute-start(bf16[256,384]{1,0:T(8,128)(2,1)S(1)} %constant_dynamic-update-slice_fusion.5.refs_6_), channel_id=1, source_target_pairs={{0,8},{4,12},{8,0},{12,4},{16,24},{20,28},{24,16},{28,20},{1,9},{5... | collective-permute-start | bytes 589832 | tf_op jit(solution)/shard_map/ppermute | solution.py:303
  43.5 1.4 %collective-permute-done.19.refs_4_ = bf16[256,384]{1,0:T(8,128)(2,1)S(1)} collective-permute-done((bf16[256,384]{1,0:T(8,128)(2,1)S(1)}, bf16[256,384]{1,0:T(8,128)(2,1)S(1)}, u32[]{:S(2)}, u32[]{:S(2)}) %collective-permute-start.19) | collective-permute-done | bytes 196640 | tf_op jit(solution)/shard_map/ppermute | solution.py:303
  44.9 4.0 %collective-permute-start.20 = (bf16[256,384]{1,0:T(8,128)(2,1)S(1)}, bf16[256,384]{1,0:T(8,128)(2,1)S(1)}, u32[]{:S(2)}, u32[]{:S(2)}) collective-permute-start(bf16[256,384]{1,0:T(8,128)(2,1)S(1)} %collective-permute-done.19.refs_4_), channel_id=1, source_target_pairs={{0,4},{4,0},{8,12},{12,8},{16,20},{20,16},{24,28},{28,24},{1,5},{5... | collective-permute-start | bytes 589832 | tf_op jit(solution)/shard_map/ppermute | solution.py:303
  49.1 1.2 %collective-permute-start.23 = (bf16[256,384]{1,0:T(8,128)(2,1)S(1)}, bf16[256,384]{1,0:T(8,128)(2,1)S(1)}, u32[]{:S(2)}, u32[]{:S(2)}) collective-permute-start(bf16[256,384]{1,0:T(8,128)(2,1)S(1)} %collective-permute-done.22.refs_8_), channel_id=1, source_target_pairs={{0,4},{4,0},{8,12},{12,8},{16,20},{20,16},{24,28},{28,24},{1,5},{5... | collective-permute-start | bytes 589832 | tf_op jit(solution)/shard_map/ppermute | solution.py:303
  50.6 1.3 %attend_own_slab.1 = (f32[384,256]{1,0:T(8,128)S(1)}, f32[384,256]{1,0:T(8,128)S(1)}) custom-call(bf16[384,256]{1,0:T(8,128)(2,1)S(1)} %project_queries.1.queries_ref, bf16[384,512]{1,0:T(8,128)(2,1)S(1)} %project_keys_values.1.stacked_ref, bf16[256,512]{1,0:T(8,128)(2,1)S(1)} %collective-permute-done.15.near_ref), custom_call_target="tpu_custom_call" | custom-call | flops 150994944 | bytes 1376256 | tf_op jit(solution)/shard_map/attend_own_slab/pallas_call | solution.py:204
  52.0 1.9 %attend_and_mix.1 = bf16[1,384,3072]{2,1,0:T(8,128)(2,1)} custom-call(bf16[384,256]{1,0:T(8,128)(2,1)S(1)} %project_queries.1.queries_ref, f32[384,256]{1,0:T(8,128)S(1)} %get-tuple-element.69.weighted_ref, f32[384,256]{1,0:T(8,128)S(1)} %get-tuple-element.70.mass_ref, bf16[256,512]{1,0:T(8,128)(2,1)S(1)} %collective-permute-done.17.refs_0_, ...), custom_call_target="tpu_custom_call" | custom-call | flops 704643072 | bytes 3932160 | tf_op jit(solution)/shard_map/attend_and_mix/pallas_call | solution.py:280
  (58 shorter events, 8.2 us)
Async XLA Ops:
  1.0 9.8 %collective-permute-start = (bf16[96,768]{1,0:T(8,128)(2,1)S(1)}, bf16[96,768]{1,0:T(8,128)(2,1)S(1)}, u32[]{:S(2)}, u32[]{:S(2)}) collective-permute-start(bf16[96,768]{1,0:T(8,128)(2,1)S(1)} %get-tuple-element.78), channel_id=1, source_target_pairs={{0,24},{4,28},{8,16},{12,20},{16,8},{20,12},{24,0},{28,4},{1,25},{... | collective-permute-start | bytes 442376 | tf_op jit(solution)/shard_map/ppermute | solution.py:303
  6.1 9.7 %collective-permute-start.3 = (bf16[96,768]{1,0:T(8,128)(2,1)S(1)}, bf16[96,768]{1,0:T(8,128)(2,1)S(1)}, u32[]{:S(2)}, u32[]{:S(2)}) collective-permute-start(bf16[96,768]{1,0:T(8,128)(2,1)S(1)} %get-tuple-element.78), channel_id=1, source_target_pairs={{0,8},{4,12},{8,0},{12,4},{16,24},{20,28},{24,16},{28,20},{1,9},{5... | collective-permute-start | bytes 442376 | tf_op jit(solution)/shard_map/ppermute | solution.py:303
  10.8 5.1 %collective-permute-start.1 = (bf16[96,768]{1,0:T(8,128)(2,1)S(1)}, bf16[96,768]{1,0:T(8,128)(2,1)S(1)}, u32[]{:S(2)}, u32[]{:S(2)}) collective-permute-start(bf16[96,768]{1,0:T(8,128)(2,1)S(1)} %collective-permute-done), channel_id=1, source_target_pairs={{0,1},{1,0},{2,3},{3,2},{4,6},{5,7},{6,4},{7,5},{8,9},{9,8},{10,11... | collective-permute-start | bytes 442376 | tf_op jit(solution)/shard_map/ppermute | solution.py:312
  12.5 5.1 %collective-permute-start.2 = (bf16[96,768]{1,0:T(8,128)(2,1)S(1)}, bf16[96,768]{1,0:T(8,128)(2,1)S(1)}, u32[]{:S(2)}, u32[]{:S(2)}) collective-permute-start(bf16[96,768]{1,0:T(8,128)(2,1)S(1)} %collective-permute-done), channel_id=1, source_target_pairs={{0,8},{4,12},{8,0},{12,4},{16,24},{20,28},{24,16},{28,20},{1,9},{5... | collective-permute-start | bytes 442376 | tf_op jit(solution)/shard_map/ppermute | solution.py:303
  14.3 9.2 %collective-permute-start.8 = (bf16[384,768]{1,0:T(8,128)(2,1)S(1)}, bf16[384,768]{1,0:T(8,128)(2,1)S(1)}, u32[]{:S(2)}, u32[]{:S(2)}) collective-permute-start(bf16[384,768]{1,0:T(8,128)(2,1)S(1)} %copy-done.1), channel_id=1, source_target_pairs={{0,4},{4,0},{8,12},{12,8},{16,20},{20,16},{24,28},{28,24},{1,5},{5... | collective-permute-start | bytes 1769480 | tf_op jit(solution)/shard_map/ppermute | solution.py:303
  17.7 11.5 %collective-permute-start.4 = (bf16[384,768]{1,0:T(8,128)(2,1)S(1)}, bf16[384,768]{1,0:T(8,128)(2,1)S(1)}, u32[]{:S(2)}, u32[]{:S(2)}) collective-permute-start(bf16[384,768]{1,0:T(8,128)(2,1)S(1)} %pad_maximum_fusion), channel_id=1, source_target_pairs={{0,2},{1,3},{2,0},{3,1},{4,5},{5,4},{6,7},{7,6},{8,10},{9,11},{10,... | collective-permute-start | bytes 1769480 | tf_op jit(solution)/shard_map/ppermute | solution.py:312
  19.3 7.7 %collective-permute-start.7 = (bf16[256,256]{1,0:T(8,128)(2,1)S(1)}, bf16[256,256]{1,0:T(8,128)(2,1)S(1)}, u32[]{:S(2)}, u32[]{:S(2)}) collective-permute-start(bf16[256,256]{1,0:T(8,128)(2,1)S(1)} %slice.12), channel_id=1, source_target_pairs={{0,24},{4,28},{8,16},{12,20},{16,8},{20,12},{24,0},{28,4},{1,25},{... | collective-permute-start | bytes 393224 | tf_op jit(solution)/shard_map/ppermute | solution.py:303
  23.0 5.1 %collective-permute-start.5 = (bf16[96,768]{1,0:T(8,128)(2,1)S(1)}, bf16[96,768]{1,0:T(8,128)(2,1)S(1)}, u32[]{:S(2)}, u32[]{:S(2)}) collective-permute-start(bf16[96,768]{1,0:T(8,128)(2,1)S(1)} %collective-permute-done.3), channel_id=1, source_target_pairs={{0,1},{1,0},{2,3},{3,2},{4,6},{5,7},{6,4},{7,5},{8,9},{9,8},{10,11... | collective-permute-start | bytes 442376 | tf_op jit(solution)/shard_map/ppermute | solution.py:312
  23.5 5.1 %collective-permute-start.6 = (bf16[96,768]{1,0:T(8,128)(2,1)S(1)}, bf16[96,768]{1,0:T(8,128)(2,1)S(1)}, u32[]{:S(2)}, u32[]{:S(2)}) collective-permute-start(bf16[96,768]{1,0:T(8,128)(2,1)S(1)} %get-tuple-element.59), channel_id=1, source_target_pairs={{0,8},{4,12},{8,0},{12,4},{16,24},{20,28},{24,16},{28,20},{1,9},{5... | collective-permute-start | bytes 442376 | tf_op jit(solution)/shard_map/ppermute | solution.py:303
  29.4 4.1 %collective-permute-start.9 = (bf16[576,768]{1,0:T(8,128)(2,1)S(1)}, bf16[576,768]{1,0:T(8,128)(2,1)S(1)}, u32[]{:S(2)}, u32[]{:S(2)}) collective-permute-start(bf16[576,768]{1,0:T(8,128)(2,1)S(1)} %constant_dynamic-update-slice_fusion.refs_4_), channel_id=1, source_target_pairs={{0,4},{4,0},{8,12},{12,8},{16,20},{20,16},{24,28},{28,24},{1,5},{5... | collective-permute-start | bytes 2654216 | tf_op jit(solution)/shard_map/ppermute | solution.py:303
  29.4 4.0 %collective-permute-start.10 = (bf16[384,768]{1,0:T(8,128)(2,1)S(1)}, bf16[384,768]{1,0:T(8,128)(2,1)S(1)}, u32[]{:S(2)}, u32[]{:S(2)}) collective-permute-start(bf16[384,768]{1,0:T(8,128)(2,1)S(1)} %collective-permute-done.4.refs_6_), channel_id=1, source_target_pairs={{0,4},{4,0},{8,12},{12,8},{16,20},{20,16},{24,28},{28,24},{1,5},{5... | collective-permute-start | bytes 1769480 | tf_op jit(solution)/shard_map/ppermute | solution.py:303
  30.0 7.6 %collective-permute-start.11 = (bf16[192,768]{1,0:T(8,128)(2,1)S(1)}, bf16[192,768]{1,0:T(8,128)(2,1)S(1)}, u32[]{:S(2)}, u32[]{:S(2)}) collective-permute-start(bf16[192,768]{1,0:T(8,128)(2,1)S(1)} %pad_maximum_fusion.2), channel_id=1, source_target_pairs={{0,1},{1,0},{2,3},{3,2},{4,6},{5,7},{6,4},{7,5},{8,9},{9,8},{10,11... | collective-permute-start | bytes 884744 | tf_op jit(solution)/shard_map/ppermute | solution.py:312
  31.2 6.4 %collective-permute-start.13 = (bf16[256,384]{1,0:T(8,128)(2,1)S(1)}, bf16[256,384]{1,0:T(8,128)(2,1)S(1)}, u32[]{:S(2)}, u32[]{:S(2)}) collective-permute-start(bf16[256,384]{1,0:T(8,128)(2,1)S(1)} %copy-done.2), channel_id=1, source_target_pairs={{0,4},{4,0},{8,12},{12,8},{16,20},{20,16},{24,28},{28,24},{1,5},{5... | collective-permute-start | bytes 589832 | tf_op jit(solution)/shard_map/ppermute | solution.py:303
  31.4 6.2 %collective-permute-start.12 = (bf16[256,128]{1,0:T(8,128)(2,1)S(1)}, bf16[256,128]{1,0:T(8,128)(2,1)S(1)}, u32[]{:S(2)}, u32[]{:S(2)}) collective-permute-start(bf16[256,128]{1,0:T(8,128)(2,1)S(1)} %slice.15), channel_id=1, source_target_pairs={{0,24},{4,28},{8,16},{12,20},{16,8},{20,12},{24,0},{28,4},{1,25},{... | collective-permute-start | bytes 196616 | tf_op jit(solution)/shard_map/ppermute | solution.py:303
  37.6 1.6 %collective-permute-start.14 = (bf16[192,768]{1,0:T(8,128)(2,1)S(1)}, bf16[192,768]{1,0:T(8,128)(2,1)S(1)}, u32[]{:S(2)}, u32[]{:S(2)}) collective-permute-start(bf16[192,768]{1,0:T(8,128)(2,1)S(1)} %collective-permute-done.11.refs_2_), channel_id=1, source_target_pairs={{0,4},{4,0},{8,12},{12,8},{16,20},{20,16},{24,28},{28,24},{1,5},{5... | collective-permute-start | bytes 884744 | tf_op jit(solution)/shard_map/ppermute | solution.py:303
  37.6 7.3 %collective-permute-start.19 = (bf16[256,384]{1,0:T(8,128)(2,1)S(1)}, bf16[256,384]{1,0:T(8,128)(2,1)S(1)}, u32[]{:S(2)}, u32[]{:S(2)}) collective-permute-start(bf16[256,384]{1,0:T(8,128)(2,1)S(1)} %copy-done.2), channel_id=1, source_target_pairs={{0,8},{4,12},{8,0},{12,4},{16,24},{20,28},{24,16},{28,20},{1,9},{5... | collective-permute-start | bytes 589832 | tf_op jit(solution)/shard_map/ppermute | solution.py:303
  39.7 3.1 %collective-permute-start.16 = (bf16[256,512]{1,0:T(8,128)(2,1)S(1)}, bf16[256,512]{1,0:T(8,128)(2,1)S(1)}, u32[]{:S(2)}, u32[]{:S(2)}) collective-permute-start(bf16[256,512]{1,0:T(8,128)(2,1)S(1)} %get-tuple-element.79), channel_id=1, source_target_pairs={{5,7},{6,4},{13,15},{14,12},{21,23},{22,20},{29,31},{30,28}} | collective-permute-start | bytes 786440 | tf_op jit(solution)/shard_map/ppermute | solution.py:337
  40.4 8.7 %collective-permute-start.15 = (bf16[256,512]{1,0:T(8,128)(2,1)S(1)}, bf16[256,512]{1,0:T(8,128)(2,1)S(1)}, u32[]{:S(2)}, u32[]{:S(2)}) collective-permute-start(bf16[256,512]{1,0:T(8,128)(2,1)S(1)} %get-tuple-element.80), channel_id=1, source_target_pairs={{0,1},{1,0},{2,3},{3,2},{4,5},{5,4},{6,7},{7,6},{8,9},{9,8},{10,11... | collective-permute-start | bytes 786440 | tf_op jit(solution)/shard_map/ppermute | solution.py:345
  41.4 7.5 %collective-permute-start.22 = (bf16[256,384]{1,0:T(8,128)(2,1)S(1)}, bf16[256,384]{1,0:T(8,128)(2,1)S(1)}, u32[]{:S(2)}, u32[]{:S(2)}) collective-permute-start(bf16[256,384]{1,0:T(8,128)(2,1)S(1)} %constant_dynamic-update-slice_fusion.5.refs_6_), channel_id=1, source_target_pairs={{0,8},{4,12},{8,0},{12,4},{16,24},{20,28},{24,16},{28,20},{1,9},{5... | collective-permute-start | bytes 589832 | tf_op jit(solution)/shard_map/ppermute | solution.py:303
  42.2 9.7 %collective-permute-start.18 = (bf16[256,512]{1,0:T(8,128)(2,1)S(1)}, bf16[256,512]{1,0:T(8,128)(2,1)S(1)}, u32[]{:S(2)}, u32[]{:S(2)}) collective-permute-start(bf16[256,512]{1,0:T(8,128)(2,1)S(1)} %get-tuple-element.79), channel_id=1, source_target_pairs={{1,2},{2,1},{9,10},{10,9},{17,18},{18,17},{25,26},{26,25}} | collective-permute-start | bytes 786440 | tf_op jit(solution)/shard_map/ppermute | solution.py:338
  42.9 9.1 %collective-permute-start.17 = (bf16[256,512]{1,0:T(8,128)(2,1)S(1)}, bf16[256,512]{1,0:T(8,128)(2,1)S(1)}, u32[]{:S(2)}, u32[]{:S(2)}) collective-permute-start(bf16[256,512]{1,0:T(8,128)(2,1)S(1)} %collective-permute-done.16), channel_id=1, source_target_pairs={{7,6},{4,5},{15,14},{12,13},{23,22},{20,21},{31,30},{28,29}} | collective-permute-start | bytes 786440 | tf_op jit(solution)/shard_map/ppermute | solution.py:338
  44.9 7.0 %collective-permute-start.20 = (bf16[256,384]{1,0:T(8,128)(2,1)S(1)}, bf16[256,384]{1,0:T(8,128)(2,1)S(1)}, u32[]{:S(2)}, u32[]{:S(2)}) collective-permute-start(bf16[256,384]{1,0:T(8,128)(2,1)S(1)} %collective-permute-done.19.refs_4_), channel_id=1, source_target_pairs={{0,4},{4,0},{8,12},{12,8},{16,20},{20,16},{24,28},{28,24},{1,5},{5... | collective-permute-start | bytes 589832 | tf_op jit(solution)/shard_map/ppermute | solution.py:303
  48.9 3.0 %collective-permute-start.21 = (bf16[256,384]{1,0:T(8,128)(2,1)S(1)}, bf16[256,384]{1,0:T(8,128)(2,1)S(1)}, u32[]{:S(2)}, u32[]{:S(2)}) collective-permute-start(bf16[256,384]{1,0:T(8,128)(2,1)S(1)} %constant_dynamic-update-slice_fusion.5.refs_6_), channel_id=1, source_target_pairs={{0,4},{4,0},{8,12},{12,8},{16,20},{20,16},{24,28},{28,24},{1,5},{5... | collective-permute-start | bytes 589832 | tf_op jit(solution)/shard_map/ppermute | solution.py:303
  49.1 2.9 %collective-permute-start.23 = (bf16[256,384]{1,0:T(8,128)(2,1)S(1)}, bf16[256,384]{1,0:T(8,128)(2,1)S(1)}, u32[]{:S(2)}, u32[]{:S(2)}) collective-permute-start(bf16[256,384]{1,0:T(8,128)(2,1)S(1)} %collective-permute-done.22.refs_8_), channel_id=1, source_target_pairs={{0,4},{4,0},{8,12},{12,8},{16,20},{20,16},{24,28},{28,24},{1,5},{5... | collective-permute-start | bytes 589832 | tf_op jit(solution)/shard_map/ppermute | solution.py:303
  (5 other events, 19.6 us)

commit v8 on v7

--- a/solution.py
+++ b/solution.py
@@ -408,8 +408,8 @@
     two = swap_plane(jnp.concatenate([one, one_rest, late], axis=0), 1)
     near_rest = swap_plane(near, 0)
     across = swap(next_part, "fsdp", 2)
-    cut = 2 * (shard_columns // TILE) // 3 * TILE
-    wides = [swap(w_out[:, :cut], "fsdp", 2 * k) for k in front]
+    cut = 7 * WIDTH // 8
+    wides = [swap(w_out[:cut], "fsdp", 2 * k) for k in front]
     total = project(
         [(normed, w_qkv), (normed, other_qkv)], qk_gain, (0, columns), "project_own", own_places
     )
@@ -419,7 +419,7 @@
 
     relayed = two[2 * nf * quarter : (2 * nf + nb) * quarter]
     three = swap_plane(jnp.concatenate([late[: nb * quarter], relayed], axis=0), 0)
-    narrows = [swap(w_out[:, cut:], "fsdp", 2 * k) for k in front]
+    narrows = [swap(w_out[cut:], "fsdp", 2 * k) for k in front]
     kept = jnp.concatenate([one, one_rest, late, across, near_rest], axis=0)
     pieces = [kept, swap(kept, "fsdp", 1), two, swap(two, "fsdp", 1)]
     total = project(
@@ -434,7 +434,7 @@
     )
     queries = project(last, qk_gain, (0, WIDTH), "project_queries", kinds=(0,), total=total)
 
-    joined = [jnp.concatenate(pair, axis=1) for pair in zip(wides, narrows)]
+    joined = [jnp.concatenate(pair, axis=0) for pair in zip(wides, narrows)]
     sources = [w_out, other_out]
     edges, way = halos(stacked)
     for x in [swap(w_out, "fsdp", 2)] + joined + [swap(x, "fsdp", 2) for x in joined]:

time: 54.2 us -> 53.4 us (0.985)
  waiting for transfers between devices: 11.7 us -> 10.7 us
    ppermute x4, waiting for transfers between devices: 1.9 us -> 0.48 us  [swap_plane(): return lax.ppermute(x, ('fsdp', 'frame'), pairs)]
  transfers between devices with their start and end apart: 24 -> 24, of which waited for: 10 -> 9; matrix products, arithmetic and copies ran while one was open for 0% -> 0% of each run, Pallas kernels for 15% -> 15%
where the time goes in v8:
time: 53.4 us; the launch traced here: 53 us
  starting transfers between devices  28.3 us (53%)
  waiting for transfers between devices  10.7 us (20%)
  Pallas kernels  9.99 us (19%)
  local copies, waits for them, and re-layouts  3.6 us (7%)
    ppermute x16, starting transfers between devices, swap(): lax.ppermute(x, axis, [(i, i ^ bits) for i in range(lax.axis_size(axis))])  20.5 us
    ppermute x16, waiting for transfers between devices, swap(): lax.ppermute(x, axis, [(i, i ^ bits) for i in range(lax.axis_size(axis))])  10.2 us
    ppermute x4, starting transfers between devices, swap_plane(): return lax.ppermute(x, ('fsdp', 'frame'), pairs)  4.83 us
    pallas_call x4, Pallas kernels, project(): pl.pallas_call(functools.partial(project_kernel, len(pairs), starts, kind...  3.26 us
    unnamed x15, local copies, waits for them, and re-layouts  2.49 us
    pallas_call x1, Pallas kernels, norm_rows(): pl.pallas_call(norm_kernel, grid=(rows // block,), in_specs=[pl.BlockSpec...  2.15 us
    pallas_call x1, Pallas kernels, attend(): pl.pallas_call(functools.partial(attend_kernel, layout, len(sources), len...  1.86 us
    pallas_call x1, Pallas kernels, arrange(): pl.pallas_call(functools.partial(arrange_kernel, starts, order, homes), i...  1.42 us
  transfers between devices with their start and end apart: 24, of which 9 were waited for; matrix products, arithmetic and copies ran while one was open for 0% of the time, Pallas kernels for 15%

profile of v8, /device:TPU:0, one launch (start us, length us, event | category | flops | bytes accessed | tf_op | source)
XLA Modules:
  0.0 53.0 jit_solution(17034972018447815148)
XLA Ops:
  0.0 1.0 %constant_dynamic-slice_fusion.2 = (bf16[96,768]{1,0:T(8,128)(2,1)S(1)}, bf16[96,768]{1,0:T(8,128)(2,1)S(1)}) fusion(bf16[384,768]{1,0:T(8,128)(2,1)} %refs_2_.2, s32[]{:T(128)S(6)} %select_n.13, s32[]{:T(128)S(6)} %select_n.12), kind=kLoop, calls=%fused_computation.12 | loop fusion | bytes 589832 | tf_op jit(solution)/shard_map/dynamic_slice | solution.py:402
  1.0 5.1 %collective-permute-start = (bf16[96,768]{1,0:T(8,128)(2,1)S(1)}, bf16[96,768]{1,0:T(8,128)(2,1)S(1)}, u32[]{:S(2)}, u32[]{:S(2)}) collective-permute-start(bf16[96,768]{1,0:T(8,128)(2,1)S(1)} %get-tuple-element.78), channel_id=1, source_target_pairs={{0,24},{4,28},{8,16},{12,20},{16,8},{20,12},{24,0},{28,4},{1,25},{... | collective-permute-start | bytes 442376 | tf_op jit(solution)/shard_map/ppermute | solution.py:303
  6.1 1.7 %copy-done = bf16[1,384,3072]{2,1,0:T(8,128)(2,1)S(1)} copy-done((bf16[1,384,3072]{2,1,0:T(8,128)(2,1)S(1)}, bf16[1,384,3072]{2,1,0:T(8,128)(2,1)}, u32[]{:S(2)}) %copy-start) | copy-done | bytes 2359320
  8.5 2.2 %layer_norm.1.normed_ref.refs_0_.refs_1_ = bf16[384,3072]{1,0:T(8,128)(2,1)S(1)} custom-call(bf16[384,3072]{1,0:T(8,128)(2,1)S(1)} %bitcast.2, f32[2,3072]{1,0:T(2,128)S(1)} %bitcast.3), custom_call_target="tpu_custom_call" | custom-call | flops 11796480 | bytes 4718592 | tf_op jit(solution)/shard_map/layer_norm/pallas_call | solution.py:49
  10.8 1.7 %collective-permute-start.1 = (bf16[96,768]{1,0:T(8,128)(2,1)S(1)}, bf16[96,768]{1,0:T(8,128)(2,1)S(1)}, u32[]{:S(2)}, u32[]{:S(2)}) collective-permute-start(bf16[96,768]{1,0:T(8,128)(2,1)S(1)} %collective-permute-done), channel_id=1, source_target_pairs={{0,1},{1,0},{2,3},{3,2},{4,6},{5,7},{6,4},{7,5},{8,9},{9,8},{10,11... | collective-permute-start | bytes 442376 | tf_op jit(solution)/shard_map/ppermute | solution.py:312
  12.5 1.8 %collective-permute-start.2 = (bf16[96,768]{1,0:T(8,128)(2,1)S(1)}, bf16[96,768]{1,0:T(8,128)(2,1)S(1)}, u32[]{:S(2)}, u32[]{:S(2)}) collective-permute-start(bf16[96,768]{1,0:T(8,128)(2,1)S(1)} %collective-permute-done), channel_id=1, source_target_pairs={{0,8},{4,12},{8,0},{12,4},{16,24},{20,28},{24,16},{28,20},{1,9},{5... | collective-permute-start | bytes 442376 | tf_op jit(solution)/shard_map/ppermute | solution.py:303
  14.3 1.4 %arrange.1 = (bf16[384,576]{1,0:T(8,128)(2,1)S(1)}, bf16[384,576]{1,0:T(8,128)(2,1)S(1)}, bf16[384,384]{1,0:T(8,128)(2,1)S(1)}, bf16[384,384]{1,0:T(8,128)(2,1)S...) custom-call(bf16[384,3072]{1,0:T(8,128)(2,1)S(1)} %layer_norm.1.normed_ref.refs_0_.refs_1_), custom_call_target="tpu_custom_call" | custom-call | flops 1207959552 | bytes 4718592 | tf_op jit(solution)/shard_map/arrange/pallas_call | solution.py:140
  16.0 1.7 %collective-permute-done.2 = bf16[96,768]{1,0:T(8,128)(2,1)S(1)} collective-permute-done((bf16[96,768]{1,0:T(8,128)(2,1)S(1)}, bf16[96,768]{1,0:T(8,128)(2,1)S(1)}, u32[]{:S(2)}, u32[]{:S(2)}) %collective-permute-start.2) | collective-permute-done | bytes 147488 | tf_op jit(solution)/shard_map/ppermute | solution.py:303
  17.7 1.6 %collective-permute-start.4 = (bf16[384,768]{1,0:T(8,128)(2,1)S(1)}, bf16[384,768]{1,0:T(8,128)(2,1)S(1)}, u32[]{:S(2)}, u32[]{:S(2)}) collective-permute-start(bf16[384,768]{1,0:T(8,128)(2,1)S(1)} %pad_maximum_fusion), channel_id=1, source_target_pairs={{0,2},{1,3},{2,0},{3,1},{4,5},{5,4},{6,7},{7,6},{8,10},{9,11},{10,... | collective-permute-start | bytes 1769480 | tf_op jit(solution)/shard_map/ppermute | solution.py:312
  19.3 3.7 %collective-permute-start.7 = (bf16[224,384]{1,0:T(8,128)(2,1)S(1)}, bf16[224,384]{1,0:T(8,128)(2,1)S(1)}, u32[]{:S(2)}, u32[]{:S(2)}) collective-permute-start(bf16[224,384]{1,0:T(8,128)(2,1)S(1)} %slice.12), channel_id=1, source_target_pairs={{0,24},{4,28},{8,16},{12,20},{16,8},{20,12},{24,0},{28,4},{1,25},{... | collective-permute-start | bytes 516104 | tf_op jit(solution)/shard_map/ppermute | solution.py:303
  24.4 3.5 %collective-permute-done.7 = bf16[224,384]{1,0:T(8,128)(2,1)S(1)} collective-permute-done((bf16[224,384]{1,0:T(8,128)(2,1)S(1)}, bf16[224,384]{1,0:T(8,128)(2,1)S(1)}, u32[]{:S(2)}, u32[]{:S(2)}) %collective-permute-start.7) | collective-permute-done | bytes 172064 | tf_op jit(solution)/shard_map/ppermute | solution.py:303
  28.2 1.3 %collective-permute-done.6 = bf16[96,768]{1,0:T(8,128)(2,1)S(1)} collective-permute-done((bf16[96,768]{1,0:T(8,128)(2,1)S(1)}, bf16[96,768]{1,0:T(8,128)(2,1)S(1)}, u32[]{:S(2)}, u32[]{:S(2)}) %collective-permute-start.6) | collective-permute-done | bytes 147488 | tf_op jit(solution)/shard_map/ppermute | solution.py:303
  30.2 1.0 %collective-permute-start.11 = (bf16[192,768]{1,0:T(8,128)(2,1)S(1)}, bf16[192,768]{1,0:T(8,128)(2,1)S(1)}, u32[]{:S(2)}, u32[]{:S(2)}) collective-permute-start(bf16[192,768]{1,0:T(8,128)(2,1)S(1)} %pad_maximum_fusion.2), channel_id=1, source_target_pairs={{0,1},{1,0},{2,3},{3,2},{4,6},{5,7},{6,4},{7,5},{8,9},{9,8},{10,11... | collective-permute-start | bytes 884744 | tf_op jit(solution)/shard_map/ppermute | solution.py:312
  31.4 2.1 %collective-permute-start.12 = (bf16[32,384]{1,0:T(8,128)(2,1)S(1)}, bf16[32,384]{1,0:T(8,128)(2,1)S(1)}, u32[]{:S(2)}, u32[]{:S(2)}) collective-permute-start(bf16[32,384]{1,0:T(8,128)(2,1)S(1)} %slice.15), channel_id=1, source_target_pairs={{0,24},{4,28},{8,16},{12,20},{16,8},{20,12},{24,0},{28,4},{1,25},{... | collective-permute-start | bytes 73736 | tf_op jit(solution)/shard_map/ppermute | solution.py:303
  33.5 1.7 %project_mid.1.refs_4_ = f32[384,768]{1,0:T(8,128)S(1)} custom-call(f32[2,128]{1,0:T(2,128)S(1)} %copy-done.4, bf16[384,576]{1,0:T(8,128)(2,1)S(1)} %get-tuple-element.51.refs_0_, bf16[384,576]{1,0:T(8,128)(2,1)S(1)} %get-tuple-element.52.refs_1_, bf16[384,384]{1,0:T(8,128)(2,1)S(1)} %get-tuple-element.53.refs_2_, ...), custom_call_target="tpu_custom_call" | custom-call | flops 1132462080 | bytes 4423680 | tf_op jit(solution)/shard_map/project_mid/pallas_call | solution.py:100
  35.2 1.8 %collective-permute-done.12 = bf16[32,384]{1,0:T(8,128)(2,1)S(1)} collective-permute-done((bf16[32,384]{1,0:T(8,128)(2,1)S(1)}, bf16[32,384]{1,0:T(8,128)(2,1)S(1)}, u32[]{:S(2)}, u32[]{:S(2)}) %collective-permute-start.12) | collective-permute-done | bytes 24608 | tf_op jit(solution)/shard_map/ppermute | solution.py:303
  37.0 0.9 %collective-permute-start.19 = (bf16[256,384]{1,0:T(8,128)(2,1)S(1)}, bf16[256,384]{1,0:T(8,128)(2,1)S(1)}, u32[]{:S(2)}, u32[]{:S(2)}) collective-permute-start(bf16[256,384]{1,0:T(8,128)(2,1)S(1)} %copy-done.2), channel_id=1, source_target_pairs={{0,8},{4,12},{8,0},{12,4},{16,24},{20,28},{24,16},{28,20},{1,9},{5... | collective-permute-start | bytes 589832 | tf_op jit(solution)/shard_map/ppermute | solution.py:303
  39.8 1.0 %collective-permute-start.15 = (bf16[256,512]{1,0:T(8,128)(2,1)S(1)}, bf16[256,512]{1,0:T(8,128)(2,1)S(1)}, u32[]{:S(2)}, u32[]{:S(2)}) collective-permute-start(bf16[256,512]{1,0:T(8,128)(2,1)S(1)} %get-tuple-element.80), channel_id=1, source_target_pairs={{0,1},{1,0},{2,3},{3,2},{4,5},{5,4},{6,7},{7,6},{8,9},{9,8},{10,11... | collective-permute-start | bytes 786440 | tf_op jit(solution)/shard_map/ppermute | solution.py:345
  40.8 1.0 %collective-permute-start.22 = (bf16[256,384]{1,0:T(8,128)(2,1)S(1)}, bf16[256,384]{1,0:T(8,128)(2,1)S(1)}, u32[]{:S(2)}, u32[]{:S(2)}) collective-permute-start(bf16[256,384]{1,0:T(8,128)(2,1)S(1)} %constant_dynamic-update-slice_fusion.5.refs_6_), channel_id=1, source_target_pairs={{0,8},{4,12},{8,0},{12,4},{16,24},{20,28},{24,16},{28,20},{1,9},{5... | collective-permute-start | bytes 589832 | tf_op jit(solution)/shard_map/ppermute | solution.py:303
  43.2 1.1 %collective-permute-done.19.refs_4_ = bf16[256,384]{1,0:T(8,128)(2,1)S(1)} collective-permute-done((bf16[256,384]{1,0:T(8,128)(2,1)S(1)}, bf16[256,384]{1,0:T(8,128)(2,1)S(1)}, u32[]{:S(2)}, u32[]{:S(2)}) %collective-permute-start.19) | collective-permute-done | bytes 196640 | tf_op jit(solution)/shard_map/ppermute | solution.py:303
  44.3 3.8 %collective-permute-start.20 = (bf16[256,384]{1,0:T(8,128)(2,1)S(1)}, bf16[256,384]{1,0:T(8,128)(2,1)S(1)}, u32[]{:S(2)}, u32[]{:S(2)}) collective-permute-start(bf16[256,384]{1,0:T(8,128)(2,1)S(1)} %collective-permute-done.19.refs_4_), channel_id=1, source_target_pairs={{0,4},{4,0},{8,12},{12,8},{16,20},{20,16},{24,28},{28,24},{1,5},{5... | collective-permute-start | bytes 589832 | tf_op jit(solution)/shard_map/ppermute | solution.py:303
  48.6 0.8 %collective-permute-start.23 = (bf16[256,384]{1,0:T(8,128)(2,1)S(1)}, bf16[256,384]{1,0:T(8,128)(2,1)S(1)}, u32[]{:S(2)}, u32[]{:S(2)}) collective-permute-start(bf16[256,384]{1,0:T(8,128)(2,1)S(1)} %collective-permute-done.22.refs_8_), channel_id=1, source_target_pairs={{0,4},{4,0},{8,12},{12,8},{16,20},{20,16},{24,28},{28,24},{1,5},{5... | collective-permute-start | bytes 589832 | tf_op jit(solution)/shard_map/ppermute | solution.py:303
  49.8 1.3 %attend_own_slab.1 = (f32[384,256]{1,0:T(8,128)S(1)}, f32[384,256]{1,0:T(8,128)S(1)}) custom-call(bf16[384,256]{1,0:T(8,128)(2,1)S(1)} %project_queries.1.queries_ref, bf16[384,512]{1,0:T(8,128)(2,1)S(1)} %project_keys_values.1.stacked_ref, bf16[256,512]{1,0:T(8,128)(2,1)S(1)} %collective-permute-done.15.near_ref), custom_call_target="tpu_custom_call" | custom-call | flops 150994944 | bytes 1376256 | tf_op jit(solution)/shard_map/attend_own_slab/pallas_call | solution.py:204
  51.2 1.9 %attend_and_mix.1 = bf16[1,384,3072]{2,1,0:T(8,128)(2,1)} custom-call(bf16[384,256]{1,0:T(8,128)(2,1)S(1)} %project_queries.1.queries_ref, f32[384,256]{1,0:T(8,128)S(1)} %get-tuple-element.69.weighted_ref, f32[384,256]{1,0:T(8,128)S(1)} %get-tuple-element.70.mass_ref, bf16[256,512]{1,0:T(8,128)(2,1)S(1)} %collective-permute-done.17.refs_0_, ...), custom_call_target="tpu_custom_call" | custom-call | flops 704643072 | bytes 3932160 | tf_op jit(solution)/shard_map/attend_and_mix/pallas_call | solution.py:280
  (58 shorter events, 7.7 us)
Async XLA Ops:
  1.0 9.8 %collective-permute-start = (bf16[96,768]{1,0:T(8,128)(2,1)S(1)}, bf16[96,768]{1,0:T(8,128)(2,1)S(1)}, u32[]{:S(2)}, u32[]{:S(2)}) collective-permute-start(bf16[96,768]{1,0:T(8,128)(2,1)S(1)} %get-tuple-element.78), channel_id=1, source_target_pairs={{0,24},{4,28},{8,16},{12,20},{16,8},{20,12},{24,0},{28,4},{1,25},{... | collective-permute-start | bytes 442376 | tf_op jit(solution)/shard_map/ppermute | solution.py:303
  6.1 9.7 %collective-permute-start.3 = (bf16[96,768]{1,0:T(8,128)(2,1)S(1)}, bf16[96,768]{1,0:T(8,128)(2,1)S(1)}, u32[]{:S(2)}, u32[]{:S(2)}) collective-permute-start(bf16[96,768]{1,0:T(8,128)(2,1)S(1)} %get-tuple-element.78), channel_id=1, source_target_pairs={{0,8},{4,12},{8,0},{12,4},{16,24},{20,28},{24,16},{28,20},{1,9},{5... | collective-permute-start | bytes 442376 | tf_op jit(solution)/shard_map/ppermute | solution.py:303
  10.8 5.1 %collective-permute-start.1 = (bf16[96,768]{1,0:T(8,128)(2,1)S(1)}, bf16[96,768]{1,0:T(8,128)(2,1)S(1)}, u32[]{:S(2)}, u32[]{:S(2)}) collective-permute-start(bf16[96,768]{1,0:T(8,128)(2,1)S(1)} %collective-permute-done), channel_id=1, source_target_pairs={{0,1},{1,0},{2,3},{3,2},{4,6},{5,7},{6,4},{7,5},{8,9},{9,8},{10,11... | collective-permute-start | bytes 442376 | tf_op jit(solution)/shard_map/ppermute | solution.py:312
  12.5 5.1 %collective-permute-start.2 = (bf16[96,768]{1,0:T(8,128)(2,1)S(1)}, bf16[96,768]{1,0:T(8,128)(2,1)S(1)}, u32[]{:S(2)}, u32[]{:S(2)}) collective-permute-start(bf16[96,768]{1,0:T(8,128)(2,1)S(1)} %collective-permute-done), channel_id=1, source_target_pairs={{0,8},{4,12},{8,0},{12,4},{16,24},{20,28},{24,16},{28,20},{1,9},{5... | collective-permute-start | bytes 442376 | tf_op jit(solution)/shard_map/ppermute | solution.py:303
  14.3 9.2 %collective-permute-start.8 = (bf16[384,768]{1,0:T(8,128)(2,1)S(1)}, bf16[384,768]{1,0:T(8,128)(2,1)S(1)}, u32[]{:S(2)}, u32[]{:S(2)}) collective-permute-start(bf16[384,768]{1,0:T(8,128)(2,1)S(1)} %copy-done.1), channel_id=1, source_target_pairs={{0,4},{4,0},{8,12},{12,8},{16,20},{20,16},{24,28},{28,24},{1,5},{5... | collective-permute-start | bytes 1769480 | tf_op jit(solution)/shard_map/ppermute | solution.py:303
  17.7 11.7 %collective-permute-start.4 = (bf16[384,768]{1,0:T(8,128)(2,1)S(1)}, bf16[384,768]{1,0:T(8,128)(2,1)S(1)}, u32[]{:S(2)}, u32[]{:S(2)}) collective-permute-start(bf16[384,768]{1,0:T(8,128)(2,1)S(1)} %pad_maximum_fusion), channel_id=1, source_target_pairs={{0,2},{1,3},{2,0},{3,1},{4,5},{5,4},{6,7},{7,6},{8,10},{9,11},{10,... | collective-permute-start | bytes 1769480 | tf_op jit(solution)/shard_map/ppermute | solution.py:312
  19.3 8.5 %collective-permute-start.7 = (bf16[224,384]{1,0:T(8,128)(2,1)S(1)}, bf16[224,384]{1,0:T(8,128)(2,1)S(1)}, u32[]{:S(2)}, u32[]{:S(2)}) collective-permute-start(bf16[224,384]{1,0:T(8,128)(2,1)S(1)} %slice.12), channel_id=1, source_target_pairs={{0,24},{4,28},{8,16},{12,20},{16,8},{20,12},{24,0},{28,4},{1,25},{... | collective-permute-start | bytes 516104 | tf_op jit(solution)/shard_map/ppermute | solution.py:303
  23.0 5.1 %collective-permute-start.5 = (bf16[96,768]{1,0:T(8,128)(2,1)S(1)}, bf16[96,768]{1,0:T(8,128)(2,1)S(1)}, u32[]{:S(2)}, u32[]{:S(2)}) collective-permute-start(bf16[96,768]{1,0:T(8,128)(2,1)S(1)} %collective-permute-done.3), channel_id=1, source_target_pairs={{0,1},{1,0},{2,3},{3,2},{4,6},{5,7},{6,4},{7,5},{8,9},{9,8},{10,11... | collective-permute-start | bytes 442376 | tf_op jit(solution)/shard_map/ppermute | solution.py:312
  23.5 5.9 %collective-permute-start.6 = (bf16[96,768]{1,0:T(8,128)(2,1)S(1)}, bf16[96,768]{1,0:T(8,128)(2,1)S(1)}, u32[]{:S(2)}, u32[]{:S(2)}) collective-permute-start(bf16[96,768]{1,0:T(8,128)(2,1)S(1)} %get-tuple-element.59), channel_id=1, source_target_pairs={{0,8},{4,12},{8,0},{12,4},{16,24},{20,28},{24,16},{28,20},{1,9},{5... | collective-permute-start | bytes 442376 | tf_op jit(solution)/shard_map/ppermute | solution.py:303
  29.5 3.9 %collective-permute-start.9 = (bf16[576,768]{1,0:T(8,128)(2,1)S(1)}, bf16[576,768]{1,0:T(8,128)(2,1)S(1)}, u32[]{:S(2)}, u32[]{:S(2)}) collective-permute-start(bf16[576,768]{1,0:T(8,128)(2,1)S(1)} %constant_dynamic-update-slice_fusion.refs_4_), channel_id=1, source_target_pairs={{0,4},{4,0},{8,12},{12,8},{16,20},{20,16},{24,28},{28,24},{1,5},{5... | collective-permute-start | bytes 2654216 | tf_op jit(solution)/shard_map/ppermute | solution.py:303
  29.6 3.8 %collective-permute-start.10 = (bf16[384,768]{1,0:T(8,128)(2,1)S(1)}, bf16[384,768]{1,0:T(8,128)(2,1)S(1)}, u32[]{:S(2)}, u32[]{:S(2)}) collective-permute-start(bf16[384,768]{1,0:T(8,128)(2,1)S(1)} %collective-permute-done.4.refs_6_), channel_id=1, source_target_pairs={{0,4},{4,0},{8,12},{12,8},{16,20},{20,16},{24,28},{28,24},{1,5},{5... | collective-permute-start | bytes 1769480 | tf_op jit(solution)/shard_map/ppermute | solution.py:303
  30.2 6.8 %collective-permute-start.11 = (bf16[192,768]{1,0:T(8,128)(2,1)S(1)}, bf16[192,768]{1,0:T(8,128)(2,1)S(1)}, u32[]{:S(2)}, u32[]{:S(2)}) collective-permute-start(bf16[192,768]{1,0:T(8,128)(2,1)S(1)} %pad_maximum_fusion.2), channel_id=1, source_target_pairs={{0,1},{1,0},{2,3},{3,2},{4,6},{5,7},{6,4},{7,5},{8,9},{9,8},{10,11... | collective-permute-start | bytes 884744 | tf_op jit(solution)/shard_map/ppermute | solution.py:312
  31.2 5.8 %collective-permute-start.13 = (bf16[256,384]{1,0:T(8,128)(2,1)S(1)}, bf16[256,384]{1,0:T(8,128)(2,1)S(1)}, u32[]{:S(2)}, u32[]{:S(2)}) collective-permute-start(bf16[256,384]{1,0:T(8,128)(2,1)S(1)} %copy-done.2), channel_id=1, source_target_pairs={{0,4},{4,0},{8,12},{12,8},{16,20},{20,16},{24,28},{28,24},{1,5},{5... | collective-permute-start | bytes 589832 | tf_op jit(solution)/shard_map/ppermute | solution.py:303
  31.4 5.6 %collective-permute-start.12 = (bf16[32,384]{1,0:T(8,128)(2,1)S(1)}, bf16[32,384]{1,0:T(8,128)(2,1)S(1)}, u32[]{:S(2)}, u32[]{:S(2)}) collective-permute-start(bf16[32,384]{1,0:T(8,128)(2,1)S(1)} %slice.15), channel_id=1, source_target_pairs={{0,24},{4,28},{8,16},{12,20},{16,8},{20,12},{24,0},{28,4},{1,25},{... | collective-permute-start | bytes 73736 | tf_op jit(solution)/shard_map/ppermute | solution.py:303
  37.0 1.6 %collective-permute-start.14 = (bf16[192,768]{1,0:T(8,128)(2,1)S(1)}, bf16[192,768]{1,0:T(8,128)(2,1)S(1)}, u32[]{:S(2)}, u32[]{:S(2)}) collective-permute-start(bf16[192,768]{1,0:T(8,128)(2,1)S(1)} %collective-permute-done.11.refs_2_), channel_id=1, source_target_pairs={{0,4},{4,0},{8,12},{12,8},{16,20},{20,16},{24,28},{28,24},{1,5},{5... | collective-permute-start | bytes 884744 | tf_op jit(solution)/shard_map/ppermute | solution.py:303
  37.0 7.3 %collective-permute-start.19 = (bf16[256,384]{1,0:T(8,128)(2,1)S(1)}, bf16[256,384]{1,0:T(8,128)(2,1)S(1)}, u32[]{:S(2)}, u32[]{:S(2)}) collective-permute-start(bf16[256,384]{1,0:T(8,128)(2,1)S(1)} %copy-done.2), channel_id=1, source_target_pairs={{0,8},{4,12},{8,0},{12,4},{16,24},{20,28},{24,16},{28,20},{1,9},{5... | collective-permute-start | bytes 589832 | tf_op jit(solution)/shard_map/ppermute | solution.py:303
  39.1 3.4 %collective-permute-start.16 = (bf16[256,512]{1,0:T(8,128)(2,1)S(1)}, bf16[256,512]{1,0:T(8,128)(2,1)S(1)}, u32[]{:S(2)}, u32[]{:S(2)}) collective-permute-start(bf16[256,512]{1,0:T(8,128)(2,1)S(1)} %get-tuple-element.79), channel_id=1, source_target_pairs={{5,7},{6,4},{13,15},{14,12},{21,23},{22,20},{29,31},{30,28}} | collective-permute-start | bytes 786440 | tf_op jit(solution)/shard_map/ppermute | solution.py:337
  39.8 8.8 %collective-permute-start.15 = (bf16[256,512]{1,0:T(8,128)(2,1)S(1)}, bf16[256,512]{1,0:T(8,128)(2,1)S(1)}, u32[]{:S(2)}, u32[]{:S(2)}) collective-permute-start(bf16[256,512]{1,0:T(8,128)(2,1)S(1)} %get-tuple-element.80), channel_id=1, source_target_pairs={{0,1},{1,0},{2,3},{3,2},{4,5},{5,4},{6,7},{7,6},{8,9},{9,8},{10,11... | collective-permute-start | bytes 786440 | tf_op jit(solution)/shard_map/ppermute | solution.py:345
  40.8 7.3 %collective-permute-start.22 = (bf16[256,384]{1,0:T(8,128)(2,1)S(1)}, bf16[256,384]{1,0:T(8,128)(2,1)S(1)}, u32[]{:S(2)}, u32[]{:S(2)}) collective-permute-start(bf16[256,384]{1,0:T(8,128)(2,1)S(1)} %constant_dynamic-update-slice_fusion.5.refs_6_), channel_id=1, source_target_pairs={{0,8},{4,12},{8,0},{12,4},{16,24},{20,28},{24,16},{28,20},{1,9},{5... | collective-permute-start | bytes 589832 | tf_op jit(solution)/shard_map/ppermute | solution.py:303
  41.8 9.3 %collective-permute-start.18 = (bf16[256,512]{1,0:T(8,128)(2,1)S(1)}, bf16[256,512]{1,0:T(8,128)(2,1)S(1)}, u32[]{:S(2)}, u32[]{:S(2)}) collective-permute-start(bf16[256,512]{1,0:T(8,128)(2,1)S(1)} %get-tuple-element.79), channel_id=1, source_target_pairs={{1,2},{2,1},{9,10},{10,9},{17,18},{18,17},{25,26},{26,25}} | collective-permute-start | bytes 786440 | tf_op jit(solution)/shard_map/ppermute | solution.py:338
  42.5 8.6 %collective-permute-start.17 = (bf16[256,512]{1,0:T(8,128)(2,1)S(1)}, bf16[256,512]{1,0:T(8,128)(2,1)S(1)}, u32[]{:S(2)}, u32[]{:S(2)}) collective-permute-start(bf16[256,512]{1,0:T(8,128)(2,1)S(1)} %collective-permute-done.16), channel_id=1, source_target_pairs={{7,6},{4,5},{15,14},{12,13},{23,22},{20,21},{31,30},{28,29}} | collective-permute-start | bytes 786440 | tf_op jit(solution)/shard_map/ppermute | solution.py:338
  44.3 6.8 %collective-permute-start.20 = (bf16[256,384]{1,0:T(8,128)(2,1)S(1)}, bf16[256,384]{1,0:T(8,128)(2,1)S(1)}, u32[]{:S(2)}, u32[]{:S(2)}) collective-permute-start(bf16[256,384]{1,0:T(8,128)(2,1)S(1)} %collective-permute-done.19.refs_4_), channel_id=1, source_target_pairs={{0,4},{4,0},{8,12},{12,8},{16,20},{20,16},{24,28},{28,24},{1,5},{5... | collective-permute-start | bytes 589832 | tf_op jit(solution)/shard_map/ppermute | solution.py:303
  48.1 3.0 %collective-permute-start.21 = (bf16[256,384]{1,0:T(8,128)(2,1)S(1)}, bf16[256,384]{1,0:T(8,128)(2,1)S(1)}, u32[]{:S(2)}, u32[]{:S(2)}) collective-permute-start(bf16[256,384]{1,0:T(8,128)(2,1)S(1)} %constant_dynamic-update-slice_fusion.5.refs_6_), channel_id=1, source_target_pairs={{0,4},{4,0},{8,12},{12,8},{16,20},{20,16},{24,28},{28,24},{1,5},{5... | collective-permute-start | bytes 589832 | tf_op jit(solution)/shard_map/ppermute | solution.py:303
  48.6 2.5 %collective-permute-start.23 = (bf16[256,384]{1,0:T(8,128)(2,1)S(1)}, bf16[256,384]{1,0:T(8,128)(2,1)S(1)}, u32[]{:S(2)}, u32[]{:S(2)}) collective-permute-start(bf16[256,384]{1,0:T(8,128)(2,1)S(1)} %collective-permute-done.22.refs_8_), channel_id=1, source_target_pairs={{0,4},{4,0},{8,12},{12,8},{16,20},{20,16},{24,28},{28,24},{1,5},{5... | collective-permute-start | bytes 589832 | tf_op jit(solution)/shard_map/ppermute | solution.py:303
  (5 other events, 19.6 us)

commit v9 on v8

--- a/solution.py
+++ b/solution.py
@@ -408,7 +408,7 @@
     two = swap_plane(jnp.concatenate([one, one_rest, late], axis=0), 1)
     near_rest = swap_plane(near, 0)
     across = swap(next_part, "fsdp", 2)
-    cut = 7 * WIDTH // 8
+    cut = 15 * WIDTH // 16
     wides = [swap(w_out[:cut], "fsdp", 2 * k) for k in front]
     total = project(
         [(normed, w_qkv), (normed, other_qkv)], qk_gain, (0, columns), "project_own", own_places

time: 53.4 us -> 53.4 us (level)
  starting transfers between devices: 28.3 us -> 27.3 us
  waiting for transfers between devices: 10.7 us -> 11.7 us
    ppermute x16, waiting for transfers between devices: 10.2 us -> 11 us  [swap(): lax.ppermute(x, axis, [(i, i ^ bits) for i in range(lax.axis_size(axis))])]
    ppermute x16, starting transfers between devices: 20.5 us -> 19.9 us  [swap(): lax.ppermute(x, axis, [(i, i ^ bits) for i in range(lax.axis_size(axis))])]
  transfers between devices with their start and end apart: 24 -> 24, of which waited for: 9 -> 10; matrix products, arithmetic and copies ran while one was open for 0% -> 0% of each run, Pallas kernels for 15% -> 15%
where the time goes in v9:
time: 53.4 us; the launch traced here: 53 us
  starting transfers between devices  27.3 us (51%)
  waiting for transfers between devices  11.7 us (22%)
  Pallas kernels  9.98 us (19%)
  local copies, waits for them, and re-layouts  3.6 us (7%)
    ppermute x16, starting transfers between devices, swap(): lax.ppermute(x, axis, [(i, i ^ bits) for i in range(lax.axis_size(axis))])  19.9 us
    ppermute x16, waiting for transfers between devices, swap(): lax.ppermute(x, axis, [(i, i ^ bits) for i in range(lax.axis_size(axis))])  11 us
    ppermute x4, starting transfers between devices, swap_plane(): return lax.ppermute(x, ('fsdp', 'frame'), pairs)  4.57 us
    pallas_call x4, Pallas kernels, project(): pl.pallas_call(functools.partial(project_kernel, len(pairs), starts, kind...  3.25 us
    unnamed x15, local copies, waits for them, and re-layouts  2.5 us
    pallas_call x1, Pallas kernels, norm_rows(): pl.pallas_call(norm_kernel, grid=(rows // block,), in_specs=[pl.BlockSpec...  2.15 us
    pallas_call x1, Pallas kernels, attend(): pl.pallas_call(functools.partial(attend_kernel, layout, len(sources), len...  1.86 us
    pallas_call x1, Pallas kernels, arrange(): pl.pallas_call(functools.partial(arrange_kernel, starts, order, homes), i...  1.42 us
  transfers between devices with their start and end apart: 24, of which 10 were waited for; matrix products, arithmetic and copies ran while one was open for 0% of the time, Pallas kernels for 15%

profile of v9, /device:TPU:0, one launch (start us, length us, event | category | flops | bytes accessed | tf_op | source)
XLA Modules:
  0.0 53.0 jit_solution(4001479304495363457)
XLA Ops:
  0.0 1.0 %constant_dynamic-slice_fusion.2 = (bf16[96,768]{1,0:T(8,128)(2,1)S(1)}, bf16[96,768]{1,0:T(8,128)(2,1)S(1)}) fusion(bf16[384,768]{1,0:T(8,128)(2,1)} %refs_2_.2, s32[]{:T(128)S(6)} %select_n.13, s32[]{:T(128)S(6)} %select_n.12), kind=kLoop, calls=%fused_computation.12 | loop fusion | bytes 589832 | tf_op jit(solution)/shard_map/dynamic_slice | solution.py:402
  1.0 5.1 %collective-permute-start = (bf16[96,768]{1,0:T(8,128)(2,1)S(1)}, bf16[96,768]{1,0:T(8,128)(2,1)S(1)}, u32[]{:S(2)}, u32[]{:S(2)}) collective-permute-start(bf16[96,768]{1,0:T(8,128)(2,1)S(1)} %get-tuple-element.78), channel_id=1, source_target_pairs={{0,24},{4,28},{8,16},{12,20},{16,8},{20,12},{24,0},{28,4},{1,25},{... | collective-permute-start | bytes 442376 | tf_op jit(solution)/shard_map/ppermute | solution.py:303
  6.1 1.7 %copy-done = bf16[1,384,3072]{2,1,0:T(8,128)(2,1)S(1)} copy-done((bf16[1,384,3072]{2,1,0:T(8,128)(2,1)S(1)}, bf16[1,384,3072]{2,1,0:T(8,128)(2,1)}, u32[]{:S(2)}) %copy-start) | copy-done | bytes 2359320
  8.5 2.2 %layer_norm.1.normed_ref.refs_0_.refs_1_ = bf16[384,3072]{1,0:T(8,128)(2,1)S(1)} custom-call(bf16[384,3072]{1,0:T(8,128)(2,1)S(1)} %bitcast.2, f32[2,3072]{1,0:T(2,128)S(1)} %bitcast.3), custom_call_target="tpu_custom_call" | custom-call | flops 11796480 | bytes 4718592 | tf_op jit(solution)/shard_map/layer_norm/pallas_call | solution.py:49
  10.8 1.7 %collective-permute-start.1 = (bf16[96,768]{1,0:T(8,128)(2,1)S(1)}, bf16[96,768]{1,0:T(8,128)(2,1)S(1)}, u32[]{:S(2)}, u32[]{:S(2)}) collective-permute-start(bf16[96,768]{1,0:T(8,128)(2,1)S(1)} %collective-permute-done), channel_id=1, source_target_pairs={{0,1},{1,0},{2,3},{3,2},{4,6},{5,7},{6,4},{7,5},{8,9},{9,8},{10,11... | collective-permute-start | bytes 442376 | tf_op jit(solution)/shard_map/ppermute | solution.py:312
  12.5 1.8 %collective-permute-start.2 = (bf16[96,768]{1,0:T(8,128)(2,1)S(1)}, bf16[96,768]{1,0:T(8,128)(2,1)S(1)}, u32[]{:S(2)}, u32[]{:S(2)}) collective-permute-start(bf16[96,768]{1,0:T(8,128)(2,1)S(1)} %collective-permute-done), channel_id=1, source_target_pairs={{0,8},{4,12},{8,0},{12,4},{16,24},{20,28},{24,16},{28,20},{1,9},{5... | collective-permute-start | bytes 442376 | tf_op jit(solution)/shard_map/ppermute | solution.py:303
  14.3 1.4 %arrange.1 = (bf16[384,576]{1,0:T(8,128)(2,1)S(1)}, bf16[384,576]{1,0:T(8,128)(2,1)S(1)}, bf16[384,384]{1,0:T(8,128)(2,1)S(1)}, bf16[384,384]{1,0:T(8,128)(2,1)S...) custom-call(bf16[384,3072]{1,0:T(8,128)(2,1)S(1)} %layer_norm.1.normed_ref.refs_0_.refs_1_), custom_call_target="tpu_custom_call" | custom-call | flops 1207959552 | bytes 4718592 | tf_op jit(solution)/shard_map/arrange/pallas_call | solution.py:140
  16.0 1.7 %collective-permute-done.2 = bf16[96,768]{1,0:T(8,128)(2,1)S(1)} collective-permute-done((bf16[96,768]{1,0:T(8,128)(2,1)S(1)}, bf16[96,768]{1,0:T(8,128)(2,1)S(1)}, u32[]{:S(2)}, u32[]{:S(2)}) %collective-permute-start.2) | collective-permute-done | bytes 147488 | tf_op jit(solution)/shard_map/ppermute | solution.py:303
  17.7 1.6 %collective-permute-start.4 = (bf16[384,768]{1,0:T(8,128)(2,1)S(1)}, bf16[384,768]{1,0:T(8,128)(2,1)S(1)}, u32[]{:S(2)}, u32[]{:S(2)}) collective-permute-start(bf16[384,768]{1,0:T(8,128)(2,1)S(1)} %pad_maximum_fusion), channel_id=1, source_target_pairs={{0,2},{1,3},{2,0},{3,1},{4,5},{5,4},{6,7},{7,6},{8,10},{9,11},{10,... | collective-permute-start | bytes 1769480 | tf_op jit(solution)/shard_map/ppermute | solution.py:312
  19.3 3.7 %collective-permute-start.7 = (bf16[240,384]{1,0:T(8,128)(2,1)S(1)}, bf16[240,384]{1,0:T(8,128)(2,1)S(1)}, u32[]{:S(2)}, u32[]{:S(2)}) collective-permute-start(bf16[240,384]{1,0:T(8,128)(2,1)S(1)} %slice.12), channel_id=1, source_target_pairs={{0,24},{4,28},{8,16},{12,20},{16,8},{20,12},{24,0},{28,4},{1,25},{... | collective-permute-start | bytes 552968 | tf_op jit(solution)/shard_map/ppermute | solution.py:303
  23.6 0.8 %project_own.1.refs_8_ = f32[384,768]{1,0:T(8,128)S(1)} custom-call(f32[2,128]{1,0:T(2,128)S(1)} %copy-done.4, bf16[384,3072]{1,0:T(8,128)(2,1)S(1)} %layer_norm.1.normed_ref.refs_0_.refs_1_, bf16[384,3072]{1,0:T(8,128)(2,1)S(1)} %layer_norm.1.normed_ref.refs_0_.refs_1_, bf16[384,768]{1,0:T(8,128)(2,1)S(1)} %copy-done.1, ...), custom_call_target="tpu_custom_call" | custom-call | flops 452984832 | bytes 1769472 | tf_op jit(solution)/shard_map/project_own/pallas_call | solution.py:100
  24.4 3.8 %collective-permute-done.7 = bf16[240,384]{1,0:T(8,128)(2,1)S(1)} collective-permute-done((bf16[240,384]{1,0:T(8,128)(2,1)S(1)}, bf16[240,384]{1,0:T(8,128)(2,1)S(1)}, u32[]{:S(2)}, u32[]{:S(2)}) %collective-permute-start.7) | collective-permute-done | bytes 184352 | tf_op jit(solution)/shard_map/ppermute | solution.py:303
  28.2 1.5 %collective-permute-done.6 = bf16[96,768]{1,0:T(8,128)(2,1)S(1)} collective-permute-done((bf16[96,768]{1,0:T(8,128)(2,1)S(1)}, bf16[96,768]{1,0:T(8,128)(2,1)S(1)}, u32[]{:S(2)}, u32[]{:S(2)}) %collective-permute-start.6) | collective-permute-done | bytes 147488 | tf_op jit(solution)/shard_map/ppermute | solution.py:303
  30.4 0.8 %collective-permute-start.11 = (bf16[192,768]{1,0:T(8,128)(2,1)S(1)}, bf16[192,768]{1,0:T(8,128)(2,1)S(1)}, u32[]{:S(2)}, u32[]{:S(2)}) collective-permute-start(bf16[192,768]{1,0:T(8,128)(2,1)S(1)} %pad_maximum_fusion.2), channel_id=1, source_target_pairs={{0,1},{1,0},{2,3},{3,2},{4,6},{5,7},{6,4},{7,5},{8,9},{9,8},{10,11... | collective-permute-start | bytes 884744 | tf_op jit(solution)/shard_map/ppermute | solution.py:312
  31.4 2.1 %collective-permute-start.12 = (bf16[16,384]{1,0:T(8,128)(2,1)S(1)}, bf16[16,384]{1,0:T(8,128)(2,1)S(1)}, u32[]{:S(2)}, u32[]{:S(2)}) collective-permute-start(bf16[16,384]{1,0:T(8,128)(2,1)S(1)} %slice.15), channel_id=1, source_target_pairs={{0,24},{4,28},{8,16},{12,20},{16,8},{20,12},{24,0},{28,4},{1,25},{... | collective-permute-start | bytes 36872 | tf_op jit(solution)/shard_map/ppermute | solution.py:303
  33.5 1.7 %project_mid.1.refs_4_ = f32[384,768]{1,0:T(8,128)S(1)} custom-call(f32[2,128]{1,0:T(2,128)S(1)} %copy-done.4, bf16[384,576]{1,0:T(8,128)(2,1)S(1)} %get-tuple-element.51.refs_0_, bf16[384,576]{1,0:T(8,128)(2,1)S(1)} %get-tuple-element.52.refs_1_, bf16[384,384]{1,0:T(8,128)(2,1)S(1)} %get-tuple-element.53.refs_2_, ...), custom_call_target="tpu_custom_call" | custom-call | flops 1132462080 | bytes 4423680 | tf_op jit(solution)/shard_map/project_mid/pallas_call | solution.py:100
  35.2 1.7 %collective-permute-done.12 = bf16[16,384]{1,0:T(8,128)(2,1)S(1)} collective-permute-done((bf16[16,384]{1,0:T(8,128)(2,1)S(1)}, bf16[16,384]{1,0:T(8,128)(2,1)S(1)}, u32[]{:S(2)}, u32[]{:S(2)}) %collective-permute-start.12) | collective-permute-done | bytes 12320 | tf_op jit(solution)/shard_map/ppermute | solution.py:303
  38.0 0.8 %collective-permute-done.14.refs_3_ = bf16[192,768]{1,0:T(8,128)(2,1)S(1)} collective-permute-done((bf16[192,768]{1,0:T(8,128)(2,1)S(1)}, bf16[192,768]{1,0:T(8,128)(2,1)S(1)}, u32[]{:S(2)}, u32[]{:S(2)}) %collective-permute-start.14) | collective-permute-done | bytes 294944 | tf_op jit(solution)/shard_map/ppermute | solution.py:303
  40.0 0.9 %collective-permute-start.15 = (bf16[256,512]{1,0:T(8,128)(2,1)S(1)}, bf16[256,512]{1,0:T(8,128)(2,1)S(1)}, u32[]{:S(2)}, u32[]{:S(2)}) collective-permute-start(bf16[256,512]{1,0:T(8,128)(2,1)S(1)} %get-tuple-element.80), channel_id=1, source_target_pairs={{0,1},{1,0},{2,3},{3,2},{4,5},{5,4},{6,7},{7,6},{8,9},{9,8},{10,11... | collective-permute-start | bytes 786440 | tf_op jit(solution)/shard_map/ppermute | solution.py:345
  40.9 0.9 %collective-permute-start.22 = (bf16[256,384]{1,0:T(8,128)(2,1)S(1)}, bf16[256,384]{1,0:T(8,128)(2,1)S(1)}, u32[]{:S(2)}, u32[]{:S(2)}) collective-permute-start(bf16[256,384]{1,0:T(8,128)(2,1)S(1)} %constant_dynamic-update-slice_fusion.5.refs_6_), channel_id=1, source_target_pairs={{0,8},{4,12},{8,0},{12,4},{16,24},{20,28},{24,16},{28,20},{1,9},{5... | collective-permute-start | bytes 589832 | tf_op jit(solution)/shard_map/ppermute | solution.py:303
  43.2 1.3 %collective-permute-done.19.refs_4_ = bf16[256,384]{1,0:T(8,128)(2,1)S(1)} collective-permute-done((bf16[256,384]{1,0:T(8,128)(2,1)S(1)}, bf16[256,384]{1,0:T(8,128)(2,1)S(1)}, u32[]{:S(2)}, u32[]{:S(2)}) %collective-permute-start.19) | collective-permute-done | bytes 196640 | tf_op jit(solution)/shard_map/ppermute | solution.py:303
  44.5 3.7 %collective-permute-start.20 = (bf16[256,384]{1,0:T(8,128)(2,1)S(1)}, bf16[256,384]{1,0:T(8,128)(2,1)S(1)}, u32[]{:S(2)}, u32[]{:S(2)}) collective-permute-start(bf16[256,384]{1,0:T(8,128)(2,1)S(1)} %collective-permute-done.19.refs_4_), channel_id=1, source_target_pairs={{0,4},{4,0},{8,12},{12,8},{16,20},{20,16},{24,28},{28,24},{1,5},{5... | collective-permute-start | bytes 589832 | tf_op jit(solution)/shard_map/ppermute | solution.py:303
  49.7 1.3 %attend_own_slab.1 = (f32[384,256]{1,0:T(8,128)S(1)}, f32[384,256]{1,0:T(8,128)S(1)}) custom-call(bf16[384,256]{1,0:T(8,128)(2,1)S(1)} %project_queries.1.queries_ref, bf16[384,512]{1,0:T(8,128)(2,1)S(1)} %project_keys_values.1.stacked_ref, bf16[256,512]{1,0:T(8,128)(2,1)S(1)} %collective-permute-done.15.near_ref), custom_call_target="tpu_custom_call" | custom-call | flops 150994944 | bytes 1376256 | tf_op jit(solution)/shard_map/attend_own_slab/pallas_call | solution.py:204
  51.1 1.9 %attend_and_mix.1 = bf16[1,384,3072]{2,1,0:T(8,128)(2,1)} custom-call(bf16[384,256]{1,0:T(8,128)(2,1)S(1)} %project_queries.1.queries_ref, f32[384,256]{1,0:T(8,128)S(1)} %get-tuple-element.69.weighted_ref, f32[384,256]{1,0:T(8,128)S(1)} %get-tuple-element.70.mass_ref, bf16[256,512]{1,0:T(8,128)(2,1)S(1)} %collective-permute-done.17.refs_0_, ...), custom_call_target="tpu_custom_call" | custom-call | flops 704643072 | bytes 3932160 | tf_op jit(solution)/shard_map/attend_and_mix/pallas_call | solution.py:280
  (58 shorter events, 7.8 us)
Async XLA Ops:
  1.0 9.8 %collective-permute-start = (bf16[96,768]{1,0:T(8,128)(2,1)S(1)}, bf16[96,768]{1,0:T(8,128)(2,1)S(1)}, u32[]{:S(2)}, u32[]{:S(2)}) collective-permute-start(bf16[96,768]{1,0:T(8,128)(2,1)S(1)} %get-tuple-element.78), channel_id=1, source_target_pairs={{0,24},{4,28},{8,16},{12,20},{16,8},{20,12},{24,0},{28,4},{1,25},{... | collective-permute-start | bytes 442376 | tf_op jit(solution)/shard_map/ppermute | solution.py:303
  6.1 9.7 %collective-permute-start.3 = (bf16[96,768]{1,0:T(8,128)(2,1)S(1)}, bf16[96,768]{1,0:T(8,128)(2,1)S(1)}, u32[]{:S(2)}, u32[]{:S(2)}) collective-permute-start(bf16[96,768]{1,0:T(8,128)(2,1)S(1)} %get-tuple-element.78), channel_id=1, source_target_pairs={{0,8},{4,12},{8,0},{12,4},{16,24},{20,28},{24,16},{28,20},{1,9},{5... | collective-permute-start | bytes 442376 | tf_op jit(solution)/shard_map/ppermute | solution.py:303
  10.8 5.1 %collective-permute-start.1 = (bf16[96,768]{1,0:T(8,128)(2,1)S(1)}, bf16[96,768]{1,0:T(8,128)(2,1)S(1)}, u32[]{:S(2)}, u32[]{:S(2)}) collective-permute-start(bf16[96,768]{1,0:T(8,128)(2,1)S(1)} %collective-permute-done), channel_id=1, source_target_pairs={{0,1},{1,0},{2,3},{3,2},{4,6},{5,7},{6,4},{7,5},{8,9},{9,8},{10,11... | collective-permute-start | bytes 442376 | tf_op jit(solution)/shard_map/ppermute | solution.py:312
  12.5 5.1 %collective-permute-start.2 = (bf16[96,768]{1,0:T(8,128)(2,1)S(1)}, bf16[96,768]{1,0:T(8,128)(2,1)S(1)}, u32[]{:S(2)}, u32[]{:S(2)}) collective-permute-start(bf16[96,768]{1,0:T(8,128)(2,1)S(1)} %collective-permute-done), channel_id=1, source_target_pairs={{0,8},{4,12},{8,0},{12,4},{16,24},{20,28},{24,16},{28,20},{1,9},{5... | collective-permute-start | bytes 442376 | tf_op jit(solution)/shard_map/ppermute | solution.py:303
  14.3 9.2 %collective-permute-start.8 = (bf16[384,768]{1,0:T(8,128)(2,1)S(1)}, bf16[384,768]{1,0:T(8,128)(2,1)S(1)}, u32[]{:S(2)}, u32[]{:S(2)}) collective-permute-start(bf16[384,768]{1,0:T(8,128)(2,1)S(1)} %copy-done.1), channel_id=1, source_target_pairs={{0,4},{4,0},{8,12},{12,8},{16,20},{20,16},{24,28},{28,24},{1,5},{5... | collective-permute-start | bytes 1769480 | tf_op jit(solution)/shard_map/ppermute | solution.py:303
  17.7 12.0 %collective-permute-start.4 = (bf16[384,768]{1,0:T(8,128)(2,1)S(1)}, bf16[384,768]{1,0:T(8,128)(2,1)S(1)}, u32[]{:S(2)}, u32[]{:S(2)}) collective-permute-start(bf16[384,768]{1,0:T(8,128)(2,1)S(1)} %pad_maximum_fusion), channel_id=1, source_target_pairs={{0,2},{1,3},{2,0},{3,1},{4,5},{5,4},{6,7},{7,6},{8,10},{9,11},{10,... | collective-permute-start | bytes 1769480 | tf_op jit(solution)/shard_map/ppermute | solution.py:312
  19.3 8.8 %collective-permute-start.7 = (bf16[240,384]{1,0:T(8,128)(2,1)S(1)}, bf16[240,384]{1,0:T(8,128)(2,1)S(1)}, u32[]{:S(2)}, u32[]{:S(2)}) collective-permute-start(bf16[240,384]{1,0:T(8,128)(2,1)S(1)} %slice.12), channel_id=1, source_target_pairs={{0,24},{4,28},{8,16},{12,20},{16,8},{20,12},{24,0},{28,4},{1,25},{... | collective-permute-start | bytes 552968 | tf_op jit(solution)/shard_map/ppermute | solution.py:303
  23.0 5.1 %collective-permute-start.5 = (bf16[96,768]{1,0:T(8,128)(2,1)S(1)}, bf16[96,768]{1,0:T(8,128)(2,1)S(1)}, u32[]{:S(2)}, u32[]{:S(2)}) collective-permute-start(bf16[96,768]{1,0:T(8,128)(2,1)S(1)} %collective-permute-done.3), channel_id=1, source_target_pairs={{0,1},{1,0},{2,3},{3,2},{4,6},{5,7},{6,4},{7,5},{8,9},{9,8},{10,11... | collective-permute-start | bytes 442376 | tf_op jit(solution)/shard_map/ppermute | solution.py:312
  23.5 6.1 %collective-permute-start.6 = (bf16[96,768]{1,0:T(8,128)(2,1)S(1)}, bf16[96,768]{1,0:T(8,128)(2,1)S(1)}, u32[]{:S(2)}, u32[]{:S(2)}) collective-permute-start(bf16[96,768]{1,0:T(8,128)(2,1)S(1)} %get-tuple-element.59), channel_id=1, source_target_pairs={{0,8},{4,12},{8,0},{12,4},{16,24},{20,28},{24,16},{28,20},{1,9},{5... | collective-permute-start | bytes 442376 | tf_op jit(solution)/shard_map/ppermute | solution.py:303
  29.8 3.7 %collective-permute-start.9 = (bf16[576,768]{1,0:T(8,128)(2,1)S(1)}, bf16[576,768]{1,0:T(8,128)(2,1)S(1)}, u32[]{:S(2)}, u32[]{:S(2)}) collective-permute-start(bf16[576,768]{1,0:T(8,128)(2,1)S(1)} %constant_dynamic-update-slice_fusion.refs_4_), channel_id=1, source_target_pairs={{0,4},{4,0},{8,12},{12,8},{16,20},{20,16},{24,28},{28,24},{1,5},{5... | collective-permute-start | bytes 2654216 | tf_op jit(solution)/shard_map/ppermute | solution.py:303
  29.9 3.6 %collective-permute-start.10 = (bf16[384,768]{1,0:T(8,128)(2,1)S(1)}, bf16[384,768]{1,0:T(8,128)(2,1)S(1)}, u32[]{:S(2)}, u32[]{:S(2)}) collective-permute-start(bf16[384,768]{1,0:T(8,128)(2,1)S(1)} %collective-permute-done.4.refs_6_), channel_id=1, source_target_pairs={{0,4},{4,0},{8,12},{12,8},{16,20},{20,16},{24,28},{28,24},{1,5},{5... | collective-permute-start | bytes 1769480 | tf_op jit(solution)/shard_map/ppermute | solution.py:303
  30.4 6.8 %collective-permute-start.11 = (bf16[192,768]{1,0:T(8,128)(2,1)S(1)}, bf16[192,768]{1,0:T(8,128)(2,1)S(1)}, u32[]{:S(2)}, u32[]{:S(2)}) collective-permute-start(bf16[192,768]{1,0:T(8,128)(2,1)S(1)} %pad_maximum_fusion.2), channel_id=1, source_target_pairs={{0,1},{1,0},{2,3},{3,2},{4,6},{5,7},{6,4},{7,5},{8,9},{9,8},{10,11... | collective-permute-start | bytes 884744 | tf_op jit(solution)/shard_map/ppermute | solution.py:312
  31.2 5.7 %collective-permute-start.13 = (bf16[256,384]{1,0:T(8,128)(2,1)S(1)}, bf16[256,384]{1,0:T(8,128)(2,1)S(1)}, u32[]{:S(2)}, u32[]{:S(2)}) collective-permute-start(bf16[256,384]{1,0:T(8,128)(2,1)S(1)} %copy-done.2), channel_id=1, source_target_pairs={{0,4},{4,0},{8,12},{12,8},{16,20},{20,16},{24,28},{28,24},{1,5},{5... | collective-permute-start | bytes 589832 | tf_op jit(solution)/shard_map/ppermute | solution.py:303
  31.4 5.5 %collective-permute-start.12 = (bf16[16,384]{1,0:T(8,128)(2,1)S(1)}, bf16[16,384]{1,0:T(8,128)(2,1)S(1)}, u32[]{:S(2)}, u32[]{:S(2)}) collective-permute-start(bf16[16,384]{1,0:T(8,128)(2,1)S(1)} %slice.15), channel_id=1, source_target_pairs={{0,24},{4,28},{8,16},{12,20},{16,8},{20,12},{24,0},{28,4},{1,25},{... | collective-permute-start | bytes 36872 | tf_op jit(solution)/shard_map/ppermute | solution.py:303
  37.2 1.6 %collective-permute-start.14 = (bf16[192,768]{1,0:T(8,128)(2,1)S(1)}, bf16[192,768]{1,0:T(8,128)(2,1)S(1)}, u32[]{:S(2)}, u32[]{:S(2)}) collective-permute-start(bf16[192,768]{1,0:T(8,128)(2,1)S(1)} %collective-permute-done.11.refs_2_), channel_id=1, source_target_pairs={{0,4},{4,0},{8,12},{12,8},{16,20},{20,16},{24,28},{28,24},{1,5},{5... | collective-permute-start | bytes 884744 | tf_op jit(solution)/shard_map/ppermute | solution.py:303
  37.2 7.3 %collective-permute-start.19 = (bf16[256,384]{1,0:T(8,128)(2,1)S(1)}, bf16[256,384]{1,0:T(8,128)(2,1)S(1)}, u32[]{:S(2)}, u32[]{:S(2)}) collective-permute-start(bf16[256,384]{1,0:T(8,128)(2,1)S(1)} %copy-done.2), channel_id=1, source_target_pairs={{0,8},{4,12},{8,0},{12,4},{16,24},{20,28},{24,16},{28,20},{1,9},{5... | collective-permute-start | bytes 589832 | tf_op jit(solution)/shard_map/ppermute | solution.py:303
  39.3 3.2 %collective-permute-start.16 = (bf16[256,512]{1,0:T(8,128)(2,1)S(1)}, bf16[256,512]{1,0:T(8,128)(2,1)S(1)}, u32[]{:S(2)}, u32[]{:S(2)}) collective-permute-start(bf16[256,512]{1,0:T(8,128)(2,1)S(1)} %get-tuple-element.79), channel_id=1, source_target_pairs={{5,7},{6,4},{13,15},{14,12},{21,23},{22,20},{29,31},{30,28}} | collective-permute-start | bytes 786440 | tf_op jit(solution)/shard_map/ppermute | solution.py:337
  40.0 9.0 %collective-permute-start.15 = (bf16[256,512]{1,0:T(8,128)(2,1)S(1)}, bf16[256,512]{1,0:T(8,128)(2,1)S(1)}, u32[]{:S(2)}, u32[]{:S(2)}) collective-permute-start(bf16[256,512]{1,0:T(8,128)(2,1)S(1)} %get-tuple-element.80), channel_id=1, source_target_pairs={{0,1},{1,0},{2,3},{3,2},{4,5},{5,4},{6,7},{7,6},{8,9},{9,8},{10,11... | collective-permute-start | bytes 786440 | tf_op jit(solution)/shard_map/ppermute | solution.py:345
  40.9 7.3 %collective-permute-start.22 = (bf16[256,384]{1,0:T(8,128)(2,1)S(1)}, bf16[256,384]{1,0:T(8,128)(2,1)S(1)}, u32[]{:S(2)}, u32[]{:S(2)}) collective-permute-start(bf16[256,384]{1,0:T(8,128)(2,1)S(1)} %constant_dynamic-update-slice_fusion.5.refs_6_), channel_id=1, source_target_pairs={{0,8},{4,12},{8,0},{12,4},{16,24},{20,28},{24,16},{28,20},{1,9},{5... | collective-permute-start | bytes 589832 | tf_op jit(solution)/shard_map/ppermute | solution.py:303
  41.8 9.2 %collective-permute-start.18 = (bf16[256,512]{1,0:T(8,128)(2,1)S(1)}, bf16[256,512]{1,0:T(8,128)(2,1)S(1)}, u32[]{:S(2)}, u32[]{:S(2)}) collective-permute-start(bf16[256,512]{1,0:T(8,128)(2,1)S(1)} %get-tuple-element.79), channel_id=1, source_target_pairs={{1,2},{2,1},{9,10},{10,9},{17,18},{18,17},{25,26},{26,25}} | collective-permute-start | bytes 786440 | tf_op jit(solution)/shard_map/ppermute | solution.py:338
  42.5 8.6 %collective-permute-start.17 = (bf16[256,512]{1,0:T(8,128)(2,1)S(1)}, bf16[256,512]{1,0:T(8,128)(2,1)S(1)}, u32[]{:S(2)}, u32[]{:S(2)}) collective-permute-start(bf16[256,512]{1,0:T(8,128)(2,1)S(1)} %collective-permute-done.16), channel_id=1, source_target_pairs={{7,6},{4,5},{15,14},{12,13},{23,22},{20,21},{31,30},{28,29}} | collective-permute-start | bytes 786440 | tf_op jit(solution)/shard_map/ppermute | solution.py:338
  44.5 6.5 %collective-permute-start.20 = (bf16[256,384]{1,0:T(8,128)(2,1)S(1)}, bf16[256,384]{1,0:T(8,128)(2,1)S(1)}, u32[]{:S(2)}, u32[]{:S(2)}) collective-permute-start(bf16[256,384]{1,0:T(8,128)(2,1)S(1)} %collective-permute-done.19.refs_4_), channel_id=1, source_target_pairs={{0,4},{4,0},{8,12},{12,8},{16,20},{20,16},{24,28},{28,24},{1,5},{5... | collective-permute-start | bytes 589832 | tf_op jit(solution)/shard_map/ppermute | solution.py:303
  48.2 2.8 %collective-permute-start.21 = (bf16[256,384]{1,0:T(8,128)(2,1)S(1)}, bf16[256,384]{1,0:T(8,128)(2,1)S(1)}, u32[]{:S(2)}, u32[]{:S(2)}) collective-permute-start(bf16[256,384]{1,0:T(8,128)(2,1)S(1)} %constant_dynamic-update-slice_fusion.5.refs_6_), channel_id=1, source_target_pairs={{0,4},{4,0},{8,12},{12,8},{16,20},{20,16},{24,28},{28,24},{1,5},{5... | collective-permute-start | bytes 589832 | tf_op jit(solution)/shard_map/ppermute | solution.py:303
  49.0 2.1 %collective-permute-start.23 = (bf16[256,384]{1,0:T(8,128)(2,1)S(1)}, bf16[256,384]{1,0:T(8,128)(2,1)S(1)}, u32[]{:S(2)}, u32[]{:S(2)}) collective-permute-start(bf16[256,384]{1,0:T(8,128)(2,1)S(1)} %collective-permute-done.22.refs_8_), channel_id=1, source_target_pairs={{0,4},{4,0},{8,12},{12,8},{16,20},{20,16},{24,28},{28,24},{1,5},{5... | collective-permute-start | bytes 589832 | tf_op jit(solution)/shard_map/ppermute | solution.py:303
  (5 other events, 19.6 us)
